TPU v7x, 32 devices: a whole 2x2x4 slice. The times are simulated.
32 devices in a mesh: grp: 2 (over y), row: 8 (over z, x), col: 2 (over core).
Axes of the slice: x: 2, y: 2, z: 4, core: 2. Of those that a mesh axis runs over, the one named last changes fastest.
Arguments:
- tokens: bfloat16 [128, 256, 180], P(('grp', 'row'), 'col'), parts along dimension 0, may hold values from -6 to 6
- grad_out: bfloat16 [128, 256, 180], P(('grp', 'row'), 'col'), parts along dimension 0, may hold values from -8 to 8
- regions: int32 [128, 256], P(('grp', 'row'), 'col'), parts along dimension 0, may hold values from 0 to 15, as said below
- ln_gain: float32 [180], replicated, may hold values from 0.1 to 1.9
- ln_offset: float32 [180], replicated, may hold values from -1.5 to 1.5
- qkv_weight: bfloat16 [180, 540], replicated, may hold values from -0.4375 to 0.4375
- qkv_bias: float32 [540], replicated, may hold values from -1.5 to 1.5
- proj_weight: bfloat16 [180, 180], replicated, may hold values from -0.4375 to 0.4375
- bias_table: float32 [225, 6], replicated, may hold values from -4 to 320
Outputs:
- d_tokens: bfloat16 [128, 256, 180], P(('grp', 'row'), 'col'), parts along dimension 0
- d_qkv_weight: float32 [360, 540], P('grp'), parts along dimension 0
- d_qkv_bias: float32 [1080], P('grp'), parts along dimension 0
- d_proj_weight: float32 [360, 180], P('grp'), parts along dimension 0
- d_bias_table: float32 [450, 6], P('grp'), parts along dimension 0
- d_ln_gain: float32 [360], P('grp'), parts along dimension 0
- d_ln_offset: float32 [360], P('grp'), parts along dimension 0
There are 2 independent parts, one for each index of `grp`. A program takes and returns all parts, laid end to end along the dimension named above; an argument that names none is the same for every part. Nothing has to cross between parts.
Inputs may be any that keep to these rules, and one draw needn't show every extreme that they name: `regions`: A token attends only to tokens of its window with the same id. The map is a grid: the id is 4 a + b, where a, from 0 to 3, depends only on the token's row and b, from 0 to 3, only on its column.
All inputs are finite; a program needn't handle non-finite values.
Results may differ from a plain program's by a relative error of at most 0.0085.
Values may be sent and summed in bfloat16 or wider, within the bound.
No kernel may reach another device: no remote copies, remote signals or barrier semaphores. Data moves between devices by JAX's collectives and lax.ppermute only.
A program may use at most 64 MiB of HBM per device.

v0:
```python
import jax
import jax.numpy as jnp
from jax import lax
from jax.sharding import PartitionSpec as P

HEADS = 6
WIN = 8
SHIFT = 4


masked_score = -10000.0


def from_behind(shard, axis, by):
    count = lax.axis_size(axis)
    return lax.ppermute(shard, axis, [(i, (i + by) % count) for i in range(count)])


def multiply(form, left, right):
    return jnp.einsum(form, left, right, preferred_element_type=jnp.float32)


def relative_onehot(table_rows):
    span_size = WIN * WIN
    position = jnp.arange(span_size, dtype=jnp.int32)
    row_pos = position // WIN
    col_pos = position % WIN
    entry_index = (
        (row_pos[:, None] - row_pos[None, :] + WIN - 1) * (2 * WIN - 1)
        + col_pos[:, None]
        - col_pos[None, :]
        + WIN
        - 1
    )
    return (
        entry_index.reshape(-1)[:, None] == jnp.arange(table_rows, dtype=jnp.int32)[None, :]
    ).astype(jnp.float32)


def normalize(values, gain_vec, offset_vec):
    as_float = values.astype(jnp.float32)
    center = jnp.mean(as_float, -1, keepdims=True)
    variance = jnp.mean(jnp.square(as_float - center), -1, keepdims=True)
    inv_std = lax.rsqrt(variance + 1e-05)
    unit_tokens = (as_float - center) * inv_std
    normed = (unit_tokens * gain_vec + offset_vec).astype(jnp.bfloat16)
    return (normed, unit_tokens, inv_std)


def project(normed, weights, offsets):
    channels = normed.shape[-1]
    summed = multiply("rcd,df->rcf", normed, weights) + offsets
    factor = jnp.where(jnp.arange(3 * channels) < channels, (channels // HEADS) ** (-0.5), 1.0)
    return (summed * factor).astype(jnp.bfloat16)


def window_band(qkv, grad_band, label_band, rel_bias, proj_weight):
    channels = grad_band.shape[-1]
    head_count = rel_bias.shape[0]
    head_size = channels // head_count
    tile_cols = grad_band.shape[1]
    win_count = tile_cols // WIN
    span_size = WIN * WIN

    def windows(array):
        array = array.reshape((WIN, win_count, WIN) + array.shape[2:])
        array = jnp.moveaxis(array, 1, 0)
        return array.reshape((win_count, span_size) + array.shape[3:])

    parted = windows(qkv).reshape(win_count, span_size, 3, head_count, head_size)
    query_part = parted[:, :, 0]
    key_part = parted[:, :, 1]
    value_part = parted[:, :, 2]
    grad_win = windows(grad_band)
    label_win = windows(label_band)
    matched = label_win[:, :, None] == label_win[:, None, :]
    scores = multiply("nihd,njhd->nhij", query_part, key_part) + rel_bias[None]
    scores = jnp.where(matched[:, None], scores, masked_score)
    probability = jax.nn.softmax(scores, axis=-1)
    prob_low = probability.astype(jnp.bfloat16)
    attended = (
        multiply("nhij,njhd->nihd", prob_low, value_part)
        .astype(jnp.bfloat16)
        .reshape(win_count * span_size, channels)
    )
    flat_grad = grad_win.reshape(win_count * span_size, channels)
    d_proj = multiply("tc,td->cd", attended, flat_grad)
    d_attended = (
        multiply("td,cd->tc", flat_grad, proj_weight)
        .astype(jnp.bfloat16)
        .reshape(win_count, span_size, head_count, head_size)
    )
    d_prob = multiply("nihd,njhd->nhij", d_attended, value_part)
    d_scores = probability * (d_prob - jnp.sum(probability * d_prob, -1, keepdims=True))
    score_sum = jnp.sum(d_scores, 0)
    d_score_low = d_scores.astype(jnp.bfloat16)
    d_query = multiply("nhij,njhd->nihd", d_score_low, key_part) * head_size ** (-0.5)
    d_key = multiply("nhij,nihd->njhd", d_score_low, query_part)
    d_value = multiply("nhij,nihd->njhd", prob_low, d_attended)
    d_qkv = (
        jnp.stack([d_query, d_key, d_value], 2)
        .astype(jnp.bfloat16)
        .reshape(win_count, span_size, 3 * channels)
    )
    array = d_qkv
    array = array.reshape((win_count, WIN, WIN) + array.shape[2:])
    array = jnp.moveaxis(array, 0, 1)
    return (array.reshape((WIN, tile_cols) + array.shape[3:]), d_proj, score_sum)


def attention_backward(qkv, grad_tile, label_tile, rel_bias, proj_weight):
    tile_rows = grad_tile.shape[0]
    band_count = tile_rows // WIN
    channels = grad_tile.shape[-1]
    head_count = rel_bias.shape[0]

    def to_bands(array):
        return array.reshape((band_count, WIN) + array.shape[1:])

    def band_step(running, pieces):
        d_qkv, d_proj, score_sum = window_band(
            pieces[0], pieces[1], pieces[2], rel_bias, proj_weight
        )
        return ((running[0] + d_proj, running[1] + score_sum), d_qkv)

    initial = (
        jnp.zeros((channels, channels), jnp.float32),
        jnp.zeros((head_count, WIN * WIN, WIN * WIN), jnp.float32),
    )
    totals, d_qkv = lax.scan(
        band_step, initial, (to_bands(qkv), to_bands(grad_tile), to_bands(label_tile))
    )
    return (d_qkv.reshape((tile_rows,) + d_qkv.shape[2:]), totals[0], totals[1])


def input_backward(d_qkv, normed, unit_tokens, inv_std, gain_vec, qkv_weight):
    d_weight = multiply("rcd,rcf->df", normed, d_qkv)
    d_offsets = jnp.sum(d_qkv.astype(jnp.float32), (0, 1))
    d_normed = multiply("rcf,df->rcd", d_qkv, qkv_weight)
    d_gain = jnp.sum(d_normed * unit_tokens, (0, 1))
    d_offset = jnp.sum(d_normed, (0, 1))
    scaled_grad = d_normed * gain_vec
    d_input = inv_std * (
        scaled_grad
        - jnp.mean(scaled_grad, -1, keepdims=True)
        - unit_tokens * jnp.mean(scaled_grad * unit_tokens, -1, keepdims=True)
    )
    return (d_input, d_weight, d_offsets, d_gain, d_offset)


def into_frame(member_one, member_two, member_three):
    below_one, below_two, below_three = from_behind(
        (member_one[:SHIFT], member_two[:SHIFT], member_three[:SHIFT]), "row", -1
    )
    member_one = jnp.concatenate([member_one[SHIFT:], below_one], 0)
    member_two = jnp.concatenate([member_two[SHIFT:], below_two], 0)
    member_three = jnp.concatenate([member_three[SHIFT:], below_three], 0)
    right_one, right_two, right_three = from_behind(
        (member_one[:, :SHIFT], member_two[:, :SHIFT], member_three[:, :SHIFT]), "col", -1
    )
    member_one = jnp.concatenate([member_one[:, SHIFT:], right_one], 1)
    member_two = jnp.concatenate([member_two[:, SHIFT:], right_two], 1)
    member_three = jnp.concatenate([member_three[:, SHIFT:], right_three], 1)
    return (member_one, member_two, member_three)


def back_proj(field):
    from_left = from_behind(field[:, -SHIFT:], "col", 1)
    field = jnp.concatenate([from_left, field[:, :-SHIFT]], 1)
    from_above = from_behind(field[-SHIFT:], "row", 1)
    return jnp.concatenate([from_above, field[:-SHIFT]], 0)


def table_grad(score_sum, entry_table):
    head_count = score_sum.shape[0]
    flat_sum = jnp.transpose(score_sum, (1, 2, 0)).reshape(-1, head_count)
    return jnp.dot(entry_table.T, flat_sum, precision=lax.Precision.HIGHEST)


def attention_sums(d_proj, d_table):
    return (d_proj, d_table)


def on_device(
    tokens, grad_out, regions, ln_gain, ln_offset, qkv_weight, qkv_bias, proj_weight, bias_table
):
    head_count = bias_table.shape[1]
    entry_table = relative_onehot(bias_table.shape[0])
    rel_bias = (
        jnp.dot(entry_table, bias_table, precision=lax.Precision.HIGHEST)
        .reshape(WIN * WIN, WIN * WIN, head_count)
        .transpose(2, 0, 1)
    )
    labels = regions.astype(jnp.bfloat16)
    normed, unit_tokens, inv_std = normalize(tokens, ln_gain, ln_offset)
    qkv = project(normed, qkv_weight, qkv_bias)
    qkv_framed, grad_framed, label_framed = into_frame(qkv, grad_out, labels)
    d_framed, d_proj, score_sum = attention_backward(
        qkv_framed, grad_framed, label_framed, rel_bias, proj_weight
    )
    d_proj, d_table = attention_sums(d_proj, table_grad(score_sum, entry_table))
    d_qkv = back_proj(d_framed)
    d_input, d_weight, d_offsets, d_gain, d_offset = input_backward(
        d_qkv, normed, unit_tokens, inv_std, ln_gain, qkv_weight
    )
    d_proj, d_table, d_weight, d_offsets, d_gain, d_offset = lax.psum(
        (d_proj, d_table, d_weight, d_offsets, d_gain, d_offset), ("row", "col")
    )
    total_tokens = tokens.shape[0] * tokens.shape[1] * lax.axis_size("row") * lax.axis_size("col")
    out_scale = total_tokens ** (-0.5)
    d_tokens = (grad_out.astype(jnp.float32) + d_input).astype(jnp.bfloat16)
    return (
        d_tokens,
        d_weight * out_scale,
        d_offsets * out_scale,
        d_proj * out_scale,
        d_table * out_scale,
        d_gain * out_scale,
        d_offset * out_scale,
    )


def solution(mesh):
    placed = (
        P(("grp", "row"), "col", None),
        P(("grp", "row"), "col", None),
        P(("grp", "row"), "col"),
        P(),
        P(),
        P(),
        P(),
        P(),
        P(),
    )
    return jax.shard_map(
        on_device,
        mesh=mesh,
        in_specs=placed,
        out_specs=(
            P(("grp", "row"), "col", None),
            P("grp", None),
            P("grp"),
            P("grp", None),
            P("grp", None),
            P("grp"),
            P("grp"),
        ),
        check_vma=False,
    )
```

profile of v0, /device:TPU:0, one launch (start us, length us, event | category | flops | bytes accessed | tf_op | source)
XLA Modules:
  0.0 272.9 jit_solution(3321277854407880220)
XLA Ops:
  7.2 1.1 convert_reduce_fusion.1
  8.3 1.1 fusion.40
  9.5 0.6 copy-done.15
  10.1 1.6 multiply_convert_fusion
  12.1 6.0 %collective-permute-start = (bf16[4,128,540]{1,0,2:T(4,128)(2,1)S(1)}, bf16[4,128,540]{1,0,2:T(4,128)(2,1)S(1)}, u32[]{:S(2)}, u32[]{:S(2)}) collective-permute-start(bf16[4,128,540]{1,0,2:T(4,128)(2,1)S(1)} %copy.87), channel_id=1, source_target_pairs={{0,14},{2,0},{4,2},{6,4},{8,6},{10,8},{12,10},{14,12},{1,15},{3,1}... | collective-permute-start | bytes 1658888 | tf_op jit(solution)/shard_map/ppermute | solution.py:16
  18.2 0.6 collective-permute-start.2
  19.1 1.4 collective-permute-start.4
  20.7 0.6 copy-done.17
  21.3 2.6 fusion.2
  24.3 6.8 %collective-permute-done.2 = bf16[4,128]{1,0:T(4,128)(2,1)S(1)} collective-permute-done((bf16[4,128]{1,0:T(4,128)(2,1)S(1)}, bf16[4,128]{1,0:T(4,128)(2,1)S(1)}, u32[]{:S(2)}, u32[]{:S(2)}) %collective-permute-start.2) | collective-permute-done | bytes 1056 | tf_op jit(solution)/shard_map/ppermute | solution.py:16
  31.2 1.1 collective-permute-done.3
  32.9 2.7 %collective-permute-done.4 = bf16[4,128,180]{2,1,0:T(8,128)(2,1)S(1)} collective-permute-done((bf16[4,128,180]{2,1,0:T(8,128)(2,1)S(1)}, bf16[4,128,180]{2,1,0:T(8,128)(2,1)S(1)}, u32[]{:S(2)}, u32[]{:S(2)}) %collective-permute-start.4) | collective-permute-done | bytes 184352 | tf_op jit(solution)/shard_map/ppermute | solution.py:16
  35.8 1.0 collective-permute-done.5
  37.0 0.8 copy-done.2
  37.8 0.3 convolution_convert_fusion.3
  38.2 1.3 reshape.196
  39.7 0.5 copy.89
  40.4 0.4 slice_maximum_fusion
  40.7 0.7 collective-permute-done.1
  41.4 0.6 copy.90
  42.0 1.6 pad_maximum_fusion.3
  43.6 1.7 copy.91
  45.4 5.6 %reshape.191 = bf16[16,64,3,6,30]{4,3,2,1,0:T(8,128)(2,1)} reshape(bf16[16,8,8,540]{3,2,1,0:T(8,128)(2,1)S(1)} %copy.92) | data formatting | bytes 2211840 | tf_op jit(solution)/shard_map/while/body/eval_jaxpr/reshape;while/body/eval_jaxpr/reshape | solution.py:70
  51.1 6.6 %fusion.52 = (bf16[16,64,1,6,30]{4,3,2,1,0:T(8,128)(2,1)S(1)}, bf16[16,64,1,6,30]{4,3,2,1,0:T(8,128)(2,1)}, bf16[16,64,1,6,30]{4,3,2,1,0:T(8,128)(2,1)}) fusion(bf16[16,64,3,6,30]{4,3,2,1,0:T(8,128)(2,1)} %reshape.191), kind=kLoop, calls=%fused_computation.97 | loop fusion | bytes 2211840 | tf_op jit(solution)/shard_map/while/body/eval_jaxpr/slice | solution.py:73
  57.6 2.4 copy.123
  60.0 3.1 %copy.124 = bf16[16,64,1,6,30]{1,4,3,0,2:T(8,128)(2,1)} copy(bf16[16,64,1,6,30]{4,3,2,1,0:T(8,128)(2,1)} %get-tuple-element.77) | data formatting | bytes 737280
  63.2 1.9 copy.127
  65.1 1.7 fusion.26
  66.8 1.1 fusion.56
  68.2 1.0 multiply_reduce_fusion
  69.2 1.1 fusion.13
  70.3 0.5 fusion.12
  70.8 0.6 copy-done.1
  71.4 0.9 fusion.9
  72.4 0.9 fusion.10
  73.3 0.6 pad_maximum_fusion
  73.9 5.5 %copy.108 = bf16[16,64,3,6,30]{4,3,2,1,0:T(8,128)(2,1)} copy(bf16[16,64,3,6,30]{1,4,3,0,2:T(8,128)(2,1)S(1)} %pad_maximum_fusion) | data formatting | bytes 2211840 | tf_op jit(solution)/shard_map/while/body/eval_jaxpr/stack | solution.py:101
  79.4 7.9 %convert_element_type.55 = bf16[16,8,8,540]{3,2,1,0:T(8,128)(2,1)} reshape(bf16[16,64,3,6,30]{4,3,2,1,0:T(8,128)(2,1)} %copy.108) | data formatting | bytes 2211840 | tf_op jit(solution)/shard_map/while/body/eval_jaxpr/convert_element_type | solution.py:102
  87.3 1.4 copy_bitcast_fusion
  89.0 0.8 copy.128
  90.1 0.6 copy.112
  91.0 1.1 copy.113
  92.1 0.3 collective-permute-start.7
  92.4 0.4 copy-done.6
  92.8 1.5 fusion.11
  94.5 2.5 copy.116
  97.0 1.8 reshape.198
  98.8 1.4 fusion.1
  100.2 1.0 fusion.57
  101.2 9.2 %collective-permute-done.7 = bf16[4,128,540]{1,0,2:T(4,128)(2,1)} collective-permute-done((bf16[4,128,540]{1,0,2:T(4,128)(2,1)}, bf16[4,128,540]{1,0,2:T(4,128)(2,1)}, u32[]{:S(2)}, u32[]{:S(2)}) %collective-permute-start.7) | collective-permute-done | bytes 552992 | tf_op jit(solution)/shard_map/ppermute | solution.py:16
  110.4 1.1 copy.114
  111.6 0.6 convert_reduce_fusion
  112.2 0.4 copy-done.4
  112.6 0.7 fusion.39
  113.3 1.4 convolution_bitcast_fusion
  114.7 58.2 %all-reduce = (f32[540]{0:T(1024)S(1)}, f32[225,6]{0,1:T(8,128)S(1)}, f32[180]{0:T(256)S(1)}, f32[180]{0:T(256)S(1)}) all-reduce(f32[540]{0:T(1024)S(1)} %get-tuple-element.72, f32[225,6]{0,1:T(8,128)S(1)} %fusion.1, f32[180]{0:T(256)S(1)} %get-tuple-element.62, ...), channel_id=1, replica_groups=mesh['grp'=2,'row'=8,'col'=2] {'row','col'}, use_global_device_ids=true, to_apply=%region_9.10 | all-reduce | flops 2250 | bytes 18000 | tf_op jit(solution)/shard_map/psum | solution.py:206
  172.9 0.6 broadcast_multiply_fusion.3
  173.4 0.6 broadcast_multiply_fusion.7
  174.3 0.6 broadcast_multiply_fusion.8
  174.9 0.8 copy.118
  175.7 0.6 broadcast_multiply_fusion.2
  176.3 86.3 %all-reduce.4.cloned.1.call-done = (f32[180,540]{1,0:T(8,128)}, f32[180,180]{1,0:T(8,128)}) async-done(((f32[180,540]{1,0:T(8,128)}, f32[180,180]{1,0:T(8,128)}), (f32[180,540]{1,0:T(8,128)}, f32[180,180]{1,0:T(8,128)})) %all-reduce.4.cloned.1.call-update) | async-done | bytes 518416 | tf_op jit(solution)/shard_map/psum | solution.py:206
  262.6 1.8 broadcast_multiply_fusion
  264.5 1.6 broadcast_multiply_fusion.1
  (85 shorter events, 4.5 us)
Async XLA Ops:
  7.2 2.9 %copy-start = (bf16[180,540]{1,0:T(8,128)(2,1)S(1)}, bf16[180,540]{1,0:T(8,128)(2,1)}, u32[]{:S(2)}) copy-start(bf16[180,540]{1,0:T(8,128)(2,1)} %param.14) | copy-start | bytes 583204
  7.2 255.5 %all-reduce.4.cloned.1.call-start = ((), (), s32[]{:S(2)}) async-start(), calls=%async_computation | async-start | bytes 1318912 | tf_op jit(solution)/shard_map/psum | solution.py:206
  8.3 1.1 copy-start.13
  9.5 0.6 copy-start.15
  11.7 6.4 %copy-start.19 = (s32[8,128]{1,0:T(8,128)S(1)}, s32[8,128]{1,0:T(8,128)}, u32[]{:S(2)}) copy-start(s32[8,128]{1,0:T(8,128)} %param.11) | copy-start | bytes 12292
  11.7 7.0 %copy-start.7 = (bf16[8,128,180]{1,0,2:T(8,128)(2,1)S(1)}, bf16[8,128,180]{1,0,2:T(8,128)(2,1)}, u32[]{:S(2)}) copy-start(bf16[8,128,180]{1,0,2:T(8,128)(2,1)} %param.10) | copy-start | bytes 1105924
  11.7 9.5 %copy-start.21 = (f32[225,6]{0,1:T(8,128)S(1)}, f32[225,6]{0,1:T(8,128)}, u32[]{:S(2)}) copy-start(f32[225,6]{0,1:T(8,128)} %param.17) | copy-start | bytes 16204
  12.1 27.4 %collective-permute-start = (bf16[4,128,540]{1,0,2:T(4,128)(2,1)S(1)}, bf16[4,128,540]{1,0,2:T(4,128)(2,1)S(1)}, u32[]{:S(2)}, u32[]{:S(2)}) collective-permute-start(bf16[4,128,540]{1,0,2:T(4,128)(2,1)S(1)} %copy.87), channel_id=1, source_target_pairs={{0,14},{2,0},{4,2},{6,4},{8,6},{10,8},{12,10},{14,12},{1,15},{3,1}... | collective-permute-start | bytes 1658888 | tf_op jit(solution)/shard_map/ppermute | solution.py:16
  18.2 12.9 %collective-permute-start.2 = (bf16[4,128]{1,0:T(4,128)(2,1)S(1)}, bf16[4,128]{1,0:T(4,128)(2,1)S(1)}, u32[]{:S(2)}, u32[]{:S(2)}) collective-permute-start(bf16[4,128]{1,0:T(4,128)(2,1)S(1)} %get-tuple-element.84), channel_id=1, source_target_pairs={{0,14},{2,0},{4,2},{6,4},{8,6},{10,8},{12,10},{14,12},{1,15},{3,1}... | collective-permute-start | bytes 3080 | tf_op jit(solution)/shard_map/ppermute | solution.py:16
  19.1 16.5 %collective-permute-start.4 = (bf16[4,128,180]{2,1,0:T(8,128)(2,1)S(1)}, bf16[4,128,180]{2,1,0:T(8,128)(2,1)S(1)}, u32[]{:S(2)}, u32[]{:S(2)}) collective-permute-start(bf16[4,128,180]{2,1,0:T(8,128)(2,1)S(1)} %copy.126), channel_id=1, source_target_pairs={{0,14},{2,0},{4,2},{6,4},{8,6},{10,8},{12,10},{14,12},{1,15},{3,1}... | collective-permute-start | bytes 552968 | tf_op jit(solution)/shard_map/ppermute | solution.py:16
  20.7 0.6 copy-start.17
  24.1 13.8 %copy-start.12 = (bf16[180,180]{1,0:T(8,128)(2,1)S(1)}, bf16[180,180]{1,0:T(8,128)(2,1)}, u32[]{:S(2)}) copy-start(bf16[180,180]{1,0:T(8,128)(2,1)} %param.16) | copy-start | bytes 194404
  31.1 1.2 collective-permute-start.3
  35.6 1.2 collective-permute-start.5
  37.0 0.8 copy-start.2
  40.1 1.3 collective-permute-start.1
  66.8 1.1 copy-start.9
  66.8 1.3 copy-start.11
  67.9 4.4 %copy-start.5 = (f32[16,6,64,64]{2,3,1,0:T(8,128)}, f32[16,6,64,64]{2,3,1,0:T(8,128)S(1)}, u32[]{:S(2)}) copy-start(f32[16,6,64,64]{2,3,1,0:T(8,128)S(1)} %get-tuple-element.86) | copy-start | bytes 4718596
  70.3 1.1 copy-start.1
  88.8 1.3 collective-permute-start.6
  90.1 2.3 copy-start.10
  90.6 2.2 copy-start.6
  92.1 18.4 %collective-permute-start.7 = (bf16[4,128,540]{1,0,2:T(4,128)(2,1)}, bf16[4,128,540]{1,0,2:T(4,128)(2,1)}, u32[]{:S(2)}, u32[]{:S(2)}) collective-permute-start(bf16[4,128,540]{1,0,2:T(4,128)(2,1)} %copy.113), channel_id=1, source_target_pairs={{0,2},{2,4},{4,6},{6,8},{8,10},{10,12},{12,14},{14,0},{1,3},{3,5},... | collective-permute-start | bytes 1658888 | tf_op jit(solution)/shard_map/ppermute | solution.py:16
  94.3 4.5 %copy-start.18 = (s32[4096]{0:T(1024)S(1)}, s32[4096]{0:T(1024)}, u32[]{:S(2)}) copy-start(s32[4096]{0:T(1024)} %copy-done.17) | copy-start | bytes 49156
  94.4 5.8 %copy-start.3 = (bf16[16,8,8,180]{3,2,1,0:T(8,128)(2,1)S(1)}, bf16[16,8,8,180]{3,2,1,0:T(8,128)(2,1)}, u32[]{:S(2)}) copy-start(bf16[16,8,8,180]{3,2,1,0:T(8,128)(2,1)} %copy-done.2) | copy-start | bytes 1105924
  111.6 1.0 copy-start.4
  111.6 1.0 copy-start.14
  111.6 1.0 copy-start.16
  111.6 1.0 copy-start.20
  112.2 1.1 copy-start.22
  113.3 60.8 %copy-start.8 = (bf16[8,128,180]{1,0,2:T(8,128)(2,1)S(1)}, bf16[8,128,180]{1,0,2:T(8,128)(2,1)}, u32[]{:S(2)}) copy-start(bf16[8,128,180]{1,0,2:T(8,128)(2,1)} %param.10) | copy-start | bytes 1105924
Sparse Core Ops, SparseCore 0:
  174.2 88.4 all-reduce.3
where the time goes:
time: 274 us; the launch traced here: 273 us
  waiting for transfers between devices  108 us (39%)
  blocking collectives  58.2 us (21%)
  local copies, waits for them, and re-layouts  52.8 us (19%)
  matrix products  15.6 us (6%)
  other arithmetic  14.7 us (5%)
  between operations  14.5 us (5%)
  starting transfers between devices  8.96 us (3%)
    psum x1, waiting for transfers between devices, on_device(): lax.psum((d_proj, d_table, d_weight, d_offsets, d_gain, d_offset), ('row'...  86.3 us
    psum x1, blocking collectives, on_device(): lax.psum((d_proj, d_table, d_weight, d_offsets, d_gain, d_offset), ('row'...  58.2 us
    ppermute x8, waiting for transfers between devices, from_behind(): lax.ppermute(shard, axis, [(i, (i + by) % count) for i in range(count)])  21.8 us
    unnamed x53, local copies, waits for them, and re-layouts  13.1 us
    dot_general x11, matrix products, multiply(): return jnp.einsum(form, left, right, preferred_element_type=jnp.float32)  11.6 us
    ppermute x8, starting transfers between devices, from_behind(): lax.ppermute(shard, axis, [(i, (i + by) % count) for i in range(count)])  8.92 us
    convert_element_type x1, local copies, waits for them, and re-layouts, window_band(): d_qkv = jnp.stack([d_query, d_key, d_value], 2).astype(jnp.bfloat16).resh...  7.91 us
    slice x1, local copies, waits for them, and re-layouts, window_band(): value_part = parted[:, :, 2]  6.55 us
  transfers between devices with their start and end apart: 9, of which 8 were waited for; matrix products, arithmetic and copies ran while one was open for 7% of the time, Pallas kernels for 0%

commit v1 on v0

v1 whole, which is shorter than its diff:
```python
import functools

import jax
import jax.numpy as jnp
from jax import lax
from jax.experimental import pallas as pl
from jax.experimental.pallas import tpu as pltpu
from jax.sharding import PartitionSpec as P

HEADS = 6
WIN = 8
SHIFT = 4
SPAN = WIN * WIN
MASKED = -10000.0
LANES = 128
SLOT = 32
ROWS = 184
TABLE_ROWS = 16
BUFFER_ROWS = 6 * ROWS + TABLE_ROWS

VMEM_LIMIT = 48 * 1024 * 1024


def nn(left, right):
    return lax.dot_general(left, right, (((1,), (0,)), ((), ())), preferred_element_type=jnp.float32)


def nt(left, right):
    return lax.dot_general(left, right, (((1,), (1,)), ((), ())), preferred_element_type=jnp.float32)


def iota(shape, dim):
    return lax.broadcasted_iota(jnp.int32, shape, dim)


def table_hits(cj, lanes_first):
    shape = (LANES, 2 * LANES) if lanes_first else (2 * LANES, LANES)
    lane = iota(shape, 0 if lanes_first else 1)
    entry = iota(shape, 1 if lanes_first else 0)
    wanted = (lane // WIN) * (2 * WIN - 1) + lane % WIN + (WIN - 1) - cj
    return jnp.where((entry == wanted) & (lane < WIN * (2 * WIN - 1)), 1.0, 0.0).astype(jnp.bfloat16)


def split_three(value):
    high = value.astype(jnp.bfloat16)
    rest = value - high.astype(jnp.float32)
    middle = rest.astype(jnp.bfloat16)
    low = (rest - middle.astype(jnp.float32)).astype(jnp.bfloat16)
    return high, middle, low


def slots(rows):
    size = rows.shape[0] // HEADS
    blank = jnp.zeros((SLOT - size, rows.shape[1]), rows.dtype)
    pieces = []
    for head in range(HEADS):
        pieces += [rows[head * size : (head + 1) * size], blank]
    return jnp.concatenate(pieces, 0)


def unslot(rows, size):
    return jnp.concatenate([rows[head * SLOT : head * SLOT + size] for head in range(HEADS)], 0)


def prepare_kernel(weight_ref, offsets_ref, proj_ref, table_ref, bias_ref, tok_ref, chan_ref, proj_slots_ref, parts_ref):
    channels = weight_ref.shape[0]
    for part in range(3):
        weight = weight_ref[:, part * channels : (part + 1) * channels].astype(jnp.float32)
        parts_ref[part] = weight.astype(jnp.bfloat16)
        high, middle, low = split_three(offsets_ref[:, part * channels : (part + 1) * channels])
        full = jnp.concatenate(
            [
                weight,
                high.astype(jnp.float32),
                middle.astype(jnp.float32),
                low.astype(jnp.float32),
                jnp.zeros((256 - channels - 3, channels), jnp.float32),
            ],
            0,
        )
        turned = slots(full.T)
        chan_ref[part] = turned.astype(jnp.bfloat16)
        if part == 0:
            tok_ref[part, :, 0:channels] = full.astype(jnp.bfloat16)
            tok_ref[part, :, channels:] = jnp.zeros((256, HEADS * SLOT - channels), jnp.bfloat16)
        else:
            tok_ref[part] = turned.T.astype(jnp.bfloat16)
    proj_slots_ref[...] = slots(proj_ref[...].astype(jnp.float32)).astype(jnp.bfloat16)
    pieces = split_three(table_ref[...])
    lane = iota((8, LANES), 1)
    for cj in range(WIN):
        hits = table_hits(cj, False)
        spread = nn(pieces[0], hits) + nn(pieces[1], hits) + nn(pieces[2], hits)
        for rj in range(WIN):
            by = WIN * (WIN - 1 - rj)
            moved = spread if by == 0 else pltpu.roll(spread, LANES - by, 1)
            both = jnp.where(lane < SPAN, moved, pltpu.roll(moved, SPAN, 1))
            for head in range(HEADS):
                bias_ref[head, rj * WIN + cj : rj * WIN + cj + 1, :] = both[head : head + 1, :]


def main_kernel(
    tokens_ref,
    grad_ref,
    region_ref,
    below_ref,
    right_ref,
    corner_ref,
    gain_ref,
    offset_ref,
    bias_ref,
    tok_ref,
    chan_ref,
    proj_ref,
    proj_slots_ref,
    parts_ref,
    own_ref,
    down_ref,
    over_ref,
    sums_ref,
    x_s,
    g_s,
    id_s,
    unit_s,
    inv_s,
    unit_low_s,
    normed_s,
    grad_s,
    q_tok_s,
    k_tok_s,
    v_tok_s,
    da_tok_s,
    q_chan_s,
    k_chan_s,
    v_chan_s,
    da_chan_s,
    attended_s,
    d_qkv_s,
    score_s,
    out_s,
    pack_s,
):
    rows, cols, channels = tokens_ref.shape
    head_size = channels // HEADS
    scale = head_size ** (-0.5)
    count = rows * cols
    wins = cols // WIN
    f32 = jnp.float32
    bf16 = jnp.bfloat16

    x_s[:, :, :, LANES:] = jnp.zeros(x_s.shape[:3] + (LANES,), f32)
    ids = region_ref[...].astype(f32).T
    for r in range(rows):
        if r < rows - SHIFT:
            x_body = tokens_ref[r + SHIFT].astype(f32)
            g_body = grad_ref[r + SHIFT].astype(f32)
            side = right_ref[r].astype(f32)
            id_body = ids[:, r + SHIFT : r + SHIFT + 1]
        else:
            payload = below_ref[r - (rows - SHIFT)].astype(f32)
            x_body = payload[:, 0:channels]
            g_body = payload[:, channels : 2 * channels]
            id_body = payload[:, 2 * channels : 2 * channels + 1]
            side = corner_ref[r - (rows - SHIFT)].astype(f32)
        x_row = jnp.concatenate([x_body[SHIFT:], side[:, 0:channels]], 0)
        g_row = jnp.concatenate([g_body[SHIFT:], side[:, channels : 2 * channels]], 0)
        id_row = jnp.concatenate([id_body[SHIFT:], side[:, 2 * channels : 2 * channels + 1]], 0)
        x_s[:, r, :, 0:channels] = x_row.reshape(wins, WIN, channels)
        g_s[:, r, :, :] = g_row.reshape(wins, WIN, channels)
        id_s[:, r, :, :] = id_row.reshape(wins, WIN, 1)

    x = x_s[...].reshape(count, 2 * LANES)
    lane = iota((1, 2 * LANES), 1)
    inside = lane < channels
    center = jnp.sum(x, -1, keepdims=True) * (1.0 / channels)
    away = jnp.where(inside, x - center, 0.0)
    variance = jnp.sum(away * away, -1, keepdims=True) * (1.0 / channels)
    inv_std = lax.rsqrt(variance + 1e-05)
    unit = away * inv_std
    unit_s[...] = unit
    inv_s[...] = inv_std
    unit_low_s[...] = jnp.where(lane == channels, 1.0, unit).astype(bf16)
    normed_s[...] = jnp.where(
        (lane >= channels) & (lane < channels + 3), 1.0, unit * gain_ref[...] + offset_ref[...]
    ).astype(bf16)
    grad_s[...] = g_s[...].reshape(count, channels).astype(bf16)

    normed = normed_s[...]
    q_tok_s[...] = (nn(normed, tok_ref[0, :, 0:channels]) * scale).astype(bf16)
    k_tok_s[...] = nn(normed, tok_ref[1]).astype(bf16)
    v_tok_s[...] = nn(normed, tok_ref[2]).astype(bf16)
    da_tok_s[...] = nt(grad_s[...], proj_ref[...]).astype(bf16)
    q_chan_s[...] = (nt(chan_ref[0], normed) * scale).astype(bf16)
    k_chan_s[...] = nt(chan_ref[1], normed).astype(bf16)
    v_chan_s[...] = nt(chan_ref[2], normed).astype(bf16)
    da_chan_s[...] = nt(proj_slots_ref[...], grad_s[...]).astype(bf16)

    score_s[...] = jnp.zeros(score_s.shape, f32)
    first = iota((1, LANES), 1) < SPAN
    first_low = jnp.where(first, 1.0, 0.0).astype(bf16)
    second_low = jnp.where(first, 0.0, 1.0).astype(bf16)
    head_of = iota((1, channels), 1) // head_size
    id_lane = iota((1, LANES), 1).astype(f32)

    def pack(square):
        return jnp.where(first, square[0:SPAN], square[SPAN:])

    def spread(packed):
        low = packed.astype(bf16)
        return jnp.concatenate([low * first_low, low * second_low], 0)

    def in_blocks(chan):
        blank = jnp.zeros((SLOT, LANES), bf16)
        lines = []
        for head in range(HEADS):
            line = [blank] * HEADS
            line[head] = chan[head * SLOT : (head + 1) * SLOT]
            lines.append(jnp.concatenate(line, 1))
        return jnp.concatenate(lines, 0)

    def by_head(tok):
        return jnp.concatenate(
            [jnp.where(head_of == head, tok, jnp.zeros_like(tok)) for head in range(HEADS)], 0
        )

    def pair_step(pair, carry):
        at = pl.ds(pl.multiple_of(pair * LANES, LANES), LANES)
        hot = jnp.where(id_s[pl.ds(pair * 2, 2)].reshape(LANES, 1) == id_lane, 1.0, 0.0).astype(bf16)
        match = pack(nt(hot, hot)) > 0.5
        k_chan = k_chan_s[:, at]
        v_chan = v_chan_s[:, at]
        scores = nn(k_tok_s[at, :], in_blocks(q_chan_s[:, at]))
        d_prob = nn(v_tok_s[at, :], in_blocks(da_chan_s[:, at]))
        attended = []
        d_query = []
        probs = []
        d_scores = []
        for head in range(HEADS):
            here = slice(head * LANES, (head + 1) * LANES)
            band = slice(head * SLOT, (head + 1) * SLOT)
            score = jnp.where(match, pack(scores[:, here]) + bias_ref[head], MASKED)
            power = jnp.exp(score - jnp.max(score, 0, keepdims=True))
            prob = power * (1.0 / jnp.sum(power, 0, keepdims=True))
            gradient = pack(d_prob[:, here])
            d_score = prob * (gradient - jnp.sum(prob * gradient, 0, keepdims=True))
            score_s[head] += d_score
            prob_low = spread(prob)
            d_low = spread(d_score)
            attended.append(nn(v_chan[band], prob_low))
            d_query.append(nn(k_chan[band], d_low) * scale)
            probs.append(prob_low)
            d_scores.append(d_low)
        attended_s[:, at] = jnp.concatenate(attended, 0).astype(bf16)
        d_query = jnp.concatenate([piece[0:head_size] for piece in d_query], 0)
        d_qkv_s[0, at, :] = d_query.T.astype(bf16)
        d_qkv_s[1, at, :] = nn(jnp.concatenate(d_scores, 1), by_head(q_tok_s[at, :])).astype(bf16)
        d_qkv_s[2, at, :] = nn(jnp.concatenate(probs, 1), by_head(da_tok_s[at, :])).astype(bf16)
        return carry

    lax.fori_loop(0, count // LANES, pair_step, 0)

    unit_turned = unit_low_s[...].T[0:ROWS]
    rest = channels - LANES
    pieces = [nn(unit_turned, d_qkv_s[part]) for part in range(3)]
    d_proj = nn(attended_s[...], grad_s[...])
    pieces.append(
        jnp.concatenate([unslot(d_proj, head_size), jnp.zeros((ROWS - channels, channels), f32)], 0)
    )
    pack_s[...] = jnp.zeros(pack_s.shape, f32)
    for at, piece in enumerate(pieces):
        pack_s[at * ROWS : (at + 1) * ROWS, :] = piece[:, 0:LANES]
        low = (4 + at // 2) * ROWS
        side = (at % 2) * SPAN
        pack_s[low : low + ROWS, side : side + rest] = piece[:, LANES:]
    lines = []
    for head in range(HEADS):
        both = score_s[head]
        both = jnp.where(first, both + pltpu.roll(both, SPAN, 1), 0.0)
        line = both[(WIN - 1) * WIN :]
        for rj in range(WIN - 1):
            line += pltpu.roll(both[rj * WIN : (rj + 1) * WIN], WIN * (WIN - 1 - rj), 1)
        lines.append(line)
    lines = jnp.concatenate(lines, 0)
    high = lines.astype(bf16)
    low = (lines - high.astype(f32)).astype(bf16)
    cj_of = iota((HEADS * WIN, 1), 0) % WIN
    table = jnp.zeros((HEADS * WIN, 2 * LANES), f32)
    for cj in range(WIN):
        hits = table_hits(cj, True)
        table += jnp.where(cj_of == cj, nn(high, hits) + nn(low, hits), 0.0)
    table = table.reshape(HEADS, WIN, 2 * LANES).sum(1)
    pack_s[6 * ROWS : 6 * ROWS + HEADS, :] = table[:, 0:LANES]
    pack_s[6 * ROWS + 8 : 6 * ROWS + 8 + HEADS, :] = table[:, LANES:]
    sums_ref[...] = pack_s[...].astype(bf16)

    d_normed = nt(d_qkv_s[0], parts_ref[0]) + nt(d_qkv_s[1], parts_ref[1]) + nt(d_qkv_s[2], parts_ref[2])
    scaled = d_normed * gain_ref[:, 0:channels]
    unit = unit_s[:, 0:channels]
    mean_one = jnp.sum(scaled, -1, keepdims=True) * (1.0 / channels)
    mean_two = jnp.sum(scaled * unit, -1, keepdims=True) * (1.0 / channels)
    d_input = inv_s[...] * (scaled - mean_one - unit * mean_two)
    out_s[...] = g_s[...] + d_input.reshape(wins, rows, WIN, channels)
    for r in range(rows):
        row = out_s[:, r].reshape(cols, channels)
        moved = jnp.concatenate([row[cols - SHIFT :], row[: cols - SHIFT]], 0).astype(bf16)
        target, place = (own_ref, r) if r < rows - SHIFT else (down_ref, r - (rows - SHIFT))
        target[place] = moved
        over_ref[r] = row[cols - SHIFT :].astype(bf16)


def finish_kernel(out_scale, mine_ref, other_ref, core_ref, weight_ref, gain_ref, offset_ref, d_weight_ref, d_bias_ref, d_proj_ref, d_table_ref, d_gain_ref, d_offset_ref):
    channels = weight_ref.shape[0]
    f32 = jnp.float32
    rest = channels - LANES
    mine = mine_ref[...].astype(f32)
    other = other_ref[...].astype(f32)
    here = core_ref[0] == 0
    low = jnp.where(here, mine, other)
    high = jnp.where(here, other, mine)
    both = jnp.concatenate([low, high], 0) * out_scale
    pieces = []
    for at in range(4):
        row = (4 + at // 2) * ROWS
        side = (at % 2) * SPAN
        pieces.append(
            jnp.concatenate(
                [both[at * ROWS : (at + 1) * ROWS, :], both[row : row + ROWS, side : side + rest]], 1
            )
        )
    gain = gain_ref[...].T
    offset = offset_ref[...].T
    d_gain = jnp.zeros((channels, 1), f32)
    d_offset = jnp.zeros((channels, 1), f32)
    for part in range(3):
        across = slice(part * channels, (part + 1) * channels)
        unit = pieces[part][0:channels]
        bias = pieces[part][channels : channels + 1]
        weight = weight_ref[:, across].astype(f32)
        d_weight_ref[:, across] = gain * unit + offset * bias
        d_bias_ref[:, across] = bias
        d_gain += jnp.sum(weight * unit, -1, keepdims=True)
        d_offset += jnp.sum(weight * bias, -1, keepdims=True)
    d_gain_ref[...] = d_gain.T
    d_offset_ref[...] = d_offset.T
    d_proj_ref[...] = pieces[3][0:channels]
    table = jnp.concatenate([both[6 * ROWS : 6 * ROWS + 8], both[6 * ROWS + 8 :]], 1).T
    d_table_ref[...] = table[0 : d_table_ref.shape[0], 0:HEADS]


def whole(memory_space=pltpu.VMEM):
    return pl.BlockSpec(memory_space=memory_space)


def from_behind(shard, axis, by):
    count = lax.axis_size(axis)
    return lax.ppermute(shard, axis, [(i, (i + by) % count) for i in range(count)])


def diagonal(shard, by):
    rows, cols = lax.axis_size("row"), lax.axis_size("col")
    pairs = [
        (r * cols + c, ((r + by) % rows) * cols + (c + by) % cols) for r in range(rows) for c in range(cols)
    ]
    return lax.ppermute(shard, ("row", "col"), pairs)


def sum_over_crop(buffer):
    rows, cols = lax.axis_size("row"), lax.axis_size("col")
    half = buffer.shape[0] // cols
    core = lax.axis_index("col")
    other = from_behind(buffer, "col", 1)
    start = core * half
    mine = lax.dynamic_slice_in_dim(buffer, start, half, 0).astype(jnp.float32) + lax.dynamic_slice_in_dim(
        other, start, half, 0
    ).astype(jnp.float32)
    mine = mine.astype(jnp.bfloat16)
    steps = [1 << bit for bit in range((rows - 1).bit_length())]
    for at in range(len(steps)):
        pairs = []
        for r in range(rows):
            for c in range(cols):
                step = steps[(at + c) % len(steps)]
                pairs.append((r * cols + c, (r ^ step) * cols + c))
        came = lax.ppermute(mine, ("row", "col"), pairs)
        mine = (mine.astype(jnp.float32) + came.astype(jnp.float32)).astype(jnp.bfloat16)
    return mine, from_behind(mine, "col", 1)


def on_device(
    tokens, grad_out, regions, ln_gain, ln_offset, qkv_weight, qkv_bias, proj_weight, bias_table
):
    rows, cols, channels = tokens.shape
    f32, bf16 = jnp.float32, jnp.bfloat16
    count = rows * cols
    params = pltpu.CompilerParams(vmem_limit_bytes=VMEM_LIMIT)

    def payload(row_slice, col_slice):
        return jnp.concatenate(
            [
                tokens[row_slice, col_slice],
                grad_out[row_slice, col_slice],
                regions[row_slice, col_slice, None].astype(bf16),
            ],
            -1,
        )

    below = from_behind(payload(slice(0, SHIFT), slice(None)), "row", -1)
    right = from_behind(payload(slice(SHIFT, None), slice(0, SHIFT)), "col", -1)
    corner = diagonal(payload(slice(0, SHIFT), slice(0, SHIFT)), -1)

    table = jnp.pad(bias_table.T, ((0, 8 - HEADS), (0, 2 * LANES - bias_table.shape[0])))
    wide = HEADS * SLOT
    bias, tok, chan, proj_slots, parts = pl.pallas_call(
        prepare_kernel,
        name="prepare",
        out_shape=(
            jax.ShapeDtypeStruct((HEADS, SPAN, LANES), f32),
            jax.ShapeDtypeStruct((3, 2 * LANES, wide), bf16),
            jax.ShapeDtypeStruct((3, wide, 2 * LANES), bf16),
            jax.ShapeDtypeStruct((wide, channels), bf16),
            jax.ShapeDtypeStruct((3, channels, channels), bf16),
        ),
        in_specs=[whole()] * 4,
        out_specs=(whole(),) * 5,
        compiler_params=params,
    )(qkv_weight, qkv_bias[None], proj_weight, table)

    gain = jnp.pad(ln_gain, (0, 2 * LANES - channels))[None]
    offset = jnp.pad(ln_offset, (0, 2 * LANES - channels))[None]
    wins = cols // WIN
    own, down, over, sums = pl.pallas_call(
        main_kernel,
        name="window_attention_backward",
        out_shape=(
            jax.ShapeDtypeStruct((SHIFT, cols, channels), bf16),
            jax.ShapeDtypeStruct((SHIFT, cols, channels), bf16),
            jax.ShapeDtypeStruct((rows, SHIFT, channels), bf16),
            jax.ShapeDtypeStruct((BUFFER_ROWS, LANES), bf16),
        ),
        in_specs=[whole()] * 14,
        out_specs=(whole(),) * 4,
        scratch_shapes=[
            pltpu.VMEM((wins, rows, WIN, 2 * LANES), f32),
            pltpu.VMEM((wins, rows, WIN, channels), f32),
            pltpu.VMEM((wins, rows, WIN, 1), f32),
            pltpu.VMEM((count, 2 * LANES), f32),
            pltpu.VMEM((count, 1), f32),
            pltpu.VMEM((count, 2 * LANES), bf16),
            pltpu.VMEM((count, 2 * LANES), bf16),
            pltpu.VMEM((count, channels), bf16),
            pltpu.VMEM((count, channels), bf16),
            pltpu.VMEM((count, wide), bf16),
            pltpu.VMEM((count, wide), bf16),
            pltpu.VMEM((count, channels), bf16),
            pltpu.VMEM((wide, count), bf16),
            pltpu.VMEM((wide, count), bf16),
            pltpu.VMEM((wide, count), bf16),
            pltpu.VMEM((wide, count), bf16),
            pltpu.VMEM((wide, count), bf16),
            pltpu.VMEM((3, count, channels), bf16),
            pltpu.VMEM((HEADS, SPAN, LANES), f32),
            pltpu.VMEM((wins, rows, WIN, channels), f32),
            pltpu.VMEM((BUFFER_ROWS, LANES), f32),
        ],
        compiler_params=params,
    )(
        tokens, grad_out, regions, below, right, corner, gain, offset, bias, tok, chan, proj_weight, proj_slots, parts
    )

    mine, other = sum_over_crop(sums)

    from_above = from_behind(down, "row", 1)
    from_left = from_behind(over[: rows - SHIFT], "col", 1)
    from_corner = diagonal(over[rows - SHIFT :], 1)
    d_tokens = jnp.concatenate(
        [
            jnp.concatenate([from_corner, from_above[:, SHIFT:]], 1),
            jnp.concatenate([from_left, own[:, SHIFT:]], 1),
        ],
        0,
    )

    total_tokens = count * lax.axis_size("row") * lax.axis_size("col")
    core = lax.axis_index("col").astype(jnp.int32).reshape(1)
    d_weight, d_bias, d_proj, d_table, d_gain, d_offset = pl.pallas_call(
        functools.partial(finish_kernel, total_tokens ** (-0.5)),
        name="finish",
        out_shape=(
            jax.ShapeDtypeStruct(qkv_weight.shape, f32),
            jax.ShapeDtypeStruct((1,) + qkv_bias.shape, f32),
            jax.ShapeDtypeStruct(proj_weight.shape, f32),
            jax.ShapeDtypeStruct(bias_table.shape, f32),
            jax.ShapeDtypeStruct((1,) + ln_gain.shape, f32),
            jax.ShapeDtypeStruct((1,) + ln_offset.shape, f32),
        ),
        in_specs=[whole(), whole(), whole(pltpu.SMEM), whole(), whole(), whole()],
        out_specs=(whole(),) * 6,
        compiler_params=params,
    )(mine, other, core, qkv_weight, ln_gain[None], ln_offset[None])
    return (d_tokens, d_weight, d_bias[0], d_proj, d_table, d_gain[0], d_offset[0])


def solution(mesh):
    placed = (
        P(("grp", "row"), "col", None),
        P(("grp", "row"), "col", None),
        P(("grp", "row"), "col"),
        P(),
        P(),
        P(),
        P(),
        P(),
        P(),
    )
    return jax.shard_map(
        on_device,
        mesh=mesh,
        in_specs=placed,
        out_specs=(
            P(("grp", "row"), "col", None),
            P("grp", None),
            P("grp"),
            P("grp", None),
            P("grp", None),
            P("grp"),
            P("grp"),
        ),
        check_vma=False,
    )
```

time: 274 us -> 61.3 us (0.22)
  waiting for transfers between devices: 108 us -> 22.4 us
  blocking collectives: 58.2 us -> 0 us
  local copies, waits for them, and re-layouts: 52.8 us -> 6.45 us
  matrix products: 15.6 us -> 0 us
  between operations: 14.5 us -> 0.85 us
  other arithmetic: 14.7 us -> 1.31 us
  Pallas kernels: 0 us -> 12.1 us
  starting transfers between devices: 8.96 us -> 17.9 us
    psum x1 -> x0, waiting for transfers between devices: 86.3 us -> none  [on_device(): lax.psum((d_proj, d_table, d_weight, d_offsets, d_gain, d_offset), ('row'...]
    psum x1 -> x0, blocking collectives: 58.2 us -> none  [on_device(): lax.psum((d_proj, d_table, d_weight, d_offsets, d_gain, d_offset), ('row'...]
    ppermute x0 -> x5, waiting for transfers between devices: none -> 20.9 us  [the longest x3 14.8 us: sum_over_crop(): came = lax.ppermute(mine, ('row', 'col'), pairs)]
    ppermute x8 -> x6, waiting for transfers between devices: 21.8 us -> 1.57 us  [from_behind(): lax.ppermute(shard, axis, [(i, (i + by) % count) for i in range(count)])]
    dot_general x13 -> x0, matrix products: 15.6 us -> none  [the longest x11 11.6 us: multiply(): return jnp.einsum(form, left, right, preferred_element_type=jnp.float32)]
    pallas_call x0 -> x3, Pallas kernels: none -> 12.1 us  [the longest x1 9.15 us: on_device(): pl.pallas_call(main_kernel, name='window_attention_backward', out_shape=(...]
    reshape x8 -> x0, local copies, waits for them, and re-layouts: 10.6 us -> none  [the longest x1 5.62 us: window_band(): windows(qkv).reshape(win_count, span_size, 3, head_count, head_size)]
    convert_element_type x2 -> x5, local copies, waits for them, and re-layouts: 10.4 us -> 0.44 us  [payload(): regions[row_slice, col_slice, None].astype(bf16)]
  transfers between devices with their start and end apart: 9 -> 11, of which waited for: 8 -> 6; matrix products, arithmetic and copies ran while one was open for 7% -> 3% of each run, Pallas kernels for 0% -> 2%
where the time goes in v1:
time: 61.3 us; the launch traced here: 61 us
  waiting for transfers between devices  22.4 us (37%)
  starting transfers between devices  17.9 us (29%)
  Pallas kernels  12.1 us (20%)
  local copies, waits for them, and re-layouts  6.45 us (11%)
  other arithmetic  1.31 us (2%)
  between operations  0.85 us (1%)
    ppermute x3, waiting for transfers between devices, sum_over_crop(): came = lax.ppermute(mine, ('row', 'col'), pairs)  14.8 us
    pallas_call x1, Pallas kernels, on_device(): pl.pallas_call(main_kernel, name='window_attention_backward', out_shape=(...  9.15 us
    ppermute x6, starting transfers between devices, from_behind(): lax.ppermute(shard, axis, [(i, (i + by) % count) for i in range(count)])  8.95 us
    ppermute x2, starting transfers between devices, diagonal(): return lax.ppermute(shard, ('row', 'col'), pairs)  7.82 us
    ppermute x2, waiting for transfers between devices, diagonal(): return lax.ppermute(shard, ('row', 'col'), pairs)  6.1 us
    unnamed x24, local copies, waits for them, and re-layouts  5.1 us
    pallas_call x1, Pallas kernels, on_device(): pl.pallas_call(functools.partial(finish_kernel, total_tokens ** (-0.5)),...  1.92 us
    ppermute x6, waiting for transfers between devices, from_behind(): lax.ppermute(shard, axis, [(i, (i + by) % count) for i in range(count)])  1.57 us
  transfers between devices with their start and end apart: 11, of which 6 were waited for; matrix products, arithmetic and copies ran while one was open for 3% of the time, Pallas kernels for 2%

profile of v1, /device:TPU:0, one launch (start us, length us, event | category | flops | bytes accessed | tf_op | source)
XLA Modules:
  0.0 61.0 jit_solution(16029258897796544462)
XLA Ops:
  0.6 0.0 copy-start.7
  0.6 1.3 %copy.37.tokens_ref = bf16[8,128,180]{2,1,0:T(8,128)(2,1)S(1)} copy(bf16[8,128,180]{1,0,2:T(8,128)(2,1)} %param.9) | data formatting | bytes 737280 | tf_op args[0]
  1.9 0.0 copy-done.7
  1.9 0.0 copy-start
  2.0 0.0 copy-start.4
  2.0 0.3 copy.38.grad_ref
  2.3 0.4 copy-done.4
  2.7 0.1 copy-done
  2.7 0.0 slice-start
  2.8 0.2 copy.30
  3.0 0.7 %slice-done = bf16[4,128,180]{2,1,0:T(8,128)(2,1)S(1)} async-done(((bf16[8,128,180]{2,1,0:T(8,128)(2,1)}), bf16[4,128,180]{2,1,0:T(8,128)(2,1)S(1)}, s32[]{:S(2)}) %slice-start) | async-done | bytes 184344 | tf_op jit(solution)/shard_map/slice | solution.py:400
  3.7 0.0 copy-start.1
  3.7 0.0 copy-start.2
  3.7 0.2 pad_maximum_fusion
  3.9 0.0 copy-start.3
  3.9 6.0 %collective-permute-start = (bf16[4,128,361]{2,1,0:T(8,128)(2,1)S(1)}, bf16[4,128,361]{2,1,0:T(8,128)(2,1)S(1)}, u32[]{:S(2)}, u32[]{:S(2)}) collective-permute-start(bf16[4,128,361]{2,1,0:T(8,128)(2,1)S(1)} %pad_maximum_fusion), channel_id=1, source_target_pairs={{0,14},{2,0},{4,2},{6,4},{8,6},{10,8},{12,10},{14,12},{1,15},{3,1}... | collective-permute-start | bytes 1109000 | tf_op jit(solution)/shard_map/ppermute | solution.py:356
  10.0 0.1 copy.33
  10.1 0.0 copy-done.1
  10.1 0.1 pad_maximum_fusion.1
  10.2 0.0 collective-permute-start.1
  10.2 0.1 copy.36
  10.4 0.0 copy-start.9
  10.4 0.1 pad_maximum_fusion.2
  10.4 0.0 copy-start.8
  10.4 0.8 %collective-permute-start.2 = (bf16[4,4,361]{2,1,0:T(4,128)(2,1)S(1)}, bf16[4,4,361]{2,1,0:T(4,128)(2,1)S(1)}, u32[]{:S(2)}, u32[]{:S(2)}) collective-permute-start(bf16[4,4,361]{2,1,0:T(4,128)(2,1)S(1)} %pad_maximum_fusion.2), channel_id=1, source_target_pairs={{0,15},{1,14},{2,1},{3,0},{4,3},{5,2},{6,5},{7,4},{8,7},{9,6},{10,... | collective-permute-start | bytes 34664 | tf_op jit(solution)/shard_map/ppermute | solution.py:364
  11.2 0.0 copy-done.9
  11.2 0.0 copy-done.8
  11.2 0.0 copy-start.5
  11.3 0.7 %copy-done.5 = f32[180]{0:T(256)S(1)} copy-done((f32[180]{0:T(256)S(1)}, f32[180]{0:T(256)}, u32[]{:S(2)}) %copy-start.5) | copy-done | bytes 744
  11.9 0.0 copy-start.6
  11.9 0.7 %copy-done.6 = f32[180]{0:T(256)S(1)} copy-done((f32[180]{0:T(256)S(1)}, f32[180]{0:T(256)}, u32[]{:S(2)}) %copy-start.6) | copy-done | bytes 744
  12.6 0.0 copy-done.2
  12.6 0.0 copy-done.3
  12.6 1.1 %prepare.1 = (f32[6,64,128]{2,1,0:T(8,128)S(1)}, bf16[3,256,192]{2,1,0:T(8,128)(2,1)S(1)}, bf16[3,192,256]{2,1,0:T(8,128)(2,1)S(1)}, bf16[192,180]{1,0:T(8,128)(2,1)S(1)}, bf16[3,180,180]{2,1,0:T(8,128)(2,1)S(1)}) custom-call(bf16[180,540]{1,0:T(8,128)(2,1)S(1)} %copy-done.2, f32[1,540]{1,0:T(1,128)S(1)} %broadcast_in_dim.20.offsets_ref, ...), custom_call_target="tpu_custom_call" | custom-call | tf_op jit(solution)/shard_map/prepare/pallas_call | solution.py:413
  13.7 0.0 collective-permute-done.1.right_ref
  13.7 4.9 %collective-permute-done.2.corner_ref = bf16[4,4,361]{2,1,0:T(4,128)(2,1)S(1)} collective-permute-done((bf16[4,4,361]{2,1,0:T(4,128)(2,1)S(1)}, bf16[4,4,361]{2,1,0:T(4,128)(2,1)S(1)}, u32[]{:S(2)}, u32[]{:S(2)}) %collective-permute-start.2) | collective-permute-done | bytes 11584 | tf_op jit(solution)/shard_map/ppermute | solution.py:364
  18.6 0.0 collective-permute-done.below_ref
  18.6 9.2 %window_attention_backward.1 = (bf16[4,128,180]{2,1,0:T(8,128)(2,1)S(1)}, bf16[4,128,180]{2,1,0:T(8,128)(2,1)S(1)}, bf16[8,4,180]{2,1,0:T(4,128)(2,1)S(1)}, bf16[1120,128]{1,0:T(8,128)(2,1)S(1)}) custom-call(bf16[8,128,180]{2,1,0:T(8,128)(2,1)S(1)} %copy-done.1, bf16[8,128,180]{2,1,0:T(8,128)(2,1)S(1)} %copy.38.grad_ref, s32[8,128]{1,0:T(8,128)S(1)} %copy-done.4, ...), custom_call_target="tpu_custom_call" | custom-call | tf_op jit(solution)/shard_map/window_attention_backward/pallas_call | solution.py:431
  27.8 0.1 collective-permute-start.6
  27.8 1.6 %collective-permute-done.6 = bf16[1120,128]{1,0:T(8,128)(2,1)S(1)} collective-permute-done((bf16[1120,128]{1,0:T(8,128)(2,1)S(1)}, bf16[1120,128]{1,0:T(8,128)(2,1)S(1)}, u32[]{:S(2)}, u32[]{:S(2)}) %collective-permute-start.6) | collective-permute-done | bytes 286752 | tf_op jit(solution)/shard_map/ppermute | solution.py:356
  29.4 0.3 collective-permute-start.7
  29.7 4.9 %collective-permute-done.7 = bf16[560,128]{1,0:T(8,128)(2,1)S(1)} collective-permute-done((bf16[560,128]{1,0:T(8,128)(2,1)S(1)}, bf16[560,128]{1,0:T(8,128)(2,1)S(1)}, u32[]{:S(2)}, u32[]{:S(2)}) %collective-permute-start.7) | collective-permute-done | bytes 143392 | tf_op jit(solution)/shard_map/ppermute | solution.py:384
  34.7 0.1 collective-permute-start.8
  34.7 6.5 %collective-permute-done.8 = bf16[560,128]{1,0:T(8,128)(2,1)S(1)} collective-permute-done((bf16[560,128]{1,0:T(8,128)(2,1)S(1)}, bf16[560,128]{1,0:T(8,128)(2,1)S(1)}, u32[]{:S(2)}, u32[]{:S(2)}) %collective-permute-start.8) | collective-permute-done | bytes 143392 | tf_op jit(solution)/shard_map/ppermute | solution.py:384
  41.3 0.7 %collective-permute-start.9 = (bf16[560,128]{1,0:T(8,128)(2,1)S(1)}, bf16[560,128]{1,0:T(8,128)(2,1)S(1)}, u32[]{:S(2)}, u32[]{:S(2)}) collective-permute-start(bf16[560,128]{1,0:T(8,128)(2,1)S(1)} %add_convert_fusion.1), channel_id=1, source_target_pairs={{0,8},{1,3},{2,10},{3,1},{4,12},{5,7},{6,14},{7,5},{8,0},{9,11},{1... | collective-permute-start | bytes 430088 | tf_op jit(solution)/shard_map/ppermute | solution.py:384
  42.1 2.7 %collective-permute-start.4 = (bf16[4,128,180]{2,1,0:T(8,128)(2,1)S(1)}, bf16[4,128,180]{2,1,0:T(8,128)(2,1)S(1)}, u32[]{:S(2)}, u32[]{:S(2)}) collective-permute-start(bf16[4,128,180]{2,1,0:T(8,128)(2,1)S(1)} %get-tuple-element.28), channel_id=1, source_target_pairs={{0,2},{2,4},{4,6},{6,8},{8,10},{10,12},{12,14},{14,0},{1,3},{3,5},... | collective-permute-start | bytes 552968 | tf_op jit(solution)/shard_map/ppermute | solution.py:356
  44.8 3.3 %collective-permute-done.9 = bf16[560,128]{1,0:T(8,128)(2,1)S(1)} collective-permute-done((bf16[560,128]{1,0:T(8,128)(2,1)S(1)}, bf16[560,128]{1,0:T(8,128)(2,1)S(1)}, u32[]{:S(2)}, u32[]{:S(2)}) %collective-permute-start.9) | collective-permute-done | bytes 143392 | tf_op jit(solution)/shard_map/ppermute | solution.py:384
  48.2 0.1 collective-permute-start.10
  48.3 7.0 %collective-permute-start.3 = (bf16[4,4,180]{2,1,0:T(4,128)(2,1)S(1)}, bf16[4,4,180]{2,1,0:T(4,128)(2,1)S(1)}, u32[]{:S(2)}, u32[]{:S(2)}) collective-permute-start(bf16[4,4,180]{2,1,0:T(4,128)(2,1)S(1)} %get-tuple-element.55), channel_id=1, source_target_pairs={{0,3},{1,2},{2,5},{3,4},{4,7},{5,6},{6,9},{7,8},{8,11},{9,10},{10,... | collective-permute-start | bytes 17288 | tf_op jit(solution)/shard_map/ppermute | solution.py:364
  55.3 0.0 collective-permute-start.5
  55.3 0.1 slice.54
  55.4 0.0 collective-permute-done.4
  55.4 0.1 slice.61
  55.5 1.2 %collective-permute-done.3 = bf16[4,4,180]{2,1,0:T(4,128)(2,1)S(1)} collective-permute-done((bf16[4,4,180]{2,1,0:T(4,128)(2,1)S(1)}, bf16[4,4,180]{2,1,0:T(4,128)(2,1)S(1)}, u32[]{:S(2)}, u32[]{:S(2)}) %collective-permute-start.3) | collective-permute-done | bytes 5792 | tf_op jit(solution)/shard_map/ppermute | solution.py:364
  56.7 0.0 collective-permute-done.5
  56.7 0.2 maximum_maximum_fusion
  56.8 1.0 %copy.39 = bf16[8,128,180]{1,0,2:T(8,128)(2,1)} copy(bf16[8,128,180]{2,1,0:T(8,128)(2,1)S(1)} %maximum_maximum_fusion) | data formatting | bytes 737280
  57.8 0.0 collective-permute-done.10.other_ref
  57.8 1.9 %finish.1 = (f32[180,540]{1,0:T(8,128)}, f32[1,540]{1,0:T(1,128)S(1)}, f32[180,180]{1,0:T(8,128)}, f32[225,6]{1,0:T(8,128)S(1)}, f32[1,180]{1,0:T(1,128)}, /*index=5*/f32[1,180]{1,0:T(1,128)}) custom-call(bf16[560,128]{1,0:T(8,128)(2,1)S(1)} %add_convert_fusion.mine_ref, bf16[560,128]{1,0:T(8,128)(2,1)S(1)} %collective-permute-done.10.other_ref, ...), custom_call_target="tpu_custom_call" | custom-call | tf_op jit(solution)/shard_map/finish/pallas_call | solution.py:485
  59.8 0.7 %copy.40 = f32[225,6]{0,1:T(8,128)} copy(f32[225,6]{1,0:T(8,128)S(1)} %get-tuple-element.48) | data formatting | bytes 10800
  60.4 0.6 reduce
  (14 shorter events, 0.2 us)
Async XLA Ops:
  0.6 1.3 %copy-start.7 = (bf16[8,128,180]{1,0,2:T(8,128)(2,1)S(1)}, bf16[8,128,180]{1,0,2:T(8,128)(2,1)}, u32[]{:S(2)}) copy-start(bf16[8,128,180]{1,0,2:T(8,128)(2,1)} %param.10) | copy-start | bytes 1105924
  1.9 0.8 %copy-start = (bf16[8,128,180]{2,1,0:T(8,128)(2,1)}, bf16[8,128,180]{2,1,0:T(8,128)(2,1)S(1)}, u32[]{:S(2)}) copy-start(bf16[8,128,180]{2,1,0:T(8,128)(2,1)S(1)} %copy.37.tokens_ref) | copy-start | bytes 1105924
  2.0 0.7 %copy-start.4 = (s32[8,128]{1,0:T(8,128)S(1)}, s32[8,128]{1,0:T(8,128)}, u32[]{:S(2)}) copy-start(s32[8,128]{1,0:T(8,128)} %region_ref.1) | copy-start | bytes 12292
  2.7 0.9 %slice-start = ((bf16[8,128,180]{2,1,0:T(8,128)(2,1)}), bf16[4,128,180]{2,1,0:T(8,128)(2,1)S(1)}, s32[]{:S(2)}) async-start(bf16[8,128,180]{2,1,0:T(8,128)(2,1)} %copy-done), calls=%async_computation | async-start | bytes 524288 | tf_op jit(solution)/shard_map/slice | solution.py:400
  3.7 6.4 %copy-start.1 = (bf16[8,128,180]{2,1,0:T(8,128)(2,1)S(1)}, bf16[8,128,180]{2,1,0:T(8,128)(2,1)}, u32[]{:S(2)}) copy-start(bf16[8,128,180]{2,1,0:T(8,128)(2,1)} %copy-done) | copy-start | bytes 1105924
  3.7 8.9 %copy-start.2 = (bf16[180,540]{1,0:T(8,128)(2,1)S(1)}, bf16[180,540]{1,0:T(8,128)(2,1)}, u32[]{:S(2)}) copy-start(bf16[180,540]{1,0:T(8,128)(2,1)} %weight_ref.3) | copy-start | bytes 583204
  3.9 8.7 %copy-start.3 = (bf16[180,180]{1,0:T(8,128)(2,1)S(1)}, bf16[180,180]{1,0:T(8,128)(2,1)}, u32[]{:S(2)}) copy-start(bf16[180,180]{1,0:T(8,128)(2,1)} %proj_ref.3) | copy-start | bytes 194404
  3.9 14.7 %collective-permute-start = (bf16[4,128,361]{2,1,0:T(8,128)(2,1)S(1)}, bf16[4,128,361]{2,1,0:T(8,128)(2,1)S(1)}, u32[]{:S(2)}, u32[]{:S(2)}) collective-permute-start(bf16[4,128,361]{2,1,0:T(8,128)(2,1)S(1)} %pad_maximum_fusion), channel_id=1, source_target_pairs={{0,14},{2,0},{4,2},{6,4},{8,6},{10,8},{12,10},{14,12},{1,15},{3,1}... | collective-permute-start | bytes 1109000 | tf_op jit(solution)/shard_map/ppermute | solution.py:356
  10.2 3.5 %collective-permute-start.1 = (bf16[4,4,361]{2,1,0:T(4,128)(2,1)S(1)}, bf16[4,4,361]{2,1,0:T(4,128)(2,1)S(1)}, u32[]{:S(2)}, u32[]{:S(2)}) collective-permute-start(bf16[4,4,361]{2,1,0:T(4,128)(2,1)S(1)} %pad_maximum_fusion.1), channel_id=1, source_target_pairs={{0,1},{1,0},{2,3},{3,2},{4,5},{5,4},{6,7},{7,6},{8,9},{9,8},{10,11... | collective-permute-start | bytes 34664 | tf_op jit(solution)/shard_map/ppermute | solution.py:356
  10.4 0.9 %copy-start.9 = (f32[540]{0:T(1024)S(1)}, f32[540]{0:T(1024)}, u32[]{:S(2)}) copy-start(f32[540]{0:T(1024)} %param.15) | copy-start | bytes 6484
  10.4 0.8 %copy-start.8 = (f32[225,6]{0,1:T(8,128)S(1)}, f32[225,6]{0,1:T(8,128)}, u32[]{:S(2)}) copy-start(f32[225,6]{0,1:T(8,128)} %param.17) | copy-start | bytes 16204
  10.4 8.2 %collective-permute-start.2 = (bf16[4,4,361]{2,1,0:T(4,128)(2,1)S(1)}, bf16[4,4,361]{2,1,0:T(4,128)(2,1)S(1)}, u32[]{:S(2)}, u32[]{:S(2)}) collective-permute-start(bf16[4,4,361]{2,1,0:T(4,128)(2,1)S(1)} %pad_maximum_fusion.2), channel_id=1, source_target_pairs={{0,15},{1,14},{2,1},{3,0},{4,3},{5,2},{6,5},{7,4},{8,7},{9,6},{10,... | collective-permute-start | bytes 34664 | tf_op jit(solution)/shard_map/ppermute | solution.py:364
  11.2 0.7 %copy-start.5 = (f32[180]{0:T(256)S(1)}, f32[180]{0:T(256)}, u32[]{:S(2)}) copy-start(f32[180]{0:T(256)} %param.12) | copy-start | bytes 2164
  11.9 0.7 %copy-start.6 = (f32[180]{0:T(256)S(1)}, f32[180]{0:T(256)}, u32[]{:S(2)}) copy-start(f32[180]{0:T(256)} %param.13) | copy-start | bytes 2164
  27.8 1.6 %collective-permute-start.6 = (bf16[1120,128]{1,0:T(8,128)(2,1)S(1)}, bf16[1120,128]{1,0:T(8,128)(2,1)S(1)}, u32[]{:S(2)}, u32[]{:S(2)}) collective-permute-start(bf16[1120,128]{1,0:T(8,128)(2,1)S(1)} %get-tuple-element.30), channel_id=1, source_target_pairs={{0,1},{1,0},{2,3},{3,2},{4,5},{5,4},{6,7},{7,6},{8,9},{9,8},{10,11... | collective-permute-start | bytes 860168 | tf_op jit(solution)/shard_map/ppermute | solution.py:356
  29.4 5.2 %collective-permute-start.7 = (bf16[560,128]{1,0:T(8,128)(2,1)S(1)}, bf16[560,128]{1,0:T(8,128)(2,1)S(1)}, u32[]{:S(2)}, u32[]{:S(2)}) collective-permute-start(bf16[560,128]{1,0:T(8,128)(2,1)S(1)} %add_convert_fusion.3), channel_id=1, source_target_pairs={{0,2},{1,5},{2,0},{3,7},{4,6},{5,1},{6,4},{7,3},{8,10},{9,13},{10,... | collective-permute-start | bytes 430088 | tf_op jit(solution)/shard_map/ppermute | solution.py:384
  34.7 6.6 %collective-permute-start.8 = (bf16[560,128]{1,0:T(8,128)(2,1)S(1)}, bf16[560,128]{1,0:T(8,128)(2,1)S(1)}, u32[]{:S(2)}, u32[]{:S(2)}) collective-permute-start(bf16[560,128]{1,0:T(8,128)(2,1)S(1)} %add_convert_fusion.2), channel_id=1, source_target_pairs={{0,4},{1,9},{2,6},{3,11},{4,0},{5,13},{6,2},{7,15},{8,12},{9,1},{1... | collective-permute-start | bytes 430088 | tf_op jit(solution)/shard_map/ppermute | solution.py:384
  41.3 6.8 %collective-permute-start.9 = (bf16[560,128]{1,0:T(8,128)(2,1)S(1)}, bf16[560,128]{1,0:T(8,128)(2,1)S(1)}, u32[]{:S(2)}, u32[]{:S(2)}) collective-permute-start(bf16[560,128]{1,0:T(8,128)(2,1)S(1)} %add_convert_fusion.1), channel_id=1, source_target_pairs={{0,8},{1,3},{2,10},{3,1},{4,12},{5,7},{6,14},{7,5},{8,0},{9,11},{1... | collective-permute-start | bytes 430088 | tf_op jit(solution)/shard_map/ppermute | solution.py:384
  42.1 13.3 %collective-permute-start.4 = (bf16[4,128,180]{2,1,0:T(8,128)(2,1)S(1)}, bf16[4,128,180]{2,1,0:T(8,128)(2,1)S(1)}, u32[]{:S(2)}, u32[]{:S(2)}) collective-permute-start(bf16[4,128,180]{2,1,0:T(8,128)(2,1)S(1)} %get-tuple-element.28), channel_id=1, source_target_pairs={{0,2},{2,4},{4,6},{6,8},{8,10},{10,12},{12,14},{14,0},{1,3},{3,5},... | collective-permute-start | bytes 552968 | tf_op jit(solution)/shard_map/ppermute | solution.py:356
  48.2 9.7 %collective-permute-start.10 = (bf16[560,128]{1,0:T(8,128)(2,1)S(1)}, bf16[560,128]{1,0:T(8,128)(2,1)S(1)}, u32[]{:S(2)}, u32[]{:S(2)}) collective-permute-start(bf16[560,128]{1,0:T(8,128)(2,1)S(1)} %add_convert_fusion.mine_ref), channel_id=1, source_target_pairs={{0,1},{1,0},{2,3},{3,2},{4,5},{5,4},{6,7},{7,6},{8,9},{9,8},{10,11... | collective-permute-start | bytes 430088 | tf_op jit(solution)/shard_map/ppermute | solution.py:356
  48.3 8.4 %collective-permute-start.3 = (bf16[4,4,180]{2,1,0:T(4,128)(2,1)S(1)}, bf16[4,4,180]{2,1,0:T(4,128)(2,1)S(1)}, u32[]{:S(2)}, u32[]{:S(2)}) collective-permute-start(bf16[4,4,180]{2,1,0:T(4,128)(2,1)S(1)} %get-tuple-element.55), channel_id=1, source_target_pairs={{0,3},{1,2},{2,5},{3,4},{4,7},{5,6},{6,9},{7,8},{8,11},{9,10},{10,... | collective-permute-start | bytes 17288 | tf_op jit(solution)/shard_map/ppermute | solution.py:364
  55.3 1.4 %collective-permute-start.5 = (bf16[4,4,180]{2,1,0:T(4,128)(2,1)S(1)}, bf16[4,4,180]{2,1,0:T(4,128)(2,1)S(1)}, u32[]{:S(2)}, u32[]{:S(2)}) collective-permute-start(bf16[4,4,180]{2,1,0:T(4,128)(2,1)S(1)} %get-tuple-element.56), channel_id=1, source_target_pairs={{0,1},{1,0},{2,3},{3,2},{4,5},{5,4},{6,7},{7,6},{8,9},{9,8},{10,11... | collective-permute-start | bytes 17288 | tf_op jit(solution)/shard_map/ppermute | solution.py:356

commit v2 on v1

--- a/solution.py
+++ b/solution.py
@@ -15,6 +15,7 @@
 LANES = 128
 SLOT = 32
 ROWS = 184
+DEEP = 184
 TABLE_ROWS = 16
 BUFFER_ROWS = 6 * ROWS + TABLE_ROWS
 
@@ -62,8 +63,61 @@
     return jnp.concatenate([rows[head * SLOT : head * SLOT + size] for head in range(HEADS)], 0)
 
 
-def prepare_kernel(weight_ref, offsets_ref, proj_ref, table_ref, bias_ref, tok_ref, chan_ref, proj_slots_ref, parts_ref):
+def pack_kernel(tokens_ref, grad_ref, region_ref, first_ref, second_ref, edge_ref):
+    channels = tokens_ref.shape[0]
+    f32, bf16 = jnp.float32, jnp.bfloat16
+    tokens = tokens_ref[...].astype(f32)
+    grad = grad_ref[...].astype(f32)
+    ids = region_ref[...].astype(f32)[None]
+    left = iota((1, 1, LANES), 2) < SPAN
+    first = jnp.where(left, tokens, pltpu.roll(grad, SPAN, 2)).astype(bf16)
+    second = jnp.where(left, pltpu.roll(tokens, SPAN, 2), grad).astype(bf16)
+    blank = jnp.zeros((DEEP - channels - 1,) + ids.shape[1:], bf16)
+    id_first = ids.astype(bf16)
+    id_second = pltpu.roll(ids, SPAN, 2).astype(bf16)
+    first_ref[0:channels] = first[:, 0:SHIFT]
+    first_ref[channels : channels + 1] = id_first[:, 0:SHIFT]
+    first_ref[channels + 1 :] = blank[:, 0:SHIFT]
+    second_ref[0:channels] = second[:, 0:SHIFT]
+    second_ref[channels : channels + 1] = id_second[:, 0:SHIFT]
+    second_ref[channels + 1 :] = blank[:, 0:SHIFT]
+    edge_ref[0:channels] = first
+    edge_ref[channels : channels + 1] = id_first
+    edge_ref[channels + 1 :] = blank
+
+
+def prepare_kernel(
+    tokens_ref,
+    grad_ref,
+    region_ref,
+    weight_ref,
+    offsets_ref,
+    proj_ref,
+    table_ref,
+    x_ref,
+    g_ref,
+    id_ref,
+    bias_ref,
+    tok_ref,
+    chan_ref,
+    proj_slots_ref,
+    parts_ref,
+    turn_s,
+):
     channels = weight_ref.shape[0]
+    wins = x_ref.shape[0]
+    f32 = jnp.float32
+    ids = region_ref[...].astype(f32).T
+    for source, target in ((tokens_ref, x_ref), (grad_ref, g_ref)):
+        turn_s[...] = source[...].astype(f32)
+        for r in range(SHIFT):
+            row = turn_s[:, SHIFT + r, :].T
+            row = jnp.concatenate([row[SHIFT:], row[:SHIFT]], 0)
+            target[:, r] = row.reshape(wins, WIN, channels)
+    for r in range(SHIFT):
+        row = ids[:, SHIFT + r : SHIFT + r + 1]
+        row = jnp.concatenate([row[SHIFT:], row[:SHIFT]], 0)
+        id_ref[:, r] = row.reshape(wins, WIN, 1)
     for part in range(3):
         weight = weight_ref[:, part * channels : (part + 1) * channels].astype(jnp.float32)
         parts_ref[part] = weight.astype(jnp.bfloat16)
@@ -99,75 +153,103 @@
                 bias_ref[head, rj * WIN + cj : rj * WIN + cj + 1, :] = both[head : head + 1, :]
 
 
-def main_kernel(
-    tokens_ref,
-    grad_ref,
-    region_ref,
-    below_ref,
-    right_ref,
-    corner_ref,
-    gain_ref,
-    offset_ref,
-    bias_ref,
-    tok_ref,
-    chan_ref,
-    proj_ref,
-    proj_slots_ref,
-    parts_ref,
-    own_ref,
-    down_ref,
-    over_ref,
-    sums_ref,
-    x_s,
-    g_s,
-    id_s,
-    unit_s,
-    inv_s,
-    unit_low_s,
-    normed_s,
-    grad_s,
-    q_tok_s,
-    k_tok_s,
-    v_tok_s,
-    da_tok_s,
-    q_chan_s,
-    k_chan_s,
-    v_chan_s,
-    da_chan_s,
-    attended_s,
-    d_qkv_s,
-    score_s,
-    out_s,
-    pack_s,
+def unpack(payload_ref, turn_s, lo):
+    turn_s[...] = payload_ref[...].astype(jnp.float32)
+    rows = []
+    for r in range(lo, lo + SHIFT):
+        row = turn_s[:, r, :].T
+        rows.append((row[0:SPAN], row[SPAN:]))
+    return rows
+
+
+def windows_kernel(
+    last,
+    first_win,
+    *refs,
 ):
-    rows, cols, channels = tokens_ref.shape
+    if last:
+        (payload_ref, payload_two_ref, edge_ref, corner_ref, sums_in_ref, score_in_ref) = refs[:6]
+        refs = refs[6:]
+    else:
+        payload_ref = refs[0]
+        refs = refs[1:]
+    (
+        own_x_ref,
+        own_g_ref,
+        own_id_ref,
+        gain_ref,
+        offset_ref,
+        bias_ref,
+        tok_ref,
+        chan_ref,
+        proj_ref,
+        proj_slots_ref,
+        d_qkv_s,
+        unit_s,
+        inv_s,
+        g_s,
+        sums_ref,
+    ) = refs[:15]
+    refs = refs[15:]
+    if last:
+        score_s = refs[-1]
+        pack_s = refs[-2]
+        refs = refs[:-2]
+    else:
+        score_s = refs[0]
+        refs = refs[1:]
+    (
+        turn_s,
+        turn_two_s,
+        x_s,
+        id_s,
+        unit_low_s,
+        normed_s,
+        grad_s,
+        q_tok_s,
+        k_tok_s,
+        v_tok_s,
+        da_tok_s,
+        q_chan_s,
+        k_chan_s,
+        v_chan_s,
+        da_chan_s,
+        attended_s,
+    ) = refs
+    wins, rows = x_s.shape[0:2]
+    channels = g_s.shape[-1]
     head_size = channels // HEADS
     scale = head_size ** (-0.5)
+    cols = wins * WIN
     count = rows * cols
-    wins = cols // WIN
     f32 = jnp.float32
     bf16 = jnp.bfloat16
 
+    here = slice(first_win, first_win + wins)
     x_s[:, :, :, LANES:] = jnp.zeros(x_s.shape[:3] + (LANES,), f32)
-    ids = region_ref[...].astype(f32).T
-    for r in range(rows):
-        if r < rows - SHIFT:
-            x_body = tokens_ref[r + SHIFT].astype(f32)
-            g_body = grad_ref[r + SHIFT].astype(f32)
-            side = right_ref[r].astype(f32)
-            id_body = ids[:, r + SHIFT : r + SHIFT + 1]
+    x_s[:, 0:SHIFT, :, 0:channels] = own_x_ref[here]
+    g_s[:, 0:SHIFT] = own_g_ref[here]
+    id_s[:, 0:SHIFT] = own_id_ref[here]
+    start = SHIFT + first_win * WIN
+    halves = [unpack(payload_ref, turn_s, 0)]
+    if last:
+        halves.append(unpack(payload_two_ref, turn_s, 0))
+        corner = unpack(corner_ref, turn_s, 0)
+        edge = unpack(edge_ref, turn_two_s, SHIFT)
+    for r in range(SHIFT):
+        if last:
+            x_row = jnp.concatenate([halves[0][r][0][start:], halves[1][r][0], corner[r][0][:SHIFT]], 0)
+            g_row = jnp.concatenate([halves[0][r][1][start:], halves[1][r][1], corner[r][1][:SHIFT]], 0)
         else:
-            payload = below_ref[r - (rows - SHIFT)].astype(f32)
-            x_body = payload[:, 0:channels]
-            g_body = payload[:, channels : 2 * channels]
-            id_body = payload[:, 2 * channels : 2 * channels + 1]
-            side = corner_ref[r - (rows - SHIFT)].astype(f32)
-        x_row = jnp.concatenate([x_body[SHIFT:], side[:, 0:channels]], 0)
-        g_row = jnp.concatenate([g_body[SHIFT:], side[:, channels : 2 * channels]], 0)
-        id_row = jnp.concatenate([id_body[SHIFT:], side[:, 2 * channels : 2 * channels + 1]], 0)
-        x_s[:, r, :, 0:channels] = x_row.reshape(wins, WIN, channels)
-        g_s[:, r, :, :] = g_row.reshape(wins, WIN, channels)
-        id_s[:, r, :, :] = id_row.reshape(wins, WIN, 1)
+            x_row = halves[0][r][0][start : start + cols]
+            g_row = halves[0][r][1][start : start + cols]
+        x_s[:, SHIFT + r, :, 0:channels] = x_row[:, 0:channels].reshape(wins, WIN, channels)
+        g_s[:, SHIFT + r] = g_row[:, 0:channels].reshape(wins, WIN, channels)
+        id_s[:, SHIFT + r] = x_row[:, channels : channels + 1].reshape(wins, WIN, 1)
+        if last:
+            x_s[wins - 1, r, SHIFT:, 0:channels] = edge[r][0][:SHIFT, 0:channels]
+            g_s[wins - 1, r, SHIFT:, :] = edge[r][1][:SHIFT, 0:channels]
+            id_s[wins - 1, r, SHIFT:, :] = edge[r][0][:SHIFT, channels : channels + 1]
 
     x = x_s[...].reshape(count, 2 * LANES)
     lane = iota((1, 2 * LANES), 1)
@@ -195,7 +277,7 @@
     v_chan_s[...] = nt(chan_ref[2], normed).astype(bf16)
     da_chan_s[...] = nt(proj_slots_ref[...], grad_s[...]).astype(bf16)
 
-    score_s[...] = jnp.zeros(score_s.shape, f32)
+    score_s[...] = score_in_ref[...] if last else jnp.zeros(score_s.shape, f32)
     first = iota((1, LANES), 1) < SPAN
     first_low = jnp.where(first, 1.0, 0.0).astype(bf16)
     second_low = jnp.where(first, 0.0, 1.0).astype(bf16)
@@ -266,8 +348,13 @@
     pieces.append(
         jnp.concatenate([unslot(d_proj, head_size), jnp.zeros((ROWS - channels, channels), f32)], 0)
     )
+    if not last:
+        for at, piece in enumerate(pieces):
+            sums_ref[at] = piece
+        return
     pack_s[...] = jnp.zeros(pack_s.shape, f32)
     for at, piece in enumerate(pieces):
+        piece = piece + sums_in_ref[at]
         pack_s[at * ROWS : (at + 1) * ROWS, :] = piece[:, 0:LANES]
         low = (4 + at // 2) * ROWS
         side = (at % 2) * SPAN
@@ -293,19 +380,25 @@
     pack_s[6 * ROWS + 8 : 6 * ROWS + 8 + HEADS, :] = table[:, LANES:]
     sums_ref[...] = pack_s[...].astype(bf16)
 
-    d_normed = nt(d_qkv_s[0], parts_ref[0]) + nt(d_qkv_s[1], parts_ref[1]) + nt(d_qkv_s[2], parts_ref[2])
-    scaled = d_normed * gain_ref[:, 0:channels]
-    unit = unit_s[:, 0:channels]
-    mean_one = jnp.sum(scaled, -1, keepdims=True) * (1.0 / channels)
-    mean_two = jnp.sum(scaled * unit, -1, keepdims=True) * (1.0 / channels)
-    d_input = inv_s[...] * (scaled - mean_one - unit * mean_two)
-    out_s[...] = g_s[...] + d_input.reshape(wins, rows, WIN, channels)
-    for r in range(rows):
-        row = out_s[:, r].reshape(cols, channels)
-        moved = jnp.concatenate([row[cols - SHIFT :], row[: cols - SHIFT]], 0).astype(bf16)
-        target, place = (own_ref, r) if r < rows - SHIFT else (down_ref, r - (rows - SHIFT))
-        target[place] = moved
-        over_ref[r] = row[cols - SHIFT :].astype(bf16)
+def input_kernel(*refs):
+    blocks = [refs[0:4], refs[4:8]]
+    gain_ref, parts_ref, out_ref, turn_s = refs[8:]
+    f32 = jnp.float32
+    channels = parts_ref.shape[1]
+    done = []
+    for d_qkv_ref, unit_ref, inv_ref, g_ref in blocks:
+        d_normed = sum(nt(d_qkv_ref[part], parts_ref[part]) for part in range(3))
+        scaled = d_normed * gain_ref[:, 0:channels]
+        unit = unit_ref[:, 0:channels]
+        mean_one = jnp.sum(scaled, -1, keepdims=True) * (1.0 / channels)
+        mean_two = jnp.sum(scaled * unit, -1, keepdims=True) * (1.0 / channels)
+        d_input = inv_ref[...] * (scaled - mean_one - unit * mean_two)
+        done.append(g_ref[...] + d_input.reshape(g_ref.shape))
+    for r in range(turn_s.shape[1]):
+        row = jnp.concatenate([block[:, r].reshape(-1, channels) for block in done], 0)
+        row = jnp.concatenate([row[-SHIFT:], row[:-SHIFT]], 0)
+        turn_s[:, r, :] = row.T
+    out_ref[...] = turn_s[...].astype(out_ref.dtype)
 
 
 def finish_kernel(out_scale, mine_ref, other_ref, core_ref, weight_ref, gain_ref, offset_ref, d_weight_ref, d_bias_ref, d_proj_ref, d_table_ref, d_gain_ref, d_offset_ref):
@@ -356,14 +449,6 @@
     return lax.ppermute(shard, axis, [(i, (i + by) % count) for i in range(count)])
 
 
-def diagonal(shard, by):
-    rows, cols = lax.axis_size("row"), lax.axis_size("col")
-    pairs = [
-        (r * cols + c, ((r + by) % rows) * cols + (c + by) % cols) for r in range(rows) for c in range(cols)
-    ]
-    return lax.ppermute(shard, ("row", "col"), pairs)
-
-
 def sum_over_crop(buffer):
     rows, cols = lax.axis_size("row"), lax.axis_size("col")
     half = buffer.shape[0] // cols
@@ -392,111 +477,117 @@
     rows, cols, channels = tokens.shape
     f32, bf16 = jnp.float32, jnp.bfloat16
     count = rows * cols
+    wins = cols // WIN
+    wide = HEADS * SLOT
     params = pltpu.CompilerParams(vmem_limit_bytes=VMEM_LIMIT)
 
-    def payload(row_slice, col_slice):
-        return jnp.concatenate(
-            [
-                tokens[row_slice, col_slice],
-                grad_out[row_slice, col_slice],
-                regions[row_slice, col_slice, None].astype(bf16),
-            ],
-            -1,
-        )
-
-    below = from_behind(payload(slice(0, SHIFT), slice(None)), "row", -1)
-    right = from_behind(payload(slice(SHIFT, None), slice(0, SHIFT)), "col", -1)
-    corner = diagonal(payload(slice(0, SHIFT), slice(0, SHIFT)), -1)
+    def call(kernel, name, ins, outs, scratch=()):
+        return pl.pallas_call(
+            kernel,
+            name=name,
+            out_shape=tuple(jax.ShapeDtypeStruct(*out) for out in outs),
+            in_specs=[whole(pltpu.SMEM) if value.dtype == jnp.int32 and value.ndim == 1 else whole() for value in ins],
+            out_specs=(whole(),) * len(outs),
+            scratch_shapes=[pltpu.VMEM(*each) for each in scratch],
+            compiler_params=params,
+        )(*ins)
+
+    x_turned = tokens.transpose(2, 0, 1)
+    g_turned = grad_out.transpose(2, 0, 1)
+    thin = ((DEEP, SHIFT, cols), bf16)
+    first, second, edge = call(
+        pack_kernel, "pack", (x_turned, g_turned, regions), (thin, thin, ((DEEP, rows, cols), bf16))
+    )
+    below = from_behind(first, "row", -1)
+    below_two = from_behind(second, "row", -1)
+    edge = from_behind(edge, "col", -1)
 
     table = jnp.pad(bias_table.T, ((0, 8 - HEADS), (0, 2 * LANES - bias_table.shape[0])))
-    wide = HEADS * SLOT
-    bias, tok, chan, proj_slots, parts = pl.pallas_call(
+    own_x, own_g, own_id, bias, tok, chan, proj_slots, parts = call(
         prepare_kernel,
-        name="prepare",
-        out_shape=(
-            jax.ShapeDtypeStruct((HEADS, SPAN, LANES), f32),
-            jax.ShapeDtypeStruct((3, 2 * LANES, wide), bf16),
-            jax.ShapeDtypeStruct((3, wide, 2 * LANES), bf16),
-            jax.ShapeDtypeStruct((wide, channels), bf16),
-            jax.ShapeDtypeStruct((3, channels, channels), bf16),
+        "prepare",
+        (x_turned, g_turned, regions, qkv_weight, qkv_bias[None], proj_weight, table),
+        (
+            ((wins, SHIFT, WIN, channels), f32),
+            ((wins, SHIFT, WIN, channels), f32),
+            ((wins, SHIFT, WIN, 1), f32),
+            ((HEADS, SPAN, LANES), f32),
+            ((3, 2 * LANES, wide), bf16),
+            ((3, wide, 2 * LANES), bf16),
+            ((wide, channels), bf16),
+            ((3, channels, channels), bf16),
         ),
-        in_specs=[whole()] * 4,
-        out_specs=(whole(),) * 5,
-        compiler_params=params,
-    )(qkv_weight, qkv_bias[None], proj_weight, table)
-
+        (((channels, rows, cols), f32),),
+    )
     gain = jnp.pad(ln_gain, (0, 2 * LANES - channels))[None]
     offset = jnp.pad(ln_offset, (0, 2 * LANES - channels))[None]
-    wins = cols // WIN
-    own, down, over, sums = pl.pallas_call(
-        main_kernel,
-        name="window_attention_backward",
-        out_shape=(
-            jax.ShapeDtypeStruct((SHIFT, cols, channels), bf16),
-            jax.ShapeDtypeStruct((SHIFT, cols, channels), bf16),
-            jax.ShapeDtypeStruct((rows, SHIFT, channels), bf16),
-            jax.ShapeDtypeStruct((BUFFER_ROWS, LANES), bf16),
-        ),
-        in_specs=[whole()] * 14,
-        out_specs=(whole(),) * 4,
-        scratch_shapes=[
-            pltpu.VMEM((wins, rows, WIN, 2 * LANES), f32),
-            pltpu.VMEM((wins, rows, WIN, channels), f32),
-            pltpu.VMEM((wins, rows, WIN, 1), f32),
-            pltpu.VMEM((count, 2 * LANES), f32),
-            pltpu.VMEM((count, 1), f32),
-            pltpu.VMEM((count, 2 * LANES), bf16),
-            pltpu.VMEM((count, 2 * LANES), bf16),
-            pltpu.VMEM((count, channels), bf16),
-            pltpu.VMEM((count, channels), bf16),
-            pltpu.VMEM((count, wide), bf16),
-            pltpu.VMEM((count, wide), bf16),
-            pltpu.VMEM((count, channels), bf16),
-            pltpu.VMEM((wide, count), bf16),
-            pltpu.VMEM((wide, count), bf16),
-            pltpu.VMEM((wide, count), bf16),
-            pltpu.VMEM((wide, count), bf16),
-            pltpu.VMEM((wide, count), bf16),
-            pltpu.VMEM((3, count, channels), bf16),
-            pltpu.VMEM((HEADS, SPAN, LANES), f32),
-            pltpu.VMEM((wins, rows, WIN, channels), f32),
-            pltpu.VMEM((BUFFER_ROWS, LANES), f32),
-        ],
-        compiler_params=params,
-    )(
-        tokens, grad_out, regions, below, right, corner, gain, offset, bias, tok, chan, proj_weight, proj_slots, parts
+    shared = (own_x, own_g, own_id, gain, offset, bias, tok, chan, proj_weight, proj_slots)
+
+    def block(first_win, n, last, ins, name):
+        here = n * SPAN
+        outs = [
+            ((3, here, channels), bf16),
+            ((here, 2 * LANES), f32),
+            ((here, 1), f32),
+            ((n, rows, WIN, channels), f32),
+        ]
+        score = ((HEADS, SPAN, LANES), f32)
+        scratch = [
+            ((DEEP, SHIFT, cols), f32),
+            ((DEEP, rows, cols), f32),
+            ((n, rows, WIN, 2 * LANES), f32),
+            ((n, rows, WIN, 1), f32),
+            ((here, 2 * LANES), bf16),
+            ((here, 2 * LANES), bf16),
+            ((here, channels), bf16),
+            ((here, channels), bf16),
+            ((here, wide), bf16),
+            ((here, wide), bf16),
+            ((here, channels), bf16),
+        ] + [((wide, here), bf16)] * 5
+        if last:
+            outs += [((BUFFER_ROWS, LANES), bf16)]
+            scratch += [((BUFFER_ROWS, LANES), f32), score]
+        else:
+            outs += [((4, ROWS, channels), f32), score]
+        return call(functools.partial(windows_kernel, last, first_win), name, ins + shared, outs, scratch)
+
+    early = (cols // 2 - SHIFT) // (2 * WIN) * 2
+    corner = from_behind(below, "col", -1)
+    *one, part_sums, score = block(0, early, False, (below,), "windows_left")
+    *two, sums = block(
+        early, wins - early, True, (below, below_two, edge, corner, part_sums, score), "windows_right"
     )
 
     mine, other = sum_over_crop(sums)
 
-    from_above = from_behind(down, "row", 1)
-    from_left = from_behind(over[: rows - SHIFT], "col", 1)
-    from_corner = diagonal(over[rows - SHIFT :], 1)
-    d_tokens = jnp.concatenate(
-        [
-            jnp.concatenate([from_corner, from_above[:, SHIFT:]], 1),
-            jnp.concatenate([from_left, own[:, SHIFT:]], 1),
-        ],
-        0,
-    )
+    (framed,) = call(
+        input_kernel,
+        "input_backward",
+        (*one, *two, gain, parts),
+        (((channels, rows, cols), bf16),),
+        (((channels, rows, cols), f32),),
+    )
+    beside = from_behind(framed, "col", 1)
+    framed = jnp.where(jnp.arange(cols) < SHIFT, beside, framed)
+    above = from_behind(framed[:, rows - SHIFT :], "row", 1)
+    d_tokens = jnp.concatenate([above, framed[:, : rows - SHIFT]], 1).transpose(1, 2, 0)
 
     total_tokens = count * lax.axis_size("row") * lax.axis_size("col")
     core = lax.axis_index("col").astype(jnp.int32).reshape(1)
-    d_weight, d_bias, d_proj, d_table, d_gain, d_offset = pl.pallas_call(
+    d_weight, d_bias, d_proj, d_table, d_gain, d_offset = call(
         functools.partial(finish_kernel, total_tokens ** (-0.5)),
-        name="finish",
-        out_shape=(
-            jax.ShapeDtypeStruct(qkv_weight.shape, f32),
-            jax.ShapeDtypeStruct((1,) + qkv_bias.shape, f32),
-            jax.ShapeDtypeStruct(proj_weight.shape, f32),
-            jax.ShapeDtypeStruct(bias_table.shape, f32),
-            jax.ShapeDtypeStruct((1,) + ln_gain.shape, f32),
-            jax.ShapeDtypeStruct((1,) + ln_offset.shape, f32),
+        "finish",
+        (mine, other, core, qkv_weight, ln_gain[None], ln_offset[None]),
+        (
+            (qkv_weight.shape, f32),
+            ((1,) + qkv_bias.shape, f32),
+            (proj_weight.shape, f32),
+            (bias_table.shape, f32),
+            ((1,) + ln_gain.shape, f32),
+            ((1,) + ln_offset.shape, f32),
         ),
-        in_specs=[whole(), whole(), whole(pltpu.SMEM), whole(), whole(), whole()],
-        out_specs=(whole(),) * 6,
-        compiler_params=params,
-    )(mine, other, core, qkv_weight, ln_gain[None], ln_offset[None])
+    )
     return (d_tokens, d_weight, d_bias[0], d_proj, d_table, d_gain[0], d_offset[0])
 
 

time: 61.3 us -> 60.3 us (0.984)
  starting transfers between devices: 17.9 us -> 11.9 us
  Pallas kernels: 12.1 us -> 16.3 us
  other arithmetic: 1.31 us -> 2.73 us
    ppermute x6 -> x8, waiting for transfers between devices: 1.57 us -> 11 us  [from_behind(): lax.ppermute(shard, axis, [(i, (i + by) % count) for i in range(count)])]
    ppermute x2 -> x0, starting transfers between devices: 7.82 us -> none  [diagonal(): return lax.ppermute(shard, ('row', 'col'), pairs)]
    ppermute x2 -> x0, waiting for transfers between devices: 6.1 us -> none  [diagonal(): return lax.ppermute(shard, ('row', 'col'), pairs)]
    pallas_call x3 -> x6, Pallas kernels: 12.1 us -> 16.3 us  [call(): pl.pallas_call(kernel, name=name, out_shape=tuple((jax.ShapeDtypeStruct(*...]
    ppermute x3, waiting for transfers between devices: 14.8 us -> 11.2 us  [sum_over_crop(): came = lax.ppermute(mine, ('row', 'col'), pairs)]
    ppermute x3, starting transfers between devices: 1.08 us -> 2.92 us  [sum_over_crop(): came = lax.ppermute(mine, ('row', 'col'), pairs)]
    convert_element_type x1, other arithmetic: 0.04 us -> 1.02 us  [sum_over_crop(): mine = mine.astype(jnp.bfloat16)]
    transpose x0 -> x1, other arithmetic: none -> 0.93 us  [on_device(): jnp.concatenate([above, framed[:, :rows - SHIFT]], 1).transpose(1, 2, 0)]
  transfers between devices with their start and end apart: 11 -> 11, of which waited for: 6 -> 6; matrix products, arithmetic and copies ran while one was open for 3% -> 2% of each run, Pallas kernels for 2% -> 11%
where the time goes in v2:
time: 60.3 us; the launch traced here: 60 us
  waiting for transfers between devices  22.1 us (37%)
  Pallas kernels  16.3 us (27%)
  starting transfers between devices  11.9 us (20%)
  local copies, waits for them, and re-layouts  6.03 us (10%)
  other arithmetic  2.73 us (5%)
  between operations  0.8 us (1%)
    pallas_call x6, Pallas kernels, call(): pl.pallas_call(kernel, name=name, out_shape=tuple((jax.ShapeDtypeStruct(*...  16.3 us
    ppermute x3, waiting for transfers between devices, sum_over_crop(): came = lax.ppermute(mine, ('row', 'col'), pairs)  11.2 us
    ppermute x8, waiting for transfers between devices, from_behind(): lax.ppermute(shard, axis, [(i, (i + by) % count) for i in range(count)])  11 us
    ppermute x8, starting transfers between devices, from_behind(): lax.ppermute(shard, axis, [(i, (i + by) % count) for i in range(count)])  9.02 us
    unnamed x25, local copies, waits for them, and re-layouts  5.9 us
    ppermute x3, starting transfers between devices, sum_over_crop(): came = lax.ppermute(mine, ('row', 'col'), pairs)  2.92 us
  transfers between devices with their start and end apart: 11, of which 6 were waited for; matrix products, arithmetic and copies ran while one was open for 2% of the time, Pallas kernels for 11%

profile of v2, /device:TPU:0, one launch (start us, length us, event | category | flops | bytes accessed | tf_op | source)
XLA Modules:
  0.0 60.0 jit_solution(7727230720460895836)
XLA Ops:
  0.6 0.0 copy-start
  0.6 1.0 %copy-done = bf16[8,128,180]{1,0,2:T(8,128)(2,1)S(1)} copy-done((bf16[8,128,180]{1,0,2:T(8,128)(2,1)S(1)}, bf16[8,128,180]{1,0,2:T(8,128)(2,1)}, u32[]{:S(2)}) %copy-start) | copy-done | bytes 368664
  1.6 0.0 copy-start.1
  1.6 1.0 %copy-done.1 = bf16[8,128,180]{1,0,2:T(8,128)(2,1)S(1)} copy-done((bf16[8,128,180]{1,0,2:T(8,128)(2,1)S(1)}, bf16[8,128,180]{1,0,2:T(8,128)(2,1)}, u32[]{:S(2)}) %copy-start.1) | copy-done | bytes 368664
  2.6 0.0 copy-start.7
  2.6 0.7 %copy-done.7 = s32[8,128]{1,0:T(8,128)S(1)} copy-done((s32[8,128]{1,0:T(8,128)S(1)}, s32[8,128]{1,0:T(8,128)}, u32[]{:S(2)}) %copy-start.7) | copy-done | bytes 4120
  3.3 0.0 copy-start.11
  3.3 0.0 copy-start.3
  3.3 0.0 copy-start.4
  3.3 0.3 pack.1
  3.6 0.0 copy-start.10
  3.6 6.0 %collective-permute-start = (bf16[184,4,128]{2,1,0:T(4,128)(2,1)S(1)}, bf16[184,4,128]{2,1,0:T(4,128)(2,1)S(1)}, u32[]{:S(2)}, u32[]{:S(2)}) collective-permute-start(bf16[184,4,128]{2,1,0:T(4,128)(2,1)S(1)} %get-tuple-element.35), channel_id=1, source_target_pairs={{0,14},{2,0},{4,2},{6,4},{8,6},{10,8},{12,10},{14,12},{1,15},{3,1}... | collective-permute-start | bytes 565256 | tf_op jit(solution)/shard_map/ppermute | solution.py:449
  9.7 0.0 collective-permute-start.2
  9.7 0.5 collective-permute-start.1
  10.2 4.6 %collective-permute-done.refs_0_ = bf16[184,4,128]{2,1,0:T(4,128)(2,1)S(1)} collective-permute-done((bf16[184,4,128]{2,1,0:T(4,128)(2,1)S(1)}, bf16[184,4,128]{2,1,0:T(4,128)(2,1)S(1)}, u32[]{:S(2)}, u32[]{:S(2)}) %collective-permute-start) | collective-permute-done | bytes 188448 | tf_op jit(solution)/shard_map/ppermute | solution.py:449
  14.8 0.0 collective-permute-start.3
  14.8 0.0 copy-done.11
  14.8 0.0 copy-done.10
  14.8 0.0 copy-start.8
  14.8 0.7 %copy-done.8 = f32[180]{0:T(256)S(1)} copy-done((f32[180]{0:T(256)S(1)}, f32[180]{0:T(256)}, u32[]{:S(2)}) %copy-start.8) | copy-done | bytes 744
  15.5 0.0 copy-start.9
  15.5 0.7 %copy-done.9 = f32[180]{0:T(256)S(1)} copy-done((f32[180]{0:T(256)S(1)}, f32[180]{0:T(256)}, u32[]{:S(2)}) %copy-start.9) | copy-done | bytes 744
  16.2 0.0 copy-done.3
  16.2 0.0 copy-done.4
  16.2 1.6 %prepare.1 = (f32[16,4,8,180]{3,2,1,0:T(8,128)S(1)}, f32[16,4,8,180]{3,2,1,0:T(8,128)S(1)}, f32[16,4,8,1]{3,2,1,0:T(8,128)S(1)}, f32[6,64,128]{2,1,0:T(8,128)S(1...) custom-call(bf16[180,8,128]{2,1,0:T(8,128)(2,1)S(1)} %bitcast.13, ...), custom_call_target="tpu_custom_call" | custom-call | tf_op jit(solution)/shard_map/prepare/pallas_call | solution.py:485
  17.8 3.7 %windows_left.1 = (bf16[3,384,180]{2,1,0:T(8,128)(2,1)S(1)}, f32[384,256]{1,0:T(8,128)S(1)}, f32[384,1]{1,0:T(8,128)S(1)}, f32[6,8,8,180]{3,2,1,0:T(8,128)S(1)},...) custom-call(bf16[184,4,128]{2,1,0:T(4,128)(2,1)S(1)} %collective-permute-done.refs_0_, ...), custom_call_target="tpu_custom_call" | custom-call | tf_op jit(solution)/shard_map/windows_left/pallas_call | solution.py:485
  21.5 0.0 copy-start.5
  21.5 0.0 collective-permute-done.1.refs_1_
  21.5 0.0 collective-permute-done.2.refs_2_
  21.5 0.0 collective-permute-done.3.refs_3_
  21.5 7.4 %windows_right.1 = (bf16[3,640,180]{2,1,0:T(8,128)(2,1)}, f32[640,256]{1,0:T(8,128)S(1)}, f32[640,1]{1,0:T(8,128)S(1)}, f32[10,8,8,180]{3,2,1,0:T(8,128)S(1)}, bf16[1120,128]{1,0:T(8,128)(2,1)}) custom-call(bf16[184,4,128]{2,1,0:T(4,128)(2,1)S(1)} %collective-permute-done.refs_0_, bf16[184,4,128]{2,1,0:T(4,128)(2,1)S(1)} %collective-permute-done.1.refs_1_, ...), custom_call_target="tpu_custom_call" | custom-call | tf_op jit(solution)/shard_map/windows_right/pallas_call | solution.py:485
  28.9 0.0 copy-done.5
  28.9 0.5 collective-permute-start.6
  29.4 0.0 copy-start.6
  29.4 1.5 %collective-permute-done.6 = bf16[1120,128]{1,0:T(8,128)(2,1)} collective-permute-done((bf16[1120,128]{1,0:T(8,128)(2,1)}, bf16[1120,128]{1,0:T(8,128)(2,1)}, u32[]{:S(2)}, u32[]{:S(2)}) %collective-permute-start.6) | collective-permute-done | bytes 286752 | tf_op jit(solution)/shard_map/ppermute | solution.py:449
  30.9 1.0 %add_convert_fusion.3 = bf16[560,128]{1,0:T(8,128)(2,1)S(1)} fusion(bf16[1120,128]{1,0:T(8,128)(2,1)} %collective-permute-done.6, s32[]{:T(128)S(6)} %select_n.9, bf16[1120,128]{1,0:T(8,128)(2,1)} %get-tuple-element.56), kind=kLoop, calls=%fused_computation.5 | loop fusion | flops 286720 | bytes 430084 | tf_op jit(solution)/shard_map/convert_element_type | solution.py:461
  31.9 0.4 collective-permute-start.7
  32.3 0.0 copy-done.6
  32.3 0.0 copy-start.2
  32.3 1.2 %copy-done.2 = bf16[3,640,180]{2,1,0:T(8,128)(2,1)S(1)} copy-done((bf16[3,640,180]{2,1,0:T(8,128)(2,1)S(1)}, bf16[3,640,180]{2,1,0:T(8,128)(2,1)}, u32[]{:S(2)}) %copy-start.2) | copy-done | bytes 691224
  33.5 1.5 %input_backward.1 = bf16[180,8,128]{2,1,0:T(8,128)(2,1)S(1)} custom-call(bf16[3,384,180]{2,1,0:T(8,128)(2,1)S(1)} %get-tuple-element.43.refs_0_, f32[384,256]{1,0:T(8,128)S(1)} %get-tuple-element.44.refs_1_, f32[384,1]{1,0:T(8,128)S(1)} %copy-done.6, f32[6,8,8,180]{3,2,1,0:T(8,128)S(1)} %get-tuple-element.46.refs_3_, bf16[3,640,180]{2,1,0:T(8,128)(2,1)S(1)} %copy-done.2, ...), custom_call_target="tpu_custom_call" | custom-call | tf_op jit(solution)/shard_map/input_backward/pallas_call | solution.py:485
  35.0 0.1 collective-permute-start.4
  35.1 2.0 %collective-permute-done.7 = bf16[560,128]{1,0:T(8,128)(2,1)S(1)} collective-permute-done((bf16[560,128]{1,0:T(8,128)(2,1)S(1)}, bf16[560,128]{1,0:T(8,128)(2,1)S(1)}, u32[]{:S(2)}, u32[]{:S(2)}) %collective-permute-start.7) | collective-permute-done | bytes 143392 | tf_op jit(solution)/shard_map/ppermute | solution.py:469
  37.1 0.1 collective-permute-start.8
  37.2 0.0 collective-permute-done.4
  37.2 0.1 broadcast_select_fusion
  37.3 6.0 %collective-permute-done.8 = bf16[560,128]{1,0:T(8,128)(2,1)S(1)} collective-permute-done((bf16[560,128]{1,0:T(8,128)(2,1)S(1)}, bf16[560,128]{1,0:T(8,128)(2,1)S(1)}, u32[]{:S(2)}, u32[]{:S(2)}) %collective-permute-start.8) | collective-permute-done | bytes 143392 | tf_op jit(solution)/shard_map/ppermute | solution.py:469
  43.3 2.4 %collective-permute-start.9 = (bf16[560,128]{1,0:T(8,128)(2,1)S(1)}, bf16[560,128]{1,0:T(8,128)(2,1)S(1)}, u32[]{:S(2)}, u32[]{:S(2)}) collective-permute-start(bf16[560,128]{1,0:T(8,128)(2,1)S(1)} %add_convert_fusion.1), channel_id=1, source_target_pairs={{0,8},{1,3},{2,10},{3,1},{4,12},{5,7},{6,14},{7,5},{8,0},{9,11},{1... | collective-permute-start | bytes 430088 | tf_op jit(solution)/shard_map/ppermute | solution.py:469
  45.7 0.1 fusion
  45.9 1.8 %collective-permute-start.5 = (bf16[180,4,128]{2,1,0:T(4,128)(2,1)S(1)}, bf16[180,4,128]{2,1,0:T(4,128)(2,1)S(1)}, u32[]{:S(2)}, u32[]{:S(2)}) collective-permute-start(bf16[180,4,128]{2,1,0:T(4,128)(2,1)S(1)} %get-tuple-element.70), channel_id=1, source_target_pairs={{0,2},{2,4},{4,6},{6,8},{8,10},{10,12},{12,14},{14,0},{1,3},{3,5},... | collective-permute-start | bytes 552968 | tf_op jit(solution)/shard_map/ppermute | solution.py:449
  47.7 3.2 %collective-permute-done.9 = bf16[560,128]{1,0:T(8,128)(2,1)S(1)} collective-permute-done((bf16[560,128]{1,0:T(8,128)(2,1)S(1)}, bf16[560,128]{1,0:T(8,128)(2,1)S(1)}, u32[]{:S(2)}, u32[]{:S(2)}) %collective-permute-start.9) | collective-permute-done | bytes 143392 | tf_op jit(solution)/shard_map/ppermute | solution.py:469
  51.0 0.1 collective-permute-start.10
  51.0 4.8 %collective-permute-done.5 = bf16[180,4,128]{2,1,0:T(4,128)(2,1)S(1)} collective-permute-done((bf16[180,4,128]{2,1,0:T(4,128)(2,1)S(1)}, bf16[180,4,128]{2,1,0:T(4,128)(2,1)S(1)}, u32[]{:S(2)}, u32[]{:S(2)}) %collective-permute-start.5) | collective-permute-done | bytes 184352 | tf_op jit(solution)/shard_map/ppermute | solution.py:449
  55.9 0.9 %maximum_bitcast_fusion = bf16[8,128,180]{1,0,2:T(8,128)(2,1)} fusion(bf16[180,4,128]{2,1,0:T(4,128)(2,1)S(1)} %get-tuple-element.71, bf16[180,4,128]{2,1,0:T(4,128)(2,1)S(1)} %collective-permute-done.5), kind=kLoop, calls=%fused_computation | loop fusion | flops 737280 | bytes 737280 | tf_op jit(solution)/shard_map/transpose | solution.py:574
  56.8 0.0 collective-permute-done.10.other_ref
  56.8 1.9 %finish.1 = (f32[180,540]{1,0:T(8,128)}, f32[1,540]{1,0:T(1,128)S(1)}, f32[180,180]{1,0:T(8,128)}, f32[225,6]{1,0:T(8,128)S(1)}, f32[1,180]{1,0:T(1,128)}, /*index=5*/f32[1,180]{1,0:T(1,128)}) custom-call(bf16[560,128]{1,0:T(8,128)(2,1)S(1)} %add_convert_fusion.mine_ref, bf16[560,128]{1,0:T(8,128)(2,1)S(1)} %collective-permute-done.10.other_ref, ...), custom_call_target="tpu_custom_call" | custom-call | tf_op jit(solution)/shard_map/finish/pallas_call | solution.py:485
  58.7 0.7 %copy.16 = f32[225,6]{0,1:T(8,128)} copy(f32[225,6]{1,0:T(8,128)S(1)} %get-tuple-element.67) | data formatting | bytes 10800
  59.4 0.6 %reduce = f32[540]{0:T(1024)} reduce(f32[1,540]{1,0:T(1,128)S(1)} %get-tuple-element.58, f32[]{:T(128)} %constant.23), dimensions={0}, to_apply=%get-tuple-element.58.reduce_sub_computation | reduce | bytes 4324 | tf_op jit(solution)/shard_map/finish/pallas_call | solution.py:485
  (8 shorter events, 0.1 us)
Async XLA Ops:
  0.6 1.0 %copy-start = (bf16[8,128,180]{1,0,2:T(8,128)(2,1)S(1)}, bf16[8,128,180]{1,0,2:T(8,128)(2,1)}, u32[]{:S(2)}) copy-start(bf16[8,128,180]{1,0,2:T(8,128)(2,1)} %param.9) | copy-start | bytes 1105924
  1.6 1.0 %copy-start.1 = (bf16[8,128,180]{1,0,2:T(8,128)(2,1)S(1)}, bf16[8,128,180]{1,0,2:T(8,128)(2,1)}, u32[]{:S(2)}) copy-start(bf16[8,128,180]{1,0,2:T(8,128)(2,1)} %param.10) | copy-start | bytes 1105924
  2.6 0.7 %copy-start.7 = (s32[8,128]{1,0:T(8,128)S(1)}, s32[8,128]{1,0:T(8,128)}, u32[]{:S(2)}) copy-start(s32[8,128]{1,0:T(8,128)} %region_ref.3) | copy-start | bytes 12292
  3.3 11.5 %copy-start.11 = (f32[540]{0:T(1024)S(1)}, f32[540]{0:T(1024)}, u32[]{:S(2)}) copy-start(f32[540]{0:T(1024)} %param.15) | copy-start | bytes 6484
  3.3 12.9 %copy-start.3 = (bf16[180,540]{1,0:T(8,128)(2,1)S(1)}, bf16[180,540]{1,0:T(8,128)(2,1)}, u32[]{:S(2)}) copy-start(bf16[180,540]{1,0:T(8,128)(2,1)} %weight_ref.3) | copy-start | bytes 583204
  3.3 12.9 %copy-start.4 = (bf16[180,180]{1,0:T(8,128)(2,1)S(1)}, bf16[180,180]{1,0:T(8,128)(2,1)}, u32[]{:S(2)}) copy-start(bf16[180,180]{1,0:T(8,128)(2,1)} %refs_14_.1) | copy-start | bytes 194404
  3.6 11.2 %copy-start.10 = (f32[225,6]{0,1:T(8,128)S(1)}, f32[225,6]{0,1:T(8,128)}, u32[]{:S(2)}) copy-start(f32[225,6]{0,1:T(8,128)} %param.17) | copy-start | bytes 16204
  3.6 11.2 %collective-permute-start = (bf16[184,4,128]{2,1,0:T(4,128)(2,1)S(1)}, bf16[184,4,128]{2,1,0:T(4,128)(2,1)S(1)}, u32[]{:S(2)}, u32[]{:S(2)}) collective-permute-start(bf16[184,4,128]{2,1,0:T(4,128)(2,1)S(1)} %get-tuple-element.35), channel_id=1, source_target_pairs={{0,14},{2,0},{4,2},{6,4},{8,6},{10,8},{12,10},{14,12},{1,15},{3,1}... | collective-permute-start | bytes 565256 | tf_op jit(solution)/shard_map/ppermute | solution.py:449
  9.7 11.8 %collective-permute-start.2 = (bf16[184,8,128]{2,1,0:T(8,128)(2,1)S(1)}, bf16[184,8,128]{2,1,0:T(8,128)(2,1)S(1)}, u32[]{:S(2)}, u32[]{:S(2)}) collective-permute-start(bf16[184,8,128]{2,1,0:T(8,128)(2,1)S(1)} %get-tuple-element.48), channel_id=1, source_target_pairs={{0,1},{1,0},{2,3},{3,2},{4,5},{5,4},{6,7},{7,6},{8,9},{9,8},{10,11... | collective-permute-start | bytes 1130504 | tf_op jit(solution)/shard_map/ppermute | solution.py:449
  9.7 11.8 %collective-permute-start.1 = (bf16[184,4,128]{2,1,0:T(4,128)(2,1)S(1)}, bf16[184,4,128]{2,1,0:T(4,128)(2,1)S(1)}, u32[]{:S(2)}, u32[]{:S(2)}) collective-permute-start(bf16[184,4,128]{2,1,0:T(4,128)(2,1)S(1)} %get-tuple-element.47), channel_id=1, source_target_pairs={{0,14},{2,0},{4,2},{6,4},{8,6},{10,8},{12,10},{14,12},{1,15},{3,1}... | collective-permute-start | bytes 565256 | tf_op jit(solution)/shard_map/ppermute | solution.py:449
  14.8 6.7 %collective-permute-start.3 = (bf16[184,4,128]{2,1,0:T(4,128)(2,1)S(1)}, bf16[184,4,128]{2,1,0:T(4,128)(2,1)S(1)}, u32[]{:S(2)}, u32[]{:S(2)}) collective-permute-start(bf16[184,4,128]{2,1,0:T(4,128)(2,1)S(1)} %collective-permute-done.refs_0_), channel_id=1, source_target_pairs={{0,1},{1,0},{2,3},{3,2},{4,5},{5,4},{6,7},{7,6},{8,9},{9,8},{10,11... | collective-permute-start | bytes 565256 | tf_op jit(solution)/shard_map/ppermute | solution.py:449
  14.8 0.7 %copy-start.8 = (f32[180]{0:T(256)S(1)}, f32[180]{0:T(256)}, u32[]{:S(2)}) copy-start(f32[180]{0:T(256)} %param.12) | copy-start | bytes 2164
  15.5 0.7 %copy-start.9 = (f32[180]{0:T(256)S(1)}, f32[180]{0:T(256)}, u32[]{:S(2)}) copy-start(f32[180]{0:T(256)} %param.13) | copy-start | bytes 2164
  21.5 7.4 %copy-start.5 = (f32[384,1]{1,0:T(8,128)}, f32[384,1]{1,0:T(8,128)S(1)}, u32[]{:S(2)}) copy-start(f32[384,1]{1,0:T(8,128)S(1)} %get-tuple-element.45.refs_2_) | copy-start | bytes 4612
  28.9 2.0 %collective-permute-start.6 = (bf16[1120,128]{1,0:T(8,128)(2,1)}, bf16[1120,128]{1,0:T(8,128)(2,1)}, u32[]{:S(2)}, u32[]{:S(2)}) collective-permute-start(bf16[1120,128]{1,0:T(8,128)(2,1)} %get-tuple-element.56), channel_id=1, source_target_pairs={{0,1},{1,0},{2,3},{3,2},{4,5},{5,4},{6,7},{7,6},{8,9},{9,8},{10,11... | collective-permute-start | bytes 860168 | tf_op jit(solution)/shard_map/ppermute | solution.py:449
  29.4 3.0 %copy-start.6 = (f32[384,1]{1,0:T(8,128)S(1)}, f32[384,1]{1,0:T(8,128)}, u32[]{:S(2)}) copy-start(f32[384,1]{1,0:T(8,128)} %copy-done.5) | copy-start | bytes 4612
  31.9 5.2 %collective-permute-start.7 = (bf16[560,128]{1,0:T(8,128)(2,1)S(1)}, bf16[560,128]{1,0:T(8,128)(2,1)S(1)}, u32[]{:S(2)}, u32[]{:S(2)}) collective-permute-start(bf16[560,128]{1,0:T(8,128)(2,1)S(1)} %add_convert_fusion.3), channel_id=1, source_target_pairs={{0,2},{1,5},{2,0},{3,7},{4,6},{5,1},{6,4},{7,3},{8,10},{9,13},{10,... | collective-permute-start | bytes 430088 | tf_op jit(solution)/shard_map/ppermute | solution.py:469
  32.3 1.2 %copy-start.2 = (bf16[3,640,180]{2,1,0:T(8,128)(2,1)S(1)}, bf16[3,640,180]{2,1,0:T(8,128)(2,1)}, u32[]{:S(2)}) copy-start(bf16[3,640,180]{2,1,0:T(8,128)(2,1)} %get-tuple-element.51.refs_4_) | copy-start | bytes 2073604
  35.0 2.2 %collective-permute-start.4 = (bf16[180,8,128]{2,1,0:T(8,128)(2,1)S(1)}, bf16[180,8,128]{2,1,0:T(8,128)(2,1)S(1)}, u32[]{:S(2)}, u32[]{:S(2)}) collective-permute-start(bf16[180,8,128]{2,1,0:T(8,128)(2,1)S(1)} %input_backward.1), channel_id=1, source_target_pairs={{0,1},{1,0},{2,3},{3,2},{4,5},{5,4},{6,7},{7,6},{8,9},{9,8},{10,11... | collective-permute-start | bytes 1105928 | tf_op jit(solution)/shard_map/ppermute | solution.py:449
  37.1 6.1 %collective-permute-start.8 = (bf16[560,128]{1,0:T(8,128)(2,1)S(1)}, bf16[560,128]{1,0:T(8,128)(2,1)S(1)}, u32[]{:S(2)}, u32[]{:S(2)}) collective-permute-start(bf16[560,128]{1,0:T(8,128)(2,1)S(1)} %add_convert_fusion.2), channel_id=1, source_target_pairs={{0,4},{1,9},{2,6},{3,11},{4,0},{5,13},{6,2},{7,15},{8,12},{9,1},{1... | collective-permute-start | bytes 430088 | tf_op jit(solution)/shard_map/ppermute | solution.py:469
  43.3 7.6 %collective-permute-start.9 = (bf16[560,128]{1,0:T(8,128)(2,1)S(1)}, bf16[560,128]{1,0:T(8,128)(2,1)S(1)}, u32[]{:S(2)}, u32[]{:S(2)}) collective-permute-start(bf16[560,128]{1,0:T(8,128)(2,1)S(1)} %add_convert_fusion.1), channel_id=1, source_target_pairs={{0,8},{1,3},{2,10},{3,1},{4,12},{5,7},{6,14},{7,5},{8,0},{9,11},{1... | collective-permute-start | bytes 430088 | tf_op jit(solution)/shard_map/ppermute | solution.py:469
  45.9 10.0 %collective-permute-start.5 = (bf16[180,4,128]{2,1,0:T(4,128)(2,1)S(1)}, bf16[180,4,128]{2,1,0:T(4,128)(2,1)S(1)}, u32[]{:S(2)}, u32[]{:S(2)}) collective-permute-start(bf16[180,4,128]{2,1,0:T(4,128)(2,1)S(1)} %get-tuple-element.70), channel_id=1, source_target_pairs={{0,2},{2,4},{4,6},{6,8},{8,10},{10,12},{12,14},{14,0},{1,3},{3,5},... | collective-permute-start | bytes 552968 | tf_op jit(solution)/shard_map/ppermute | solution.py:449
  51.0 5.8 %collective-permute-start.10 = (bf16[560,128]{1,0:T(8,128)(2,1)S(1)}, bf16[560,128]{1,0:T(8,128)(2,1)S(1)}, u32[]{:S(2)}, u32[]{:S(2)}) collective-permute-start(bf16[560,128]{1,0:T(8,128)(2,1)S(1)} %add_convert_fusion.mine_ref), channel_id=1, source_target_pairs={{0,1},{1,0},{2,3},{3,2},{4,5},{5,4},{6,7},{7,6},{8,9},{9,8},{10,11... | collective-permute-start | bytes 430088 | tf_op jit(solution)/shard_map/ppermute | solution.py:449

commit v3 on v1

--- a/solution.py
+++ b/solution.py
@@ -18,7 +18,7 @@
 TABLE_ROWS = 16
 BUFFER_ROWS = 6 * ROWS + TABLE_ROWS
 
-VMEM_LIMIT = 48 * 1024 * 1024
+VMEM_LIMIT = 32 * 1024 * 1024
 
 
 def nn(left, right):
@@ -114,10 +114,12 @@
     proj_ref,
     proj_slots_ref,
     parts_ref,
-    own_ref,
-    down_ref,
-    over_ref,
-    sums_ref,
+    core_ref,
+    keep_ref,
+    send_ref,
+    framed_ref,
+    turn_s,
+    turn_out_s,
     x_s,
     g_s,
     id_s,
@@ -137,7 +139,6 @@
     attended_s,
     d_qkv_s,
     score_s,
-    out_s,
     pack_s,
 ):
     rows, cols, channels = tokens_ref.shape
@@ -149,7 +150,10 @@
     bf16 = jnp.bfloat16
 
     x_s[:, :, :, LANES:] = jnp.zeros(x_s.shape[:3] + (LANES,), f32)
+    turn_s[...] = below_ref[...].astype(f32)
     ids = region_ref[...].astype(f32).T
+    at_id = slice(2 * channels, 2 * channels + 1)
+    col_part = ids[:, 0:1] - 4.0 * jnp.floor(ids[:, 0:1] * 0.25)
     for r in range(rows):
         if r < rows - SHIFT:
             x_body = tokens_ref[r + SHIFT].astype(f32)
@@ -157,14 +161,15 @@
             side = right_ref[r].astype(f32)
             id_body = ids[:, r + SHIFT : r + SHIFT + 1]
         else:
-            payload = below_ref[r - (rows - SHIFT)].astype(f32)
-            x_body = payload[:, 0:channels]
-            g_body = payload[:, channels : 2 * channels]
-            id_body = payload[:, 2 * channels : 2 * channels + 1]
-            side = corner_ref[r - (rows - SHIFT)].astype(f32)
+            here = r - (rows - SHIFT)
+            body = turn_s[:, here, :].T
+            x_body = body[:, 0:channels]
+            g_body = body[:, channels : 2 * channels]
+            side = corner_ref[here].astype(f32)
+            id_body = col_part + 4.0 * jnp.floor(side[0:1, at_id] * 0.25)
         x_row = jnp.concatenate([x_body[SHIFT:], side[:, 0:channels]], 0)
         g_row = jnp.concatenate([g_body[SHIFT:], side[:, channels : 2 * channels]], 0)
-        id_row = jnp.concatenate([id_body[SHIFT:], side[:, 2 * channels : 2 * channels + 1]], 0)
+        id_row = jnp.concatenate([id_body[SHIFT:], side[:, at_id]], 0)
         x_s[:, r, :, 0:channels] = x_row.reshape(wins, WIN, channels)
         g_s[:, r, :, :] = g_row.reshape(wins, WIN, channels)
         id_s[:, r, :, :] = id_row.reshape(wins, WIN, 1)
@@ -257,7 +262,7 @@
         d_qkv_s[2, at, :] = nn(jnp.concatenate(probs, 1), by_head(da_tok_s[at, :])).astype(bf16)
         return carry
 
-    lax.fori_loop(0, count // LANES, pair_step, 0)
+    lax.fori_loop(0, count // LANES, pair_step, 0, unroll=True)
 
     unit_turned = unit_low_s[...].T[0:ROWS]
     rest = channels - LANES
@@ -291,7 +296,12 @@
     table = table.reshape(HEADS, WIN, 2 * LANES).sum(1)
     pack_s[6 * ROWS : 6 * ROWS + HEADS, :] = table[:, 0:LANES]
     pack_s[6 * ROWS + 8 : 6 * ROWS + 8 + HEADS, :] = table[:, LANES:]
-    sums_ref[...] = pack_s[...].astype(bf16)
+    half = keep_ref.shape[0]
+    low_half = pack_s[0:half, :].astype(bf16)
+    high_half = pack_s[half:, :].astype(bf16)
+    lower = core_ref[0] == 0
+    keep_ref[...] = jnp.where(lower, low_half, high_half)
+    send_ref[...] = jnp.where(lower, high_half, low_half)
 
     d_normed = nt(d_qkv_s[0], parts_ref[0]) + nt(d_qkv_s[1], parts_ref[1]) + nt(d_qkv_s[2], parts_ref[2])
     scaled = d_normed * gain_ref[:, 0:channels]
@@ -299,13 +309,12 @@
     mean_one = jnp.sum(scaled, -1, keepdims=True) * (1.0 / channels)
     mean_two = jnp.sum(scaled * unit, -1, keepdims=True) * (1.0 / channels)
     d_input = inv_s[...] * (scaled - mean_one - unit * mean_two)
-    out_s[...] = g_s[...] + d_input.reshape(wins, rows, WIN, channels)
+    g_s[...] = g_s[...] + d_input.reshape(g_s.shape)
     for r in range(rows):
-        row = out_s[:, r].reshape(cols, channels)
-        moved = jnp.concatenate([row[cols - SHIFT :], row[: cols - SHIFT]], 0).astype(bf16)
-        target, place = (own_ref, r) if r < rows - SHIFT else (down_ref, r - (rows - SHIFT))
-        target[place] = moved
-        over_ref[r] = row[cols - SHIFT :].astype(bf16)
+        row = g_s[:, r].reshape(cols, channels)
+        row = jnp.concatenate([row[cols - SHIFT :], row[: cols - SHIFT]], 0)
+        turn_out_s[:, r, :] = row.T
+    framed_ref[...] = turn_out_s[...].astype(bf16)
 
 
 def finish_kernel(out_scale, mine_ref, other_ref, core_ref, weight_ref, gain_ref, offset_ref, d_weight_ref, d_bias_ref, d_proj_ref, d_table_ref, d_gain_ref, d_offset_ref):
@@ -331,20 +340,22 @@
     offset = offset_ref[...].T
     d_gain = jnp.zeros((channels, 1), f32)
     d_offset = jnp.zeros((channels, 1), f32)
+    biases = []
     for part in range(3):
         across = slice(part * channels, (part + 1) * channels)
         unit = pieces[part][0:channels]
         bias = pieces[part][channels : channels + 1]
         weight = weight_ref[:, across].astype(f32)
         d_weight_ref[:, across] = gain * unit + offset * bias
-        d_bias_ref[:, across] = bias
+        biases.append(bias)
         d_gain += jnp.sum(weight * unit, -1, keepdims=True)
         d_offset += jnp.sum(weight * bias, -1, keepdims=True)
-    d_gain_ref[...] = d_gain.T
-    d_offset_ref[...] = d_offset.T
+    d_bias_ref[...] = jnp.concatenate(biases, 1).reshape(d_bias_ref.shape)
+    d_gain_ref[...] = d_gain.T.reshape(channels)
+    d_offset_ref[...] = d_offset.T.reshape(channels)
     d_proj_ref[...] = pieces[3][0:channels]
-    table = jnp.concatenate([both[6 * ROWS : 6 * ROWS + 8], both[6 * ROWS + 8 :]], 1).T
-    d_table_ref[...] = table[0 : d_table_ref.shape[0], 0:HEADS]
+    table = jnp.concatenate([both[6 * ROWS : 6 * ROWS + 8], both[6 * ROWS + 8 :]], 1)
+    d_table_ref[...] = table[0:HEADS, 0 : d_table_ref.shape[1]]
 
 
 def whole(memory_space=pltpu.VMEM):
@@ -364,26 +375,17 @@
     return lax.ppermute(shard, ("row", "col"), pairs)
 
 
-def sum_over_crop(buffer):
+def exchange_steps():
     rows, cols = lax.axis_size("row"), lax.axis_size("col")
-    half = buffer.shape[0] // cols
-    core = lax.axis_index("col")
-    other = from_behind(buffer, "col", 1)
-    start = core * half
-    mine = lax.dynamic_slice_in_dim(buffer, start, half, 0).astype(jnp.float32) + lax.dynamic_slice_in_dim(
-        other, start, half, 0
-    ).astype(jnp.float32)
-    mine = mine.astype(jnp.bfloat16)
     steps = [1 << bit for bit in range((rows - 1).bit_length())]
     for at in range(len(steps)):
-        pairs = []
-        for r in range(rows):
-            for c in range(cols):
-                step = steps[(at + c) % len(steps)]
-                pairs.append((r * cols + c, (r ^ step) * cols + c))
-        came = lax.ppermute(mine, ("row", "col"), pairs)
-        mine = (mine.astype(jnp.float32) + came.astype(jnp.float32)).astype(jnp.bfloat16)
-    return mine, from_behind(mine, "col", 1)
+        yield [
+            (r * cols + c, (r ^ steps[(at + c) % len(steps)]) * cols + c) for r in range(rows) for c in range(cols)
+        ]
+
+
+def add(left, right):
+    return (left.astype(jnp.float32) + right.astype(jnp.float32)).astype(jnp.bfloat16)
 
 
 def on_device(
@@ -394,19 +396,26 @@
     count = rows * cols
     params = pltpu.CompilerParams(vmem_limit_bytes=VMEM_LIMIT)
 
-    def payload(row_slice, col_slice):
+    x_turned = tokens.transpose(2, 0, 1)
+    g_turned = grad_out.transpose(2, 0, 1)
+    core = lax.axis_index("col").astype(jnp.int32).reshape(1)
+
+    below = jnp.concatenate([x_turned[:, :SHIFT], g_turned[:, :SHIFT]], 0)
+    below, near_tokens, near_grad, near_ids = lax.optimization_barrier((below, tokens, grad_out, regions))
+    below = from_behind(below, "row", -1)
+
+    def border(row_slice):
         return jnp.concatenate(
             [
-                tokens[row_slice, col_slice],
-                grad_out[row_slice, col_slice],
-                regions[row_slice, col_slice, None].astype(bf16),
+                near_tokens[row_slice, :SHIFT],
+                near_grad[row_slice, :SHIFT],
+                near_ids[row_slice, :SHIFT, None].astype(bf16),
             ],
             -1,
         )
 
-    below = from_behind(payload(slice(0, SHIFT), slice(None)), "row", -1)
-    right = from_behind(payload(slice(SHIFT, None), slice(0, SHIFT)), "col", -1)
-    corner = diagonal(payload(slice(0, SHIFT), slice(0, SHIFT)), -1)
+    right = from_behind(border(slice(SHIFT, None)), "col", -1)
+    corner = diagonal(border(slice(0, SHIFT)), -1)
 
     table = jnp.pad(bias_table.T, ((0, 8 - HEADS), (0, 2 * LANES - bias_table.shape[0])))
     wide = HEADS * SLOT
@@ -428,18 +437,19 @@
     gain = jnp.pad(ln_gain, (0, 2 * LANES - channels))[None]
     offset = jnp.pad(ln_offset, (0, 2 * LANES - channels))[None]
     wins = cols // WIN
-    own, down, over, sums = pl.pallas_call(
+    keep, send, framed = pl.pallas_call(
         main_kernel,
         name="window_attention_backward",
         out_shape=(
-            jax.ShapeDtypeStruct((SHIFT, cols, channels), bf16),
-            jax.ShapeDtypeStruct((SHIFT, cols, channels), bf16),
-            jax.ShapeDtypeStruct((rows, SHIFT, channels), bf16),
-            jax.ShapeDtypeStruct((BUFFER_ROWS, LANES), bf16),
+            jax.ShapeDtypeStruct((BUFFER_ROWS // 2, LANES), bf16),
+            jax.ShapeDtypeStruct((BUFFER_ROWS // 2, LANES), bf16),
+            jax.ShapeDtypeStruct((channels, rows, cols), bf16),
         ),
-        in_specs=[whole()] * 14,
-        out_specs=(whole(),) * 4,
+        in_specs=[whole()] * 14 + [whole(pltpu.SMEM)],
+        out_specs=(whole(),) * 3,
         scratch_shapes=[
+            pltpu.VMEM((2 * channels, SHIFT, cols), f32),
+            pltpu.VMEM((channels, rows, cols), f32),
             pltpu.VMEM((wins, rows, WIN, 2 * LANES), f32),
             pltpu.VMEM((wins, rows, WIN, channels), f32),
             pltpu.VMEM((wins, rows, WIN, 1), f32),
@@ -459,45 +469,44 @@
             pltpu.VMEM((wide, count), bf16),
             pltpu.VMEM((3, count, channels), bf16),
             pltpu.VMEM((HEADS, SPAN, LANES), f32),
-            pltpu.VMEM((wins, rows, WIN, channels), f32),
             pltpu.VMEM((BUFFER_ROWS, LANES), f32),
         ],
         compiler_params=params,
     )(
-        tokens, grad_out, regions, below, right, corner, gain, offset, bias, tok, chan, proj_weight, proj_slots, parts
+        near_tokens, near_grad, near_ids, below, right, corner, gain, offset, bias, tok, chan, proj_weight, proj_slots, parts, core
     )
 
-    mine, other = sum_over_crop(sums)
-
-    from_above = from_behind(down, "row", 1)
-    from_left = from_behind(over[: rows - SHIFT], "col", 1)
-    from_corner = diagonal(over[rows - SHIFT :], 1)
-    d_tokens = jnp.concatenate(
-        [
-            jnp.concatenate([from_corner, from_above[:, SHIFT:]], 1),
-            jnp.concatenate([from_left, own[:, SHIFT:]], 1),
-        ],
-        0,
-    )
+    above = from_behind(framed[:, rows - SHIFT :], "row", 1)
+    mine = add(keep, from_behind(send, "col", 1))
+    steps = list(exchange_steps())
+    for at, pairs in enumerate(steps):
+        if at == 1 or len(steps) == 1:
+            above, mine = lax.optimization_barrier((above, mine))
+            framed = jnp.concatenate([above, framed[:, : rows - SHIFT]], 1)
+            beside = from_behind(framed, "col", 1)
+        if at == 2:
+            beside, mine = lax.optimization_barrier((beside, mine))
+        mine = add(mine, lax.ppermute(mine, ("row", "col"), pairs))
+    d_tokens = jnp.where(jnp.arange(cols) < SHIFT, beside, framed).transpose(1, 2, 0)
+    other = from_behind(mine, "col", 1)
 
     total_tokens = count * lax.axis_size("row") * lax.axis_size("col")
-    core = lax.axis_index("col").astype(jnp.int32).reshape(1)
     d_weight, d_bias, d_proj, d_table, d_gain, d_offset = pl.pallas_call(
         functools.partial(finish_kernel, total_tokens ** (-0.5)),
         name="finish",
         out_shape=(
             jax.ShapeDtypeStruct(qkv_weight.shape, f32),
-            jax.ShapeDtypeStruct((1,) + qkv_bias.shape, f32),
+            jax.ShapeDtypeStruct(qkv_bias.shape, f32),
             jax.ShapeDtypeStruct(proj_weight.shape, f32),
-            jax.ShapeDtypeStruct(bias_table.shape, f32),
-            jax.ShapeDtypeStruct((1,) + ln_gain.shape, f32),
-            jax.ShapeDtypeStruct((1,) + ln_offset.shape, f32),
+            jax.ShapeDtypeStruct(bias_table.shape[::-1], f32),
+            jax.ShapeDtypeStruct(ln_gain.shape, f32),
+            jax.ShapeDtypeStruct(ln_offset.shape, f32),
         ),
         in_specs=[whole(), whole(), whole(pltpu.SMEM), whole(), whole(), whole()],
         out_specs=(whole(),) * 6,
         compiler_params=params,
     )(mine, other, core, qkv_weight, ln_gain[None], ln_offset[None])
-    return (d_tokens, d_weight, d_bias[0], d_proj, d_table, d_gain[0], d_offset[0])
+    return (d_tokens, d_weight, d_bias, d_proj, d_table.T, d_gain, d_offset)
 
 
 def solution(mesh):

time: 61.3 us -> 54.5 us (0.89)
  starting transfers between devices: 17.9 us -> 10.1 us
  waiting for transfers between devices: 22.4 us -> 26 us
  local copies, waits for them, and re-layouts: 6.45 us -> 3.86 us
    ppermute x2 -> x1, starting transfers between devices: 7.82 us -> 0.12 us  [diagonal(): return lax.ppermute(shard, ('row', 'col'), pairs)]
    ppermute x6, waiting for transfers between devices: 1.57 us -> 7.26 us  [from_behind(): lax.ppermute(shard, axis, [(i, (i + by) % count) for i in range(count)])]
    unnamed x24 -> x18, local copies, waits for them, and re-layouts: 5.1 us -> 1.73 us
    ppermute x2 -> x1, waiting for transfers between devices: 6.1 us -> 3.33 us  [diagonal(): return lax.ppermute(shard, ('row', 'col'), pairs)]
    transpose x0 -> x1, other arithmetic: none -> 0.99 us  [on_device(): jnp.where(jnp.arange(cols) < SHIFT, beside, framed).transpose(1, 2, 0)]
    slice x7 -> x4, local copies, waits for them, and re-layouts: 0.89 us -> 1.27 us  [the longest x2 1.14 us: on_device(): below = jnp.concatenate([x_turned[:, :SHIFT], g_turned[:, :SHIFT]], 0)]
  transfers between devices with their start and end apart: 11 -> 10, of which waited for: 6 -> 7; matrix products, arithmetic and copies ran while one was open for 3% -> 4% of each run, Pallas kernels for 2% -> 2%
where the time goes in v3:
time: 54.5 us; the launch traced here: 54.3 us
  waiting for transfers between devices  26 us (48%)
  Pallas kernels  11.8 us (22%)
  starting transfers between devices  10.1 us (19%)
  local copies, waits for them, and re-layouts  3.86 us (7%)
  other arithmetic  1.77 us (3%)
  between operations  0.82 us (2%)
    ppermute x3, waiting for transfers between devices, on_device(): mine = add(mine, lax.ppermute(mine, ('row', 'col'), pairs))  15.4 us
    ppermute x6, starting transfers between devices, from_behind(): lax.ppermute(shard, axis, [(i, (i + by) % count) for i in range(count)])  9.51 us
    pallas_call x1, Pallas kernels, on_device(): pl.pallas_call(main_kernel, name='window_attention_backward', out_shape=(...  8.76 us
    ppermute x6, waiting for transfers between devices, from_behind(): lax.ppermute(shard, axis, [(i, (i + by) % count) for i in range(count)])  7.26 us
    ppermute x1, waiting for transfers between devices, diagonal(): return lax.ppermute(shard, ('row', 'col'), pairs)  3.33 us
    pallas_call x1, Pallas kernels, on_device(): pl.pallas_call(functools.partial(finish_kernel, total_tokens ** (-0.5)),...  1.94 us
    unnamed x18, local copies, waits for them, and re-layouts  1.73 us
    slice x2, local copies, waits for them, and re-layouts, on_device(): below = jnp.concatenate([x_turned[:, :SHIFT], g_turned[:, :SHIFT]], 0)  1.14 us
  transfers between devices with their start and end apart: 10, of which 7 were waited for; matrix products, arithmetic and copies ran while one was open for 4% of the time, Pallas kernels for 2%

profile of v3, /device:TPU:0, one launch (start us, length us, event | category | flops | bytes accessed | tf_op | source)
XLA Modules:
  0.0 54.3 jit_solution(4413751412736445411)
XLA Ops:
  0.6 0.0 copy-start.6
  0.6 1.1 %slice.42 = bf16[180,4,128]{2,1,0:T(4,128)(2,1)S(1)} slice(bf16[180,8,128]{2,1,0:T(8,128)(2,1)} %bitcast.19), slice={[0:180], [0:4], [0:128]} | slice | bytes 368640 | tf_op jit(solution)/shard_map/slice | solution.py:403
  1.7 0.0 copy-done.6
  1.7 0.1 slice.43
  1.8 0.0 copy-start.5
  1.8 0.2 pad_maximum_fusion
  2.1 6.0 %collective-permute-start = (bf16[360,4,128]{2,1,0:T(4,128)(2,1)S(1)}, bf16[360,4,128]{2,1,0:T(4,128)(2,1)S(1)}, u32[]{:S(2)}, u32[]{:S(2)}) collective-permute-start(bf16[360,4,128]{2,1,0:T(4,128)(2,1)S(1)} %pad_maximum_fusion), channel_id=1, source_target_pairs={{0,14},{2,0},{4,2},{6,4},{8,6},{10,8},{12,10},{14,12},{1,15},{3,1}... | collective-permute-start | bytes 1105928 | tf_op jit(solution)/shard_map/ppermute | solution.py:367
  8.1 0.0 copy-done.5
  8.1 0.3 copy.22.tokens_ref
  8.4 0.0 copy-start.2
  8.4 0.0 copy-start
  8.4 0.3 copy.23.grad_ref
  8.7 0.4 copy-done.2
  9.1 0.0 copy-start.1
  9.1 0.1 copy.21
  9.3 0.1 pad_maximum_fusion.3
  9.3 0.1 collective-permute-start.2
  9.5 0.1 copy.18
  9.6 0.0 copy-start.8
  9.6 0.1 pad_maximum_fusion.2
  9.7 0.0 copy-start.7
  9.7 0.7 %collective-permute-start.1 = (bf16[4,4,361]{2,1,0:T(4,128)(2,1)S(1)}, bf16[4,4,361]{2,1,0:T(4,128)(2,1)S(1)}, u32[]{:S(2)}, u32[]{:S(2)}) collective-permute-start(bf16[4,4,361]{2,1,0:T(4,128)(2,1)S(1)} %pad_maximum_fusion.2), channel_id=1, source_target_pairs={{0,1},{1,0},{2,3},{3,2},{4,5},{5,4},{6,7},{7,6},{8,9},{9,8},{10,11... | collective-permute-start | bytes 34664 | tf_op jit(solution)/shard_map/ppermute | solution.py:367
  10.4 0.0 copy-done.8
  10.4 0.0 copy-done.7
  10.4 0.0 copy-start.3
  10.4 0.7 %copy-done.3 = f32[180]{0:T(256)S(1)} copy-done((f32[180]{0:T(256)S(1)}, f32[180]{0:T(256)}, u32[]{:S(2)}) %copy-start.3) | copy-done | bytes 744
  11.1 0.0 copy-start.4
  11.1 0.7 %copy-done.4 = f32[180]{0:T(256)S(1)} copy-done((f32[180]{0:T(256)S(1)}, f32[180]{0:T(256)}, u32[]{:S(2)}) %copy-start.4) | copy-done | bytes 744
  11.8 0.0 copy-done
  11.8 0.0 copy-done.1
  11.8 1.1 %prepare.1 = (f32[6,64,128]{2,1,0:T(8,128)S(1)}, bf16[3,256,192]{2,1,0:T(8,128)(2,1)S(1)}, bf16[3,192,256]{2,1,0:T(8,128)(2,1)S(1)}, bf16[192,180]{1,0:T(8,128)(2,1)S(1)}, bf16[3,180,180]{2,1,0:T(8,128)(2,1)S(1)}) custom-call(bf16[180,540]{1,0:T(8,128)(2,1)S(1)} %copy-done, f32[1,540]{1,0:T(1,128)S(1)} %broadcast_in_dim.24.offsets_ref, ...), custom_call_target="tpu_custom_call" | custom-call | tf_op jit(solution)/shard_map/prepare/pallas_call | solution.py:422
  12.9 3.3 %collective-permute-done.2.corner_ref = bf16[4,4,361]{2,1,0:T(4,128)(2,1)S(1)} collective-permute-done((bf16[4,4,361]{2,1,0:T(4,128)(2,1)S(1)}, bf16[4,4,361]{2,1,0:T(4,128)(2,1)S(1)}, u32[]{:S(2)}, u32[]{:S(2)}) %collective-permute-start.2) | collective-permute-done | bytes 11584 | tf_op jit(solution)/shard_map/ppermute | solution.py:375
  16.2 0.0 collective-permute-done.1.right_ref
  16.2 0.0 collective-permute-done.below_ref
  16.2 8.8 %window_attention_backward.1 = (bf16[560,128]{1,0:T(8,128)(2,1)S(1)}, bf16[560,128]{1,0:T(8,128)(2,1)S(1)}, bf16[180,8,128]{2,1,0:T(8,128)(2,1)S(1)}) custom-call(bf16[8,128,180]{2,1,0:T(8,128)(2,1)S(1)} %copy.22.tokens_ref, bf16[8,128,180]{2,1,0:T(8,128)(2,1)S(1)} %copy.23.grad_ref, s32[8,128]{1,0:T(8,128)S(1)} %copy-done.2, ...), custom_call_target="tpu_custom_call" | custom-call | tf_op jit(solution)/shard_map/window_attention_backward/pallas_call | solution.py:440
  25.0 0.1 collective-permute-start.4
  25.1 1.4 %collective-permute-done.4 = bf16[560,128]{1,0:T(8,128)(2,1)S(1)} collective-permute-done((bf16[560,128]{1,0:T(8,128)(2,1)S(1)}, bf16[560,128]{1,0:T(8,128)(2,1)S(1)}, u32[]{:S(2)}, u32[]{:S(2)}) %collective-permute-start.4) | collective-permute-done | bytes 143392 | tf_op jit(solution)/shard_map/ppermute | solution.py:367
  26.4 0.3 collective-permute-start.5
  26.7 0.1 fusion.2
  26.8 1.9 %collective-permute-start.3 = (bf16[180,4,128]{2,1,0:T(4,128)(2,1)S(1)}, bf16[180,4,128]{2,1,0:T(4,128)(2,1)S(1)}, u32[]{:S(2)}, u32[]{:S(2)}) collective-permute-start(bf16[180,4,128]{2,1,0:T(4,128)(2,1)S(1)} %get-tuple-element.55), channel_id=1, source_target_pairs={{0,2},{2,4},{4,6},{6,8},{8,10},{10,12},{12,14},{14,0},{1,3},{3,5},... | collective-permute-start | bytes 552968 | tf_op jit(solution)/shard_map/ppermute | solution.py:367
  28.7 2.9 %collective-permute-done.5 = bf16[560,128]{1,0:T(8,128)(2,1)S(1)} collective-permute-done((bf16[560,128]{1,0:T(8,128)(2,1)S(1)}, bf16[560,128]{1,0:T(8,128)(2,1)S(1)}, u32[]{:S(2)}, u32[]{:S(2)}) %collective-permute-start.5) | collective-permute-done | bytes 143392 | tf_op jit(solution)/shard_map/ppermute | solution.py:489
  31.7 5.5 %collective-permute-done.3 = bf16[180,4,128]{2,1,0:T(4,128)(2,1)S(1)} collective-permute-done((bf16[180,4,128]{2,1,0:T(4,128)(2,1)S(1)}, bf16[180,4,128]{2,1,0:T(4,128)(2,1)S(1)}, u32[]{:S(2)}, u32[]{:S(2)}) %collective-permute-start.3) | collective-permute-done | bytes 184352 | tf_op jit(solution)/shard_map/ppermute | solution.py:367
  37.2 0.0 collective-permute-start.7
  37.2 0.2 pad_maximum_fusion.1
  37.4 0.7 %collective-permute-start.6 = (bf16[180,8,128]{2,1,0:T(8,128)(2,1)S(1)}, bf16[180,8,128]{2,1,0:T(8,128)(2,1)S(1)}, u32[]{:S(2)}, u32[]{:S(2)}) collective-permute-start(bf16[180,8,128]{2,1,0:T(8,128)(2,1)S(1)} %pad_maximum_fusion.1), channel_id=1, source_target_pairs={{0,1},{1,0},{2,3},{3,2},{4,5},{5,4},{6,7},{7,6},{8,9},{9,8},{10,11... | collective-permute-start | bytes 1105928 | tf_op jit(solution)/shard_map/ppermute | solution.py:367
  38.1 5.7 %collective-permute-done.7 = bf16[560,128]{1,0:T(8,128)(2,1)S(1)} collective-permute-done((bf16[560,128]{1,0:T(8,128)(2,1)S(1)}, bf16[560,128]{1,0:T(8,128)(2,1)S(1)}, u32[]{:S(2)}, u32[]{:S(2)}) %collective-permute-start.7) | collective-permute-done | bytes 143392 | tf_op jit(solution)/shard_map/ppermute | solution.py:489
  43.9 0.0 collective-permute-done.6
  43.9 0.2 collective-permute-start.8
  44.1 6.8 %collective-permute-done.8 = bf16[560,128]{1,0:T(8,128)(2,1)S(1)} collective-permute-done((bf16[560,128]{1,0:T(8,128)(2,1)S(1)}, bf16[560,128]{1,0:T(8,128)(2,1)S(1)}, u32[]{:S(2)}, u32[]{:S(2)}) %collective-permute-start.8) | collective-permute-done | bytes 143392 | tf_op jit(solution)/shard_map/ppermute | solution.py:489
  50.9 0.1 collective-permute-start.9
  51.0 1.0 %select_bitcast_fusion = bf16[8,128,180]{1,0,2:T(8,128)(2,1)} fusion(bf16[180,8,128]{2,1,0:T(8,128)(2,1)S(1)} %collective-permute-done.6, pred[128]{0:T(512)(128)(4,1)S(1)} %iota_compare_fusion, bf16[180,4,128]{2,1,0:T(4,128)(2,1)S(1)} %get-tuple-element.56, bf16[180,4,128]{2,1,0:T(4,128)(2,1)S(1)} %collective-permute-done.3), kind=kLoop, calls=%fused_computation.2 | loop fusion | flops 921600 | bytes 1106048 | tf_op jit(solution)/shard_map/transpose | solution.py:490
  52.0 0.4 collective-permute-done.9.other_ref
  52.4 1.9 %finish.1 = (f32[180,540]{1,0:T(8,128)}, f32[540]{0:T(1024)}, f32[180,180]{1,0:T(8,128)}, f32[6,225]{1,0:T(8,128)}, f32[180]{0:T(256)}, /*index=5*/f32[180]{0:T(256)}) custom-call(bf16[560,128]{1,0:T(8,128)(2,1)S(1)} %add_convert_fusion.mine_ref, bf16[560,128]{1,0:T(8,128)(2,1)S(1)} %collective-permute-done.9.other_ref, s32[1]{0:T(128)} %bitcast.7.core_ref, ...), custom_call_target="tpu_custom_call" | custom-call | tf_op jit(solution)/shard_map/finish/pallas_call | solution.py:494
  (12 shorter events, 0.2 us)
Async XLA Ops:
  0.6 1.1 %copy-start.6 = (bf16[8,128,180]{1,0,2:T(8,128)(2,1)S(1)}, bf16[8,128,180]{1,0,2:T(8,128)(2,1)}, u32[]{:S(2)}) copy-start(bf16[8,128,180]{1,0,2:T(8,128)(2,1)} %param.10) | copy-start | bytes 1105924
  1.8 6.3 %copy-start.5 = (bf16[8,128,180]{1,0,2:T(8,128)(2,1)S(1)}, bf16[8,128,180]{1,0,2:T(8,128)(2,1)}, u32[]{:S(2)}) copy-start(bf16[8,128,180]{1,0,2:T(8,128)(2,1)} %param.9) | copy-start | bytes 1105924
  2.1 14.1 %collective-permute-start = (bf16[360,4,128]{2,1,0:T(4,128)(2,1)S(1)}, bf16[360,4,128]{2,1,0:T(4,128)(2,1)S(1)}, u32[]{:S(2)}, u32[]{:S(2)}) collective-permute-start(bf16[360,4,128]{2,1,0:T(4,128)(2,1)S(1)} %pad_maximum_fusion), channel_id=1, source_target_pairs={{0,14},{2,0},{4,2},{6,4},{8,6},{10,8},{12,10},{14,12},{1,15},{3,1}... | collective-permute-start | bytes 1105928 | tf_op jit(solution)/shard_map/ppermute | solution.py:367
  8.4 0.7 %copy-start.2 = (s32[8,128]{1,0:T(8,128)S(1)}, s32[8,128]{1,0:T(8,128)}, u32[]{:S(2)}) copy-start(s32[8,128]{1,0:T(8,128)} %region_ref) | copy-start | bytes 12292
  8.4 3.4 %copy-start = (bf16[180,540]{1,0:T(8,128)(2,1)S(1)}, bf16[180,540]{1,0:T(8,128)(2,1)}, u32[]{:S(2)}) copy-start(bf16[180,540]{1,0:T(8,128)(2,1)} %weight_ref.3) | copy-start | bytes 583204
  9.1 2.7 %copy-start.1 = (bf16[180,180]{1,0:T(8,128)(2,1)S(1)}, bf16[180,180]{1,0:T(8,128)(2,1)}, u32[]{:S(2)}) copy-start(bf16[180,180]{1,0:T(8,128)(2,1)} %proj_ref.3) | copy-start | bytes 194404
  9.3 6.9 %collective-permute-start.2 = (bf16[4,4,361]{2,1,0:T(4,128)(2,1)S(1)}, bf16[4,4,361]{2,1,0:T(4,128)(2,1)S(1)}, u32[]{:S(2)}, u32[]{:S(2)}) collective-permute-start(bf16[4,4,361]{2,1,0:T(4,128)(2,1)S(1)} %pad_maximum_fusion.3), channel_id=1, source_target_pairs={{0,15},{1,14},{2,1},{3,0},{4,3},{5,2},{6,5},{7,4},{8,7},{9,6},{10,... | collective-permute-start | bytes 34664 | tf_op jit(solution)/shard_map/ppermute | solution.py:375
  9.6 0.8 %copy-start.8 = (f32[540]{0:T(1024)S(1)}, f32[540]{0:T(1024)}, u32[]{:S(2)}) copy-start(f32[540]{0:T(1024)} %param.15) | copy-start | bytes 6484
  9.7 0.8 %copy-start.7 = (f32[225,6]{0,1:T(8,128)S(1)}, f32[225,6]{0,1:T(8,128)}, u32[]{:S(2)}) copy-start(f32[225,6]{0,1:T(8,128)} %param.17) | copy-start | bytes 16204
  9.7 6.5 %collective-permute-start.1 = (bf16[4,4,361]{2,1,0:T(4,128)(2,1)S(1)}, bf16[4,4,361]{2,1,0:T(4,128)(2,1)S(1)}, u32[]{:S(2)}, u32[]{:S(2)}) collective-permute-start(bf16[4,4,361]{2,1,0:T(4,128)(2,1)S(1)} %pad_maximum_fusion.2), channel_id=1, source_target_pairs={{0,1},{1,0},{2,3},{3,2},{4,5},{5,4},{6,7},{7,6},{8,9},{9,8},{10,11... | collective-permute-start | bytes 34664 | tf_op jit(solution)/shard_map/ppermute | solution.py:367
  10.4 0.7 %copy-start.3 = (f32[180]{0:T(256)S(1)}, f32[180]{0:T(256)}, u32[]{:S(2)}) copy-start(f32[180]{0:T(256)} %param.12) | copy-start | bytes 2164
  11.1 0.7 %copy-start.4 = (f32[180]{0:T(256)S(1)}, f32[180]{0:T(256)}, u32[]{:S(2)}) copy-start(f32[180]{0:T(256)} %param.13) | copy-start | bytes 2164
  25.0 1.4 %collective-permute-start.4 = (bf16[560,128]{1,0:T(8,128)(2,1)S(1)}, bf16[560,128]{1,0:T(8,128)(2,1)S(1)}, u32[]{:S(2)}, u32[]{:S(2)}) collective-permute-start(bf16[560,128]{1,0:T(8,128)(2,1)S(1)} %get-tuple-element.40), channel_id=1, source_target_pairs={{0,1},{1,0},{2,3},{3,2},{4,5},{5,4},{6,7},{7,6},{8,9},{9,8},{10,11... | collective-permute-start | bytes 430088 | tf_op jit(solution)/shard_map/ppermute | solution.py:367
  26.4 5.2 %collective-permute-start.5 = (bf16[560,128]{1,0:T(8,128)(2,1)S(1)}, bf16[560,128]{1,0:T(8,128)(2,1)S(1)}, u32[]{:S(2)}, u32[]{:S(2)}) collective-permute-start(bf16[560,128]{1,0:T(8,128)(2,1)S(1)} %add_convert_fusion.3), channel_id=1, source_target_pairs={{0,2},{1,5},{2,0},{3,7},{4,6},{5,1},{6,4},{7,3},{8,10},{9,13},{10,... | collective-permute-start | bytes 430088 | tf_op jit(solution)/shard_map/ppermute | solution.py:489
  26.8 10.4 %collective-permute-start.3 = (bf16[180,4,128]{2,1,0:T(4,128)(2,1)S(1)}, bf16[180,4,128]{2,1,0:T(4,128)(2,1)S(1)}, u32[]{:S(2)}, u32[]{:S(2)}) collective-permute-start(bf16[180,4,128]{2,1,0:T(4,128)(2,1)S(1)} %get-tuple-element.55), channel_id=1, source_target_pairs={{0,2},{2,4},{4,6},{6,8},{8,10},{10,12},{12,14},{14,0},{1,3},{3,5},... | collective-permute-start | bytes 552968 | tf_op jit(solution)/shard_map/ppermute | solution.py:367
  37.2 6.6 %collective-permute-start.7 = (bf16[560,128]{1,0:T(8,128)(2,1)S(1)}, bf16[560,128]{1,0:T(8,128)(2,1)S(1)}, u32[]{:S(2)}, u32[]{:S(2)}) collective-permute-start(bf16[560,128]{1,0:T(8,128)(2,1)S(1)} %add_convert_fusion.2), channel_id=1, source_target_pairs={{0,4},{1,9},{2,6},{3,11},{4,0},{5,13},{6,2},{7,15},{8,12},{9,1},{1... | collective-permute-start | bytes 430088 | tf_op jit(solution)/shard_map/ppermute | solution.py:489
  37.4 6.5 %collective-permute-start.6 = (bf16[180,8,128]{2,1,0:T(8,128)(2,1)S(1)}, bf16[180,8,128]{2,1,0:T(8,128)(2,1)S(1)}, u32[]{:S(2)}, u32[]{:S(2)}) collective-permute-start(bf16[180,8,128]{2,1,0:T(8,128)(2,1)S(1)} %pad_maximum_fusion.1), channel_id=1, source_target_pairs={{0,1},{1,0},{2,3},{3,2},{4,5},{5,4},{6,7},{7,6},{8,9},{9,8},{10,11... | collective-permute-start | bytes 1105928 | tf_op jit(solution)/shard_map/ppermute | solution.py:367
  43.9 7.0 %collective-permute-start.8 = (bf16[560,128]{1,0:T(8,128)(2,1)S(1)}, bf16[560,128]{1,0:T(8,128)(2,1)S(1)}, u32[]{:S(2)}, u32[]{:S(2)}) collective-permute-start(bf16[560,128]{1,0:T(8,128)(2,1)S(1)} %add_convert_fusion.1), channel_id=1, source_target_pairs={{0,8},{1,3},{2,10},{3,1},{4,12},{5,7},{6,14},{7,5},{8,0},{9,11},{1... | collective-permute-start | bytes 430088 | tf_op jit(solution)/shard_map/ppermute | solution.py:489
  50.9 1.4 %collective-permute-start.9 = (bf16[560,128]{1,0:T(8,128)(2,1)S(1)}, bf16[560,128]{1,0:T(8,128)(2,1)S(1)}, u32[]{:S(2)}, u32[]{:S(2)}) collective-permute-start(bf16[560,128]{1,0:T(8,128)(2,1)S(1)} %add_convert_fusion.mine_ref), channel_id=1, source_target_pairs={{0,1},{1,0},{2,3},{3,2},{4,5},{5,4},{6,7},{7,6},{8,9},{9,8},{10,11... | collective-permute-start | bytes 430088 | tf_op jit(solution)/shard_map/ppermute | solution.py:367

commit v4 on v3

--- a/solution.py
+++ b/solution.py
@@ -103,7 +103,8 @@
     tokens_ref,
     grad_ref,
     region_ref,
-    below_ref,
+    x_below_ref,
+    g_below_ref,
     right_ref,
     corner_ref,
     gain_ref,
@@ -113,18 +114,16 @@
     chan_ref,
     proj_ref,
     proj_slots_ref,
-    parts_ref,
     core_ref,
     keep_ref,
     send_ref,
-    framed_ref,
-    turn_s,
-    turn_out_s,
-    x_s,
-    g_s,
-    id_s,
+    d_qkv_s,
     unit_s,
     inv_s,
+    g_s,
+    turn_s,
+    x_s,
+    id_s,
     unit_low_s,
     normed_s,
     grad_s,
@@ -137,7 +136,6 @@
     v_chan_s,
     da_chan_s,
     attended_s,
-    d_qkv_s,
     score_s,
     pack_s,
 ):
@@ -150,7 +148,8 @@
     bf16 = jnp.bfloat16
 
     x_s[:, :, :, LANES:] = jnp.zeros(x_s.shape[:3] + (LANES,), f32)
-    turn_s[...] = below_ref[...].astype(f32)
+    turn_s[0:channels] = x_below_ref[...].astype(f32)
+    turn_s[channels:] = g_below_ref[...].astype(f32)
     ids = region_ref[...].astype(f32).T
     at_id = slice(2 * channels, 2 * channels + 1)
     col_part = ids[:, 0:1] - 4.0 * jnp.floor(ids[:, 0:1] * 0.25)
@@ -303,18 +302,23 @@
     keep_ref[...] = jnp.where(lower, low_half, high_half)
     send_ref[...] = jnp.where(lower, high_half, low_half)
 
-    d_normed = nt(d_qkv_s[0], parts_ref[0]) + nt(d_qkv_s[1], parts_ref[1]) + nt(d_qkv_s[2], parts_ref[2])
+
+def input_kernel(d_qkv_ref, unit_ref, inv_ref, g_ref, gain_ref, parts_ref, framed_ref, turn_s):
+    wins, rows, _, channels = g_ref.shape
+    cols = wins * WIN
+    f32 = jnp.float32
+    d_normed = sum(nt(d_qkv_ref[part], parts_ref[part]) for part in range(3))
     scaled = d_normed * gain_ref[:, 0:channels]
-    unit = unit_s[:, 0:channels]
+    unit = unit_ref[:, 0:channels]
     mean_one = jnp.sum(scaled, -1, keepdims=True) * (1.0 / channels)
     mean_two = jnp.sum(scaled * unit, -1, keepdims=True) * (1.0 / channels)
-    d_input = inv_s[...] * (scaled - mean_one - unit * mean_two)
-    g_s[...] = g_s[...] + d_input.reshape(g_s.shape)
+    d_input = inv_ref[...] * (scaled - mean_one - unit * mean_two)
+    done = g_ref[...] + d_input.reshape(g_ref.shape)
     for r in range(rows):
-        row = g_s[:, r].reshape(cols, channels)
+        row = done[:, r].reshape(cols, channels)
         row = jnp.concatenate([row[cols - SHIFT :], row[: cols - SHIFT]], 0)
-        turn_out_s[:, r, :] = row.T
-    framed_ref[...] = turn_out_s[...].astype(bf16)
+        turn_s[:, r, :] = row.T
+    framed_ref[...] = turn_s[...].astype(framed_ref.dtype)
 
 
 def finish_kernel(out_scale, mine_ref, other_ref, core_ref, weight_ref, gain_ref, offset_ref, d_weight_ref, d_bias_ref, d_proj_ref, d_table_ref, d_gain_ref, d_offset_ref):
@@ -400,9 +404,9 @@
     g_turned = grad_out.transpose(2, 0, 1)
     core = lax.axis_index("col").astype(jnp.int32).reshape(1)
 
-    below = jnp.concatenate([x_turned[:, :SHIFT], g_turned[:, :SHIFT]], 0)
-    below, near_tokens, near_grad, near_ids = lax.optimization_barrier((below, tokens, grad_out, regions))
-    below = from_behind(below, "row", -1)
+    x_below = from_behind(x_turned[:, :SHIFT], "row", -1)
+    g_below = from_behind(g_turned[:, :SHIFT], "row", -1)
+    near_tokens, near_grad, near_ids = tokens, grad_out, regions
 
     def border(row_slice):
         return jnp.concatenate(
@@ -437,24 +441,23 @@
     gain = jnp.pad(ln_gain, (0, 2 * LANES - channels))[None]
     offset = jnp.pad(ln_offset, (0, 2 * LANES - channels))[None]
     wins = cols // WIN
-    keep, send, framed = pl.pallas_call(
+    keep, send, *saved = pl.pallas_call(
         main_kernel,
         name="window_attention_backward",
         out_shape=(
             jax.ShapeDtypeStruct((BUFFER_ROWS // 2, LANES), bf16),
             jax.ShapeDtypeStruct((BUFFER_ROWS // 2, LANES), bf16),
-            jax.ShapeDtypeStruct((channels, rows, cols), bf16),
+            jax.ShapeDtypeStruct((3, count, channels), bf16),
+            jax.ShapeDtypeStruct((count, 2 * LANES), f32),
+            jax.ShapeDtypeStruct((count, 1), f32),
+            jax.ShapeDtypeStruct((wins, rows, WIN, channels), f32),
         ),
         in_specs=[whole()] * 14 + [whole(pltpu.SMEM)],
-        out_specs=(whole(),) * 3,
+        out_specs=(whole(),) * 6,
         scratch_shapes=[
             pltpu.VMEM((2 * channels, SHIFT, cols), f32),
-            pltpu.VMEM((channels, rows, cols), f32),
             pltpu.VMEM((wins, rows, WIN, 2 * LANES), f32),
-            pltpu.VMEM((wins, rows, WIN, channels), f32),
             pltpu.VMEM((wins, rows, WIN, 1), f32),
-            pltpu.VMEM((count, 2 * LANES), f32),
-            pltpu.VMEM((count, 1), f32),
             pltpu.VMEM((count, 2 * LANES), bf16),
             pltpu.VMEM((count, 2 * LANES), bf16),
             pltpu.VMEM((count, channels), bf16),
@@ -467,27 +470,37 @@
             pltpu.VMEM((wide, count), bf16),
             pltpu.VMEM((wide, count), bf16),
             pltpu.VMEM((wide, count), bf16),
-            pltpu.VMEM((3, count, channels), bf16),
             pltpu.VMEM((HEADS, SPAN, LANES), f32),
             pltpu.VMEM((BUFFER_ROWS, LANES), f32),
         ],
         compiler_params=params,
     )(
-        near_tokens, near_grad, near_ids, below, right, corner, gain, offset, bias, tok, chan, proj_weight, proj_slots, parts, core
+        near_tokens, near_grad, near_ids, x_below, g_below, right, corner, gain, offset, bias, tok, chan, proj_weight, proj_slots, core
     )
 
-    above = from_behind(framed[:, rows - SHIFT :], "row", 1)
     mine = add(keep, from_behind(send, "col", 1))
+    mine, *saved = lax.optimization_barrier((mine, *saved))
+    (framed,) = pl.pallas_call(
+        input_kernel,
+        name="input_backward",
+        out_shape=(jax.ShapeDtypeStruct((channels, rows, cols), bf16),),
+        in_specs=[whole()] * 6,
+        out_specs=(whole(),),
+        scratch_shapes=[pltpu.VMEM((channels, rows, cols), f32)],
+        compiler_params=params,
+        cost_estimate=pl.CostEstimate(flops=10**9, bytes_accessed=0, transcendentals=0),
+    )(*saved, gain, parts)
     steps = list(exchange_steps())
     for at, pairs in enumerate(steps):
-        if at == 1 or len(steps) == 1:
-            above, mine = lax.optimization_barrier((above, mine))
-            framed = jnp.concatenate([above, framed[:, : rows - SHIFT]], 1)
+        if at == min(1, len(steps) - 1):
+            mine, framed = lax.optimization_barrier((mine, framed))
             beside = from_behind(framed, "col", 1)
-        if at == 2:
-            beside, mine = lax.optimization_barrier((beside, mine))
+            framed = jnp.where(jnp.arange(cols) < SHIFT, beside, framed)
+        if at == min(2, len(steps) - 1):
+            mine, framed = lax.optimization_barrier((mine, framed))
+            above = from_behind(framed[:, rows - SHIFT :], "row", 1)
         mine = add(mine, lax.ppermute(mine, ("row", "col"), pairs))
-    d_tokens = jnp.where(jnp.arange(cols) < SHIFT, beside, framed).transpose(1, 2, 0)
+    d_tokens = jnp.concatenate([above, framed[:, : rows - SHIFT]], 1).transpose(1, 2, 0)
     other = from_behind(mine, "col", 1)
 
     total_tokens = count * lax.axis_size("row") * lax.axis_size("col")

time: 54.5 us -> 50.1 us (0.919)
  waiting for transfers between devices: 26 us -> 18.8 us
  starting transfers between devices: 10.1 us -> 13.2 us
    ppermute x3, waiting for transfers between devices: 15.4 us -> 12 us  [on_device(): mine = add(mine, lax.ppermute(mine, ('row', 'col'), pairs))]
    ppermute x6 -> x7, waiting for transfers between devices: 7.26 us -> 5.09 us  [from_behind(): lax.ppermute(shard, axis, [(i, (i + by) % count) for i in range(count)])]
    pallas_call x1, Pallas kernels: 8.76 us -> 6.96 us  [on_device(): pl.pallas_call(main_kernel, name='window_attention_backward', out_shape=(...]
    ppermute x3, starting transfers between devices: 0.49 us -> 2.18 us  [on_device(): mine = add(mine, lax.ppermute(mine, ('row', 'col'), pairs))]
    ppermute x1, waiting for transfers between devices: 3.33 us -> 1.74 us  [diagonal(): return lax.ppermute(shard, ('row', 'col'), pairs)]
    pallas_call x0 -> x1, Pallas kernels: none -> 1.46 us  [on_device(): pl.pallas_call(input_kernel, name='input_backward', out_shape=(jax.ShapeD...]
    ppermute x1, starting transfers between devices: 0.12 us -> 1.48 us  [diagonal(): return lax.ppermute(shard, ('row', 'col'), pairs)]
    slice x2 -> x3, local copies, waits for them, and re-layouts: 1.14 us -> 2.2 us  [the longest x1 1.16 us: on_device(): x_below = from_behind(x_turned[:, :SHIFT], 'row', -1)]
  transfers between devices with their start and end apart: 10 -> 11, of which waited for: 7 -> 6; matrix products, arithmetic and copies ran while one was open for 4% -> 8% of each run, Pallas kernels for 2% -> 5%
where the time goes in v4:
time: 50.1 us; the launch traced here: 49.9 us
  waiting for transfers between devices  18.8 us (38%)
  starting transfers between devices  13.2 us (26%)
  Pallas kernels  11.4 us (23%)
  local copies, waits for them, and re-layouts  4.18 us (8%)
  other arithmetic  1.33 us (3%)
  between operations  0.92 us (2%)
    ppermute x3, waiting for transfers between devices, on_device(): mine = add(mine, lax.ppermute(mine, ('row', 'col'), pairs))  12 us
    ppermute x7, starting transfers between devices, from_behind(): lax.ppermute(shard, axis, [(i, (i + by) % count) for i in range(count)])  9.59 us
    pallas_call x1, Pallas kernels, on_device(): pl.pallas_call(main_kernel, name='window_attention_backward', out_shape=(...  6.96 us
    ppermute x7, waiting for transfers between devices, from_behind(): lax.ppermute(shard, axis, [(i, (i + by) % count) for i in range(count)])  5.09 us
    ppermute x3, starting transfers between devices, on_device(): mine = add(mine, lax.ppermute(mine, ('row', 'col'), pairs))  2.18 us
    pallas_call x1, Pallas kernels, on_device(): pl.pallas_call(functools.partial(finish_kernel, total_tokens ** (-0.5)),...  1.94 us
    ppermute x1, waiting for transfers between devices, diagonal(): return lax.ppermute(shard, ('row', 'col'), pairs)  1.74 us
    unnamed x18, local copies, waits for them, and re-layouts  1.57 us
  transfers between devices with their start and end apart: 11, of which 6 were waited for; matrix products, arithmetic and copies ran while one was open for 8% of the time, Pallas kernels for 5%

profile of v4, /device:TPU:0, one launch (start us, length us, event | category | flops | bytes accessed | tf_op | source)
XLA Modules:
  0.0 49.9 jit_solution(8378514981542403740)
XLA Ops:
  0.6 0.0 copy-start.5
  0.6 0.0 copy-start.2
  0.7 0.0 copy-start.7
  0.7 0.0 copy-start.6
  0.7 0.0 copy-start.3
  0.7 0.0 copy-start.4
  0.7 0.0 copy-start
  0.7 0.0 copy-start.1
  0.7 1.2 %slice.42 = bf16[180,4,128]{2,1,0:T(4,128)(2,1)S(1)} slice(bf16[180,8,128]{2,1,0:T(8,128)(2,1)} %bitcast.20), slice={[0:180], [0:4], [0:128]} | slice | bytes 368640 | tf_op jit(solution)/shard_map/slice | solution.py:407
  1.9 6.0 %collective-permute-start = (bf16[180,4,128]{2,1,0:T(4,128)(2,1)S(1)}, bf16[180,4,128]{2,1,0:T(4,128)(2,1)S(1)}, u32[]{:S(2)}, u32[]{:S(2)}) collective-permute-start(bf16[180,4,128]{2,1,0:T(4,128)(2,1)S(1)} %slice.42), channel_id=1, source_target_pairs={{0,14},{2,0},{4,2},{6,4},{8,6},{10,8},{12,10},{14,12},{1,15},{3,1}... | collective-permute-start | bytes 552968 | tf_op jit(solution)/shard_map/ppermute | solution.py:371
  7.9 1.0 %slice.43 = bf16[180,4,128]{2,1,0:T(4,128)(2,1)S(1)} slice(bf16[180,8,128]{2,1,0:T(8,128)(2,1)} %bitcast.21), slice={[0:180], [0:4], [0:128]} | slice | bytes 368640 | tf_op jit(solution)/shard_map/slice | solution.py:408
  8.9 0.6 %collective-permute-start.1 = (bf16[180,4,128]{2,1,0:T(4,128)(2,1)S(1)}, bf16[180,4,128]{2,1,0:T(4,128)(2,1)S(1)}, u32[]{:S(2)}, u32[]{:S(2)}) collective-permute-start(bf16[180,4,128]{2,1,0:T(4,128)(2,1)S(1)} %slice.43), channel_id=1, source_target_pairs={{0,14},{2,0},{4,2},{6,4},{8,6},{10,8},{12,10},{14,12},{1,15},{3,1}... | collective-permute-start | bytes 552968 | tf_op jit(solution)/shard_map/ppermute | solution.py:371
  9.5 1.2 %copy.22.tokens_ref = bf16[8,128,180]{2,1,0:T(8,128)(2,1)S(1)} copy(bf16[8,128,180]{1,0,2:T(8,128)(2,1)} %param.9) | data formatting | bytes 737280 | tf_op args[0]
  10.8 0.0 copy-done.5
  10.8 0.3 copy.23.grad_ref
  11.1 0.0 copy-done.2
  11.2 0.1 copy.18
  11.3 0.1 pad_maximum_fusion
  11.4 0.0 collective-permute-start.2
  11.4 0.1 copy.21
  11.5 0.1 pad_maximum_fusion.1
  11.6 1.5 %collective-permute-start.3 = (bf16[4,4,361]{2,1,0:T(4,128)(2,1)S(1)}, bf16[4,4,361]{2,1,0:T(4,128)(2,1)S(1)}, u32[]{:S(2)}, u32[]{:S(2)}) collective-permute-start(bf16[4,4,361]{2,1,0:T(4,128)(2,1)S(1)} %pad_maximum_fusion.1), channel_id=1, source_target_pairs={{0,15},{1,14},{2,1},{3,0},{4,3},{5,2},{6,5},{7,4},{8,7},{9,6},{10,... | collective-permute-start | bytes 34664 | tf_op jit(solution)/shard_map/ppermute | solution.py:379
  13.1 0.0 copy-done.7
  13.1 0.0 copy-done.6
  13.1 0.0 copy-done.3
  13.1 0.0 copy-done.4
  13.2 0.0 copy-done
  13.2 0.0 copy-done.1
  13.2 1.1 %prepare.1 = (f32[6,64,128]{2,1,0:T(8,128)S(1)}, bf16[3,256,192]{2,1,0:T(8,128)(2,1)S(1)}, bf16[3,192,256]{2,1,0:T(8,128)(2,1)S(1)}, bf16[192,180]{1,0:T(8,128)(2,1)S(1)}, bf16[3,180,180]{2,1,0:T(8,128)(2,1)S(1)}) custom-call(bf16[180,540]{1,0:T(8,128)(2,1)S(1)} %copy-done, f32[1,540]{1,0:T(1,128)S(1)} %broadcast_in_dim.23.offsets_ref, ...), custom_call_target="tpu_custom_call" | custom-call | tf_op jit(solution)/shard_map/prepare/pallas_call | solution.py:426
  14.3 0.0 collective-permute-done.2.right_ref
  14.3 1.7 %collective-permute-done.3.corner_ref = bf16[4,4,361]{2,1,0:T(4,128)(2,1)S(1)} collective-permute-done((bf16[4,4,361]{2,1,0:T(4,128)(2,1)S(1)}, bf16[4,4,361]{2,1,0:T(4,128)(2,1)S(1)}, u32[]{:S(2)}, u32[]{:S(2)}) %collective-permute-start.3) | collective-permute-done | bytes 11584 | tf_op jit(solution)/shard_map/ppermute | solution.py:379
  16.0 0.0 collective-permute-done.x_below_ref
  16.0 0.0 collective-permute-done.1.g_below_ref
  16.0 7.0 %window_attention_backward.1 = (bf16[560,128]{1,0:T(8,128)(2,1)S(1)}, bf16[560,128]{1,0:T(8,128)(2,1)S(1)}, bf16[3,1024,180]{2,1,0:T(8,128)(2,1)S(1)}, f32[1024,...) custom-call(bf16[8,128,180]{2,1,0:T(8,128)(2,1)S(1)} %copy.22.tokens_ref, ...), custom_call_target="tpu_custom_call" | custom-call | tf_op jit(solution)/shard_map/window_attention_backward/pallas_call | solution.py:444
  23.0 0.1 collective-permute-start.4
  23.1 1.4 %collective-permute-done.4 = bf16[560,128]{1,0:T(8,128)(2,1)S(1)} collective-permute-done((bf16[560,128]{1,0:T(8,128)(2,1)S(1)}, bf16[560,128]{1,0:T(8,128)(2,1)S(1)}, u32[]{:S(2)}, u32[]{:S(2)}) %collective-permute-start.4) | collective-permute-done | bytes 143392 | tf_op jit(solution)/shard_map/ppermute | solution.py:371
  24.5 1.3 %collective-permute-start.5 = (bf16[560,128]{1,0:T(8,128)(2,1)S(1)}, bf16[560,128]{1,0:T(8,128)(2,1)S(1)}, u32[]{:S(2)}, u32[]{:S(2)}) collective-permute-start(bf16[560,128]{1,0:T(8,128)(2,1)S(1)} %add_convert_fusion.3), channel_id=1, source_target_pairs={{0,2},{1,5},{2,0},{3,7},{4,6},{5,1},{6,4},{7,3},{8,10},{9,13},{10,... | collective-permute-start | bytes 430088 | tf_op jit(solution)/shard_map/ppermute | solution.py:502
  25.8 1.5 %input_backward.1 = bf16[180,8,128]{2,1,0:T(8,128)(2,1)S(1)} custom-call(bf16[3,1024,180]{2,1,0:T(8,128)(2,1)S(1)} %get-tuple-element.44.d_qkv_ref, f32[1024,256]{1,0:T(8,128)S(1)} %get-tuple-element.45.unit_ref, f32[1024,1]{1,0:T(8,128)S(1)} %get-tuple-element.46.inv_ref, f32[16,8,8,180]{3,2,1,0:T(8,128)S(1)} %get-tuple-element.47.g_ref, ...), custom_call_target="tpu_custom_call" | custom-call | flops 1000000000 | tf_op jit(solution)/shard_map/input_backward/pallas_call | solution.py:483
  27.2 2.4 %collective-permute-done.5 = bf16[560,128]{1,0:T(8,128)(2,1)S(1)} collective-permute-done((bf16[560,128]{1,0:T(8,128)(2,1)S(1)}, bf16[560,128]{1,0:T(8,128)(2,1)S(1)}, u32[]{:S(2)}, u32[]{:S(2)}) %collective-permute-start.5) | collective-permute-done | bytes 143392 | tf_op jit(solution)/shard_map/ppermute | solution.py:502
  29.7 0.1 collective-permute-start.6
  29.8 0.0 collective-permute-start.7
  29.8 6.5 %collective-permute-done.6 = bf16[560,128]{1,0:T(8,128)(2,1)S(1)} collective-permute-done((bf16[560,128]{1,0:T(8,128)(2,1)S(1)}, bf16[560,128]{1,0:T(8,128)(2,1)S(1)}, u32[]{:S(2)}, u32[]{:S(2)}) %collective-permute-start.6) | collective-permute-done | bytes 143392 | tf_op jit(solution)/shard_map/ppermute | solution.py:502
  36.3 0.0 collective-permute-done.7
  36.3 0.1 broadcast_select_fusion
  36.4 0.7 %collective-permute-start.9 = (bf16[560,128]{1,0:T(8,128)(2,1)S(1)}, bf16[560,128]{1,0:T(8,128)(2,1)S(1)}, u32[]{:S(2)}, u32[]{:S(2)}) collective-permute-start(bf16[560,128]{1,0:T(8,128)(2,1)S(1)} %add_convert_fusion.1), channel_id=1, source_target_pairs={{0,8},{1,3},{2,10},{3,1},{4,12},{5,7},{6,14},{7,5},{8,0},{9,11},{1... | collective-permute-start | bytes 430088 | tf_op jit(solution)/shard_map/ppermute | solution.py:502
  37.1 0.1 fusion.2
  37.3 2.8 %collective-permute-start.8 = (bf16[180,4,128]{2,1,0:T(4,128)(2,1)S(1)}, bf16[180,4,128]{2,1,0:T(4,128)(2,1)S(1)}, u32[]{:S(2)}, u32[]{:S(2)}) collective-permute-start(bf16[180,4,128]{2,1,0:T(4,128)(2,1)S(1)} %get-tuple-element.63), channel_id=1, source_target_pairs={{0,2},{2,4},{4,6},{6,8},{8,10},{10,12},{12,14},{14,0},{1,3},{3,5},... | collective-permute-start | bytes 552968 | tf_op jit(solution)/shard_map/ppermute | solution.py:371
  40.0 3.2 %collective-permute-done.9 = bf16[560,128]{1,0:T(8,128)(2,1)S(1)} collective-permute-done((bf16[560,128]{1,0:T(8,128)(2,1)S(1)}, bf16[560,128]{1,0:T(8,128)(2,1)S(1)}, u32[]{:S(2)}, u32[]{:S(2)}) %collective-permute-start.9) | collective-permute-done | bytes 143392 | tf_op jit(solution)/shard_map/ppermute | solution.py:502
  43.2 0.1 collective-permute-start.10
  43.3 3.7 %collective-permute-done.8 = bf16[180,4,128]{2,1,0:T(4,128)(2,1)S(1)} collective-permute-done((bf16[180,4,128]{2,1,0:T(4,128)(2,1)S(1)}, bf16[180,4,128]{2,1,0:T(4,128)(2,1)S(1)}, u32[]{:S(2)}, u32[]{:S(2)}) %collective-permute-start.8) | collective-permute-done | bytes 184352 | tf_op jit(solution)/shard_map/ppermute | solution.py:371
  47.0 0.9 %maximum_bitcast_fusion = bf16[8,128,180]{1,0,2:T(8,128)(2,1)} fusion(bf16[180,4,128]{2,1,0:T(4,128)(2,1)S(1)} %get-tuple-element.64, bf16[180,4,128]{2,1,0:T(4,128)(2,1)S(1)} %collective-permute-done.8), kind=kLoop, calls=%fused_computation | loop fusion | flops 737280 | bytes 737280 | tf_op jit(solution)/shard_map/transpose | solution.py:503
  48.0 0.0 collective-permute-done.10.other_ref
  48.0 1.9 %finish.1 = (f32[180,540]{1,0:T(8,128)}, f32[540]{0:T(1024)}, f32[180,180]{1,0:T(8,128)}, f32[6,225]{1,0:T(8,128)}, f32[180]{0:T(256)}, /*index=5*/f32[180]{0:T(256)}) custom-call(bf16[560,128]{1,0:T(8,128)(2,1)S(1)} %add_convert_fusion.mine_ref, bf16[560,128]{1,0:T(8,128)(2,1)S(1)} %collective-permute-done.10.other_ref, s32[1]{0:T(128)} %bitcast.7.core_ref, ...), custom_call_target="tpu_custom_call" | custom-call | tf_op jit(solution)/shard_map/finish/pallas_call | solution.py:507
  (13 shorter events, 0.2 us)
Async XLA Ops:
  0.6 10.1 %copy-start.5 = (bf16[8,128,180]{1,0,2:T(8,128)(2,1)S(1)}, bf16[8,128,180]{1,0,2:T(8,128)(2,1)}, u32[]{:S(2)}) copy-start(bf16[8,128,180]{1,0,2:T(8,128)(2,1)} %param.10) | copy-start | bytes 1105924
  0.6 10.5 %copy-start.2 = (s32[8,128]{1,0:T(8,128)S(1)}, s32[8,128]{1,0:T(8,128)}, u32[]{:S(2)}) copy-start(s32[8,128]{1,0:T(8,128)} %region_ref.1) | copy-start | bytes 12292
  0.7 12.4 %copy-start.7 = (f32[540]{0:T(1024)S(1)}, f32[540]{0:T(1024)}, u32[]{:S(2)}) copy-start(f32[540]{0:T(1024)} %param.15) | copy-start | bytes 6484
  0.7 12.4 %copy-start.6 = (f32[225,6]{0,1:T(8,128)S(1)}, f32[225,6]{0,1:T(8,128)}, u32[]{:S(2)}) copy-start(f32[225,6]{0,1:T(8,128)} %param.17) | copy-start | bytes 16204
  0.7 12.4 %copy-start.3 = (f32[180]{0:T(256)S(1)}, f32[180]{0:T(256)}, u32[]{:S(2)}) copy-start(f32[180]{0:T(256)} %param.12) | copy-start | bytes 2164
  0.7 12.5 %copy-start.4 = (f32[180]{0:T(256)S(1)}, f32[180]{0:T(256)}, u32[]{:S(2)}) copy-start(f32[180]{0:T(256)} %param.13) | copy-start | bytes 2164
  0.7 12.5 %copy-start = (bf16[180,540]{1,0:T(8,128)(2,1)S(1)}, bf16[180,540]{1,0:T(8,128)(2,1)}, u32[]{:S(2)}) copy-start(bf16[180,540]{1,0:T(8,128)(2,1)} %weight_ref.3) | copy-start | bytes 583204
  0.7 12.5 %copy-start.1 = (bf16[180,180]{1,0:T(8,128)(2,1)S(1)}, bf16[180,180]{1,0:T(8,128)(2,1)}, u32[]{:S(2)}) copy-start(bf16[180,180]{1,0:T(8,128)(2,1)} %proj_ref.3) | copy-start | bytes 194404
  1.9 14.1 %collective-permute-start = (bf16[180,4,128]{2,1,0:T(4,128)(2,1)S(1)}, bf16[180,4,128]{2,1,0:T(4,128)(2,1)S(1)}, u32[]{:S(2)}, u32[]{:S(2)}) collective-permute-start(bf16[180,4,128]{2,1,0:T(4,128)(2,1)S(1)} %slice.42), channel_id=1, source_target_pairs={{0,14},{2,0},{4,2},{6,4},{8,6},{10,8},{12,10},{14,12},{1,15},{3,1}... | collective-permute-start | bytes 552968 | tf_op jit(solution)/shard_map/ppermute | solution.py:371
  8.9 7.1 %collective-permute-start.1 = (bf16[180,4,128]{2,1,0:T(4,128)(2,1)S(1)}, bf16[180,4,128]{2,1,0:T(4,128)(2,1)S(1)}, u32[]{:S(2)}, u32[]{:S(2)}) collective-permute-start(bf16[180,4,128]{2,1,0:T(4,128)(2,1)S(1)} %slice.43), channel_id=1, source_target_pairs={{0,14},{2,0},{4,2},{6,4},{8,6},{10,8},{12,10},{14,12},{1,15},{3,1}... | collective-permute-start | bytes 552968 | tf_op jit(solution)/shard_map/ppermute | solution.py:371
  11.4 2.9 %collective-permute-start.2 = (bf16[4,4,361]{2,1,0:T(4,128)(2,1)S(1)}, bf16[4,4,361]{2,1,0:T(4,128)(2,1)S(1)}, u32[]{:S(2)}, u32[]{:S(2)}) collective-permute-start(bf16[4,4,361]{2,1,0:T(4,128)(2,1)S(1)} %pad_maximum_fusion), channel_id=1, source_target_pairs={{0,1},{1,0},{2,3},{3,2},{4,5},{5,4},{6,7},{7,6},{8,9},{9,8},{10,11... | collective-permute-start | bytes 34664 | tf_op jit(solution)/shard_map/ppermute | solution.py:371
  11.6 4.4 %collective-permute-start.3 = (bf16[4,4,361]{2,1,0:T(4,128)(2,1)S(1)}, bf16[4,4,361]{2,1,0:T(4,128)(2,1)S(1)}, u32[]{:S(2)}, u32[]{:S(2)}) collective-permute-start(bf16[4,4,361]{2,1,0:T(4,128)(2,1)S(1)} %pad_maximum_fusion.1), channel_id=1, source_target_pairs={{0,15},{1,14},{2,1},{3,0},{4,3},{5,2},{6,5},{7,4},{8,7},{9,6},{10,... | collective-permute-start | bytes 34664 | tf_op jit(solution)/shard_map/ppermute | solution.py:379
  23.0 1.4 %collective-permute-start.4 = (bf16[560,128]{1,0:T(8,128)(2,1)S(1)}, bf16[560,128]{1,0:T(8,128)(2,1)S(1)}, u32[]{:S(2)}, u32[]{:S(2)}) collective-permute-start(bf16[560,128]{1,0:T(8,128)(2,1)S(1)} %get-tuple-element.38), channel_id=1, source_target_pairs={{0,1},{1,0},{2,3},{3,2},{4,5},{5,4},{6,7},{7,6},{8,9},{9,8},{10,11... | collective-permute-start | bytes 430088 | tf_op jit(solution)/shard_map/ppermute | solution.py:371
  24.5 5.2 %collective-permute-start.5 = (bf16[560,128]{1,0:T(8,128)(2,1)S(1)}, bf16[560,128]{1,0:T(8,128)(2,1)S(1)}, u32[]{:S(2)}, u32[]{:S(2)}) collective-permute-start(bf16[560,128]{1,0:T(8,128)(2,1)S(1)} %add_convert_fusion.3), channel_id=1, source_target_pairs={{0,2},{1,5},{2,0},{3,7},{4,6},{5,1},{6,4},{7,3},{8,10},{9,13},{10,... | collective-permute-start | bytes 430088 | tf_op jit(solution)/shard_map/ppermute | solution.py:502
  29.7 6.6 %collective-permute-start.6 = (bf16[560,128]{1,0:T(8,128)(2,1)S(1)}, bf16[560,128]{1,0:T(8,128)(2,1)S(1)}, u32[]{:S(2)}, u32[]{:S(2)}) collective-permute-start(bf16[560,128]{1,0:T(8,128)(2,1)S(1)} %add_convert_fusion.2), channel_id=1, source_target_pairs={{0,4},{1,9},{2,6},{3,11},{4,0},{5,13},{6,2},{7,15},{8,12},{9,1},{1... | collective-permute-start | bytes 430088 | tf_op jit(solution)/shard_map/ppermute | solution.py:502
  29.8 6.5 %collective-permute-start.7 = (bf16[180,8,128]{2,1,0:T(8,128)(2,1)S(1)}, bf16[180,8,128]{2,1,0:T(8,128)(2,1)S(1)}, u32[]{:S(2)}, u32[]{:S(2)}) collective-permute-start(bf16[180,8,128]{2,1,0:T(8,128)(2,1)S(1)} %input_backward.1), channel_id=1, source_target_pairs={{0,1},{1,0},{2,3},{3,2},{4,5},{5,4},{6,7},{7,6},{8,9},{9,8},{10,11... | collective-permute-start | bytes 1105928 | tf_op jit(solution)/shard_map/ppermute | solution.py:371
  36.4 6.8 %collective-permute-start.9 = (bf16[560,128]{1,0:T(8,128)(2,1)S(1)}, bf16[560,128]{1,0:T(8,128)(2,1)S(1)}, u32[]{:S(2)}, u32[]{:S(2)}) collective-permute-start(bf16[560,128]{1,0:T(8,128)(2,1)S(1)} %add_convert_fusion.1), channel_id=1, source_target_pairs={{0,8},{1,3},{2,10},{3,1},{4,12},{5,7},{6,14},{7,5},{8,0},{9,11},{1... | collective-permute-start | bytes 430088 | tf_op jit(solution)/shard_map/ppermute | solution.py:502
  37.3 9.8 %collective-permute-start.8 = (bf16[180,4,128]{2,1,0:T(4,128)(2,1)S(1)}, bf16[180,4,128]{2,1,0:T(4,128)(2,1)S(1)}, u32[]{:S(2)}, u32[]{:S(2)}) collective-permute-start(bf16[180,4,128]{2,1,0:T(4,128)(2,1)S(1)} %get-tuple-element.63), channel_id=1, source_target_pairs={{0,2},{2,4},{4,6},{6,8},{8,10},{10,12},{12,14},{14,0},{1,3},{3,5},... | collective-permute-start | bytes 552968 | tf_op jit(solution)/shard_map/ppermute | solution.py:371
  43.2 4.7 %collective-permute-start.10 = (bf16[560,128]{1,0:T(8,128)(2,1)S(1)}, bf16[560,128]{1,0:T(8,128)(2,1)S(1)}, u32[]{:S(2)}, u32[]{:S(2)}) collective-permute-start(bf16[560,128]{1,0:T(8,128)(2,1)S(1)} %add_convert_fusion.mine_ref), channel_id=1, source_target_pairs={{0,1},{1,0},{2,3},{3,2},{4,5},{5,4},{6,7},{7,6},{8,9},{9,8},{10,11... | collective-permute-start | bytes 430088 | tf_op jit(solution)/shard_map/ppermute | solution.py:371

commit v5 on v4

--- a/solution.py
+++ b/solution.py
@@ -99,11 +99,86 @@
                 bias_ref[head, rj * WIN + cj : rj * WIN + cj + 1, :] = both[head : head + 1, :]
 
 
+def normalize(x, channels, gain_ref, offset_ref):
+    f32, bf16 = jnp.float32, jnp.bfloat16
+    lane = iota((1, 2 * LANES), 1)
+    center = jnp.sum(x, -1, keepdims=True) * (1.0 / channels)
+    away = jnp.where(lane < channels, x - center, 0.0)
+    variance = jnp.sum(away * away, -1, keepdims=True) * (1.0 / channels)
+    inv_std = lax.rsqrt(variance + 1e-05)
+    unit = away * inv_std
+    unit_low = jnp.where(lane == channels, 1.0, unit).astype(bf16)
+    normed = jnp.where(
+        (lane >= channels) & (lane < channels + 3), 1.0, unit * gain_ref[...] + offset_ref[...]
+    ).astype(bf16)
+    return unit, inv_std, unit_low, normed
+
+
+def project(normed, channels, tok_ref, chan_ref):
+    bf16 = jnp.bfloat16
+    scale = (channels // HEADS) ** (-0.5)
+    return (
+        (nn(normed, tok_ref[0, :, 0:channels]) * scale).astype(bf16),
+        nn(normed, tok_ref[1]).astype(bf16),
+        nn(normed, tok_ref[2]).astype(bf16),
+        (nt(chan_ref[0], normed) * scale).astype(bf16),
+        nt(chan_ref[1], normed).astype(bf16),
+        nt(chan_ref[2], normed).astype(bf16),
+    )
+
+
+def project_kernel(
+    tokens_ref,
+    x_below_ref,
+    right_ref,
+    gain_ref,
+    offset_ref,
+    tok_ref,
+    chan_ref,
+    unit_ref,
+    inv_ref,
+    unit_turned_ref,
+    q_tok_ref,
+    k_tok_ref,
+    v_tok_ref,
+    q_chan_ref,
+    k_chan_ref,
+    v_chan_ref,
+    x_last_ref,
+    turn_s,
+    x_s,
+):
+    rows, cols, channels = tokens_ref.shape
+    wins = cols // WIN
+    f32 = jnp.float32
+    x_s[:, :, :, LANES:] = jnp.zeros(x_s.shape[:3] + (LANES,), f32)
+    turn_s[...] = x_below_ref[...].astype(f32)
+    for r in range(rows):
+        if r < rows - SHIFT:
+            body = tokens_ref[r + SHIFT].astype(f32)
+            side = right_ref[r].astype(f32)[:, 0:channels]
+        else:
+            body = turn_s[:, r - (rows - SHIFT), :].T
+            side = jnp.zeros((SHIFT, channels), f32)
+        row = jnp.concatenate([body[SHIFT:], side], 0)
+        x_s[:, r, :, 0:channels] = row.reshape(wins, WIN, channels)
+    x_last_ref[...] = x_s[wins - 2 :]
+    unit, inv_std, unit_low, normed = normalize(
+        x_s[...].reshape(rows * cols, 2 * LANES), channels, gain_ref, offset_ref
+    )
+    unit_ref[...] = unit
+    inv_ref[...] = inv_std
+    unit_turned_ref[...] = unit_low.T[0 : unit_turned_ref.shape[0]]
+    results = project(normed, channels, tok_ref, chan_ref)
+    for target, value in zip(
+        (q_tok_ref, k_tok_ref, v_tok_ref, q_chan_ref, k_chan_ref, v_chan_ref), results
+    ):
+        target[...] = value
+
+
 def main_kernel(
-    tokens_ref,
     grad_ref,
     region_ref,
-    x_below_ref,
     g_below_ref,
     right_ref,
     corner_ref,
@@ -114,32 +189,32 @@
     chan_ref,
     proj_ref,
     proj_slots_ref,
+    unit_turned_ref,
+    q_tok_ref,
+    k_tok_ref,
+    v_tok_ref,
+    q_chan_ref,
+    k_chan_ref,
+    v_chan_ref,
+    x_last_ref,
     core_ref,
     keep_ref,
     send_ref,
     d_qkv_s,
-    unit_s,
-    inv_s,
     g_s,
+    unit_last_ref,
+    inv_last_ref,
     turn_s,
-    x_s,
+    x_last_s,
     id_s,
-    unit_low_s,
-    normed_s,
     grad_s,
-    q_tok_s,
-    k_tok_s,
-    v_tok_s,
     da_tok_s,
-    q_chan_s,
-    k_chan_s,
-    v_chan_s,
     da_chan_s,
     attended_s,
     score_s,
     pack_s,
 ):
-    rows, cols, channels = tokens_ref.shape
+    rows, cols, channels = grad_ref.shape
     head_size = channels // HEADS
     scale = head_size ** (-0.5)
     count = rows * cols
@@ -147,56 +222,35 @@
     f32 = jnp.float32
     bf16 = jnp.bfloat16
 
-    x_s[:, :, :, LANES:] = jnp.zeros(x_s.shape[:3] + (LANES,), f32)
-    turn_s[0:channels] = x_below_ref[...].astype(f32)
-    turn_s[channels:] = g_below_ref[...].astype(f32)
+    turn_s[...] = g_below_ref[...].astype(f32)
+    x_last_s[...] = x_last_ref[...]
     ids = region_ref[...].astype(f32).T
     at_id = slice(2 * channels, 2 * channels + 1)
     col_part = ids[:, 0:1] - 4.0 * jnp.floor(ids[:, 0:1] * 0.25)
     for r in range(rows):
         if r < rows - SHIFT:
-            x_body = tokens_ref[r + SHIFT].astype(f32)
             g_body = grad_ref[r + SHIFT].astype(f32)
             side = right_ref[r].astype(f32)
             id_body = ids[:, r + SHIFT : r + SHIFT + 1]
         else:
             here = r - (rows - SHIFT)
-            body = turn_s[:, here, :].T
-            x_body = body[:, 0:channels]
-            g_body = body[:, channels : 2 * channels]
+            g_body = turn_s[:, here, :].T
             side = corner_ref[here].astype(f32)
             id_body = col_part + 4.0 * jnp.floor(side[0:1, at_id] * 0.25)
-        x_row = jnp.concatenate([x_body[SHIFT:], side[:, 0:channels]], 0)
+            x_last_s[1, r, SHIFT:, 0:channels] = side[:, 0:channels]
         g_row = jnp.concatenate([g_body[SHIFT:], side[:, channels : 2 * channels]], 0)
         id_row = jnp.concatenate([id_body[SHIFT:], side[:, at_id]], 0)
-        x_s[:, r, :, 0:channels] = x_row.reshape(wins, WIN, channels)
         g_s[:, r, :, :] = g_row.reshape(wins, WIN, channels)
         id_s[:, r, :, :] = id_row.reshape(wins, WIN, 1)
-
-    x = x_s[...].reshape(count, 2 * LANES)
-    lane = iota((1, 2 * LANES), 1)
-    inside = lane < channels
-    center = jnp.sum(x, -1, keepdims=True) * (1.0 / channels)
-    away = jnp.where(inside, x - center, 0.0)
-    variance = jnp.sum(away * away, -1, keepdims=True) * (1.0 / channels)
-    inv_std = lax.rsqrt(variance + 1e-05)
-    unit = away * inv_std
-    unit_s[...] = unit
-    inv_s[...] = inv_std
-    unit_low_s[...] = jnp.where(lane == channels, 1.0, unit).astype(bf16)
-    normed_s[...] = jnp.where(
-        (lane >= channels) & (lane < channels + 3), 1.0, unit * gain_ref[...] + offset_ref[...]
-    ).astype(bf16)
     grad_s[...] = g_s[...].reshape(count, channels).astype(bf16)
 
-    normed = normed_s[...]
-    q_tok_s[...] = (nn(normed, tok_ref[0, :, 0:channels]) * scale).astype(bf16)
-    k_tok_s[...] = nn(normed, tok_ref[1]).astype(bf16)
-    v_tok_s[...] = nn(normed, tok_ref[2]).astype(bf16)
+    unit_last, inv_last, unit_low, normed = normalize(
+        x_last_s[...].reshape(LANES, 2 * LANES), channels, gain_ref, offset_ref
+    )
+    unit_last_ref[...] = unit_last
+    inv_last_ref[...] = inv_last
+    last = project(normed, channels, tok_ref, chan_ref)
     da_tok_s[...] = nt(grad_s[...], proj_ref[...]).astype(bf16)
-    q_chan_s[...] = (nt(chan_ref[0], normed) * scale).astype(bf16)
-    k_chan_s[...] = nt(chan_ref[1], normed).astype(bf16)
-    v_chan_s[...] = nt(chan_ref[2], normed).astype(bf16)
     da_chan_s[...] = nt(proj_slots_ref[...], grad_s[...]).astype(bf16)
 
     score_s[...] = jnp.zeros(score_s.shape, f32)
@@ -227,14 +281,17 @@
             [jnp.where(head_of == head, tok, jnp.zeros_like(tok)) for head in range(HEADS)], 0
         )
 
-    def pair_step(pair, carry):
-        at = pl.ds(pl.multiple_of(pair * LANES, LANES), LANES)
-        hot = jnp.where(id_s[pl.ds(pair * 2, 2)].reshape(LANES, 1) == id_lane, 1.0, 0.0).astype(bf16)
+    for pair in range(count // LANES):
+        at = slice(pair * LANES, (pair + 1) * LANES)
+        if (pair + 1) * LANES == count:
+            q_tok, k_tok, v_tok, q_chan, k_chan, v_chan = last
+        else:
+            q_tok, k_tok, v_tok = q_tok_ref[at, :], k_tok_ref[at, :], v_tok_ref[at, :]
+            q_chan, k_chan, v_chan = q_chan_ref[:, at], k_chan_ref[:, at], v_chan_ref[:, at]
+        hot = jnp.where(id_s[pair * 2 : pair * 2 + 2].reshape(LANES, 1) == id_lane, 1.0, 0.0).astype(bf16)
         match = pack(nt(hot, hot)) > 0.5
-        k_chan = k_chan_s[:, at]
-        v_chan = v_chan_s[:, at]
-        scores = nn(k_tok_s[at, :], in_blocks(q_chan_s[:, at]))
-        d_prob = nn(v_tok_s[at, :], in_blocks(da_chan_s[:, at]))
+        scores = nn(k_tok, in_blocks(q_chan))
+        d_prob = nn(v_tok, in_blocks(da_chan_s[:, at]))
         attended = []
         d_query = []
         probs = []
@@ -257,15 +314,12 @@
         attended_s[:, at] = jnp.concatenate(attended, 0).astype(bf16)
         d_query = jnp.concatenate([piece[0:head_size] for piece in d_query], 0)
         d_qkv_s[0, at, :] = d_query.T.astype(bf16)
-        d_qkv_s[1, at, :] = nn(jnp.concatenate(d_scores, 1), by_head(q_tok_s[at, :])).astype(bf16)
+        d_qkv_s[1, at, :] = nn(jnp.concatenate(d_scores, 1), by_head(q_tok)).astype(bf16)
         d_qkv_s[2, at, :] = nn(jnp.concatenate(probs, 1), by_head(da_tok_s[at, :])).astype(bf16)
-        return carry
-
-    lax.fori_loop(0, count // LANES, pair_step, 0, unroll=True)
-
-    unit_turned = unit_low_s[...].T[0:ROWS]
+
+    unit_turned = jnp.concatenate([unit_turned_ref[:, : count - LANES], unit_low.T[0 : unit_turned_ref.shape[0]]], 1)
     rest = channels - LANES
-    pieces = [nn(unit_turned, d_qkv_s[part]) for part in range(3)]
+    pieces = [nn(unit_turned, d_qkv_s[part])[0:ROWS] for part in range(3)]
     d_proj = nn(attended_s[...], grad_s[...])
     pieces.append(
         jnp.concatenate([unslot(d_proj, head_size), jnp.zeros((ROWS - channels, channels), f32)], 0)
@@ -303,16 +357,19 @@
     send_ref[...] = jnp.where(lower, high_half, low_half)
 
 
-def input_kernel(d_qkv_ref, unit_ref, inv_ref, g_ref, gain_ref, parts_ref, framed_ref, turn_s):
+def input_kernel(
+    d_qkv_ref, g_ref, unit_last_ref, inv_last_ref, unit_ref, inv_ref, gain_ref, parts_ref, framed_ref, turn_s
+):
     wins, rows, _, channels = g_ref.shape
     cols = wins * WIN
     f32 = jnp.float32
     d_normed = sum(nt(d_qkv_ref[part], parts_ref[part]) for part in range(3))
     scaled = d_normed * gain_ref[:, 0:channels]
-    unit = unit_ref[:, 0:channels]
+    unit = jnp.concatenate([unit_ref[:-LANES, 0:channels], unit_last_ref[:, 0:channels]], 0)
+    inv_std = jnp.concatenate([inv_ref[:-LANES], inv_last_ref[...]], 0)
     mean_one = jnp.sum(scaled, -1, keepdims=True) * (1.0 / channels)
     mean_two = jnp.sum(scaled * unit, -1, keepdims=True) * (1.0 / channels)
-    d_input = inv_ref[...] * (scaled - mean_one - unit * mean_two)
+    d_input = inv_std * (scaled - mean_one - unit * mean_two)
     done = g_ref[...] + d_input.reshape(g_ref.shape)
     for r in range(rows):
         row = done[:, r].reshape(cols, channels)
@@ -405,8 +462,10 @@
     core = lax.axis_index("col").astype(jnp.int32).reshape(1)
 
     x_below = from_behind(x_turned[:, :SHIFT], "row", -1)
-    g_below = from_behind(g_turned[:, :SHIFT], "row", -1)
-    near_tokens, near_grad, near_ids = tokens, grad_out, regions
+    g_rows, near_tokens, near_grad, near_ids = lax.optimization_barrier(
+        (g_turned[:, :SHIFT], tokens, grad_out, regions)
+    )
+    g_below = from_behind(g_rows, "row", -1)
 
     def border(row_slice):
         return jnp.concatenate(
@@ -436,11 +495,36 @@
         in_specs=[whole()] * 4,
         out_specs=(whole(),) * 5,
         compiler_params=params,
+        cost_estimate=pl.CostEstimate(flops=1000, bytes_accessed=1000, transcendentals=0),
     )(qkv_weight, qkv_bias[None], proj_weight, table)
 
     gain = jnp.pad(ln_gain, (0, 2 * LANES - channels))[None]
     offset = jnp.pad(ln_offset, (0, 2 * LANES - channels))[None]
     wins = cols // WIN
+    unit, inv, *projected = pl.pallas_call(
+        project_kernel,
+        name="project",
+        out_shape=(
+            jax.ShapeDtypeStruct((count, 2 * LANES), f32),
+            jax.ShapeDtypeStruct((count, 1), f32),
+            jax.ShapeDtypeStruct((wide, count), bf16),
+            jax.ShapeDtypeStruct((count, channels), bf16),
+            jax.ShapeDtypeStruct((count, wide), bf16),
+            jax.ShapeDtypeStruct((count, wide), bf16),
+            jax.ShapeDtypeStruct((wide, count), bf16),
+            jax.ShapeDtypeStruct((wide, count), bf16),
+            jax.ShapeDtypeStruct((wide, count), bf16),
+            jax.ShapeDtypeStruct((2, rows, WIN, 2 * LANES), f32),
+        ),
+        in_specs=[whole()] * 7,
+        out_specs=(whole(),) * 10,
+        scratch_shapes=[
+            pltpu.VMEM((channels, SHIFT, cols), f32),
+            pltpu.VMEM((wins, rows, WIN, 2 * LANES), f32),
+        ],
+        compiler_params=params,
+        cost_estimate=pl.CostEstimate(flops=1000, bytes_accessed=1000, transcendentals=0),
+    )(near_tokens, x_below, right, gain, offset, tok, chan)
     keep, send, *saved = pl.pallas_call(
         main_kernel,
         name="window_attention_backward",
@@ -448,26 +532,18 @@
             jax.ShapeDtypeStruct((BUFFER_ROWS // 2, LANES), bf16),
             jax.ShapeDtypeStruct((BUFFER_ROWS // 2, LANES), bf16),
             jax.ShapeDtypeStruct((3, count, channels), bf16),
-            jax.ShapeDtypeStruct((count, 2 * LANES), f32),
-            jax.ShapeDtypeStruct((count, 1), f32),
             jax.ShapeDtypeStruct((wins, rows, WIN, channels), f32),
+            jax.ShapeDtypeStruct((LANES, 2 * LANES), f32),
+            jax.ShapeDtypeStruct((LANES, 1), f32),
         ),
-        in_specs=[whole()] * 14 + [whole(pltpu.SMEM)],
+        in_specs=[whole()] * 20 + [whole(pltpu.SMEM)],
         out_specs=(whole(),) * 6,
         scratch_shapes=[
-            pltpu.VMEM((2 * channels, SHIFT, cols), f32),
-            pltpu.VMEM((wins, rows, WIN, 2 * LANES), f32),
+            pltpu.VMEM((channels, SHIFT, cols), f32),
+            pltpu.VMEM((2, rows, WIN, 2 * LANES), f32),
             pltpu.VMEM((wins, rows, WIN, 1), f32),
-            pltpu.VMEM((count, 2 * LANES), bf16),
-            pltpu.VMEM((count, 2 * LANES), bf16),
             pltpu.VMEM((count, channels), bf16),
             pltpu.VMEM((count, channels), bf16),
-            pltpu.VMEM((count, wide), bf16),
-            pltpu.VMEM((count, wide), bf16),
-            pltpu.VMEM((count, channels), bf16),
-            pltpu.VMEM((wide, count), bf16),
-            pltpu.VMEM((wide, count), bf16),
-            pltpu.VMEM((wide, count), bf16),
             pltpu.VMEM((wide, count), bf16),
             pltpu.VMEM((wide, count), bf16),
             pltpu.VMEM((HEADS, SPAN, LANES), f32),
@@ -475,8 +551,10 @@
         ],
         compiler_params=params,
     )(
-        near_tokens, near_grad, near_ids, x_below, g_below, right, corner, gain, offset, bias, tok, chan, proj_weight, proj_slots, core
-    )
+        near_grad, near_ids, g_below, right, corner, gain, offset, bias, tok, chan, proj_weight, proj_slots,
+        *projected, core,
+    )
+    saved = [*saved, unit, inv]
 
     mine = add(keep, from_behind(send, "col", 1))
     mine, *saved = lax.optimization_barrier((mine, *saved))
@@ -484,7 +562,7 @@
         input_kernel,
         name="input_backward",
         out_shape=(jax.ShapeDtypeStruct((channels, rows, cols), bf16),),
-        in_specs=[whole()] * 6,
+        in_specs=[whole()] * 8,
         out_specs=(whole(),),
         scratch_shapes=[pltpu.VMEM((channels, rows, cols), f32)],
         compiler_params=params,

time: 50.1 us -> 48.6 us (0.970)
  waiting for transfers between devices: 18.8 us -> 15 us
  starting transfers between devices: 13.2 us -> 15.3 us
    ppermute x3, starting transfers between devices: 2.18 us -> 4.63 us  [on_device(): mine = add(mine, lax.ppermute(mine, ('row', 'col'), pairs))]
    ppermute x3, waiting for transfers between devices: 12 us -> 10 us  [on_device(): mine = add(mine, lax.ppermute(mine, ('row', 'col'), pairs))]
    pallas_call x0 -> x1, Pallas kernels: none -> 1.83 us  [on_device(): pl.pallas_call(project_kernel, name='project', out_shape=(jax.ShapeDtypeS...]
    ppermute x1, waiting for transfers between devices: 1.74 us -> 0.01 us  [diagonal(): return lax.ppermute(shard, ('row', 'col'), pairs)]
    optimization_barrier x0 -> x2, local copies, waits for them, and re-layouts: none -> 1.53 us  [on_device(): lax.optimization_barrier((g_turned[:, :SHIFT], tokens, grad_out, regions))]
    unnamed x18 -> x16, local copies, waits for them, and re-layouts: 1.57 us -> 0.04 us
    pallas_call x1, Pallas kernels: 6.96 us -> 5.48 us  [on_device(): pl.pallas_call(main_kernel, name='window_attention_backward', out_shape=(...]
    slice x2 -> x1, local copies, waits for them, and re-layouts: 1.05 us -> 1.04 us  [on_device(): g_turned[:, :SHIFT]]
  transfers between devices with their start and end apart: 11 -> 11, of which waited for: 6 -> 5; matrix products, arithmetic and copies ran while one was open for 8% -> 9% of each run, Pallas kernels for 5% -> 9%
where the time goes in v5:
time: 48.6 us; the launch traced here: 48.4 us
  starting transfers between devices  15.3 us (31%)
  waiting for transfers between devices  15 us (31%)
  Pallas kernels  11.7 us (24%)
  local copies, waits for them, and re-layouts  4.14 us (9%)
  other arithmetic  1.33 us (3%)
  between operations  0.92 us (2%)
    ppermute x3, waiting for transfers between devices, on_device(): mine = add(mine, lax.ppermute(mine, ('row', 'col'), pairs))  10 us
    ppermute x7, starting transfers between devices, from_behind(): lax.ppermute(shard, axis, [(i, (i + by) % count) for i in range(count)])  9.21 us
    pallas_call x1, Pallas kernels, on_device(): pl.pallas_call(main_kernel, name='window_attention_backward', out_shape=(...  5.48 us
    ppermute x7, waiting for transfers between devices, from_behind(): lax.ppermute(shard, axis, [(i, (i + by) % count) for i in range(count)])  5.01 us
    ppermute x3, starting transfers between devices, on_device(): mine = add(mine, lax.ppermute(mine, ('row', 'col'), pairs))  4.63 us
    pallas_call x1, Pallas kernels, on_device(): pl.pallas_call(functools.partial(finish_kernel, total_tokens ** (-0.5)),...  1.94 us
    pallas_call x1, Pallas kernels, on_device(): pl.pallas_call(project_kernel, name='project', out_shape=(jax.ShapeDtypeS...  1.83 us
    optimization_barrier x2, local copies, waits for them, and re-layouts, on_device(): lax.optimization_barrier((g_turned[:, :SHIFT], tokens, grad_out, regions))  1.53 us
  transfers between devices with their start and end apart: 11, of which 5 were waited for; matrix products, arithmetic and copies ran while one was open for 9% of the time, Pallas kernels for 9%

profile of v5, /device:TPU:0, one launch (start us, length us, event | category | flops | bytes accessed | tf_op | source)
XLA Modules:
  0.0 48.4 jit_solution(16288616728328447680)
XLA Ops:
  0.6 0.0 copy-start.5
  0.6 0.0 copy-start.2
  0.7 0.0 copy-start.7
  0.7 0.0 copy-start.6
  0.7 0.0 copy-start
  0.7 0.0 copy-start.1
  0.7 0.0 copy-start.3
  0.7 0.0 copy-start.4
  0.7 1.1 %slice.47 = bf16[180,4,128]{2,1,0:T(4,128)(2,1)S(1)} slice(bf16[180,8,128]{2,1,0:T(8,128)(2,1)} %bitcast.22), slice={[0:180], [0:4], [0:128]} | slice | bytes 368640 | tf_op jit(solution)/shard_map/slice | solution.py:464
  1.8 6.0 %collective-permute-start.3 = (bf16[180,4,128]{2,1,0:T(4,128)(2,1)S(1)}, bf16[180,4,128]{2,1,0:T(4,128)(2,1)S(1)}, u32[]{:S(2)}, u32[]{:S(2)}) collective-permute-start(bf16[180,4,128]{2,1,0:T(4,128)(2,1)S(1)} %slice.47), channel_id=1, source_target_pairs={{0,14},{2,0},{4,2},{6,4},{8,6},{10,8},{12,10},{14,12},{1,15},{3,1}... | collective-permute-start | bytes 552968 | tf_op jit(solution)/shard_map/ppermute | solution.py:428
  7.9 1.0 %slice.42 = bf16[180,4,128]{2,1,0:T(4,128)(2,1)S(1)} slice(bf16[180,8,128]{2,1,0:T(8,128)(2,1)} %bitcast.23), slice={[0:180], [0:4], [0:128]} | slice | bytes 368640 | tf_op jit(solution)/shard_map/slice | solution.py:466
  8.9 0.6 %collective-permute-start = (bf16[180,4,128]{2,1,0:T(4,128)(2,1)S(1)}, bf16[180,4,128]{2,1,0:T(4,128)(2,1)S(1)}, u32[]{:S(2)}, u32[]{:S(2)}) collective-permute-start(bf16[180,4,128]{2,1,0:T(4,128)(2,1)S(1)} %slice.42), channel_id=1, source_target_pairs={{0,14},{2,0},{4,2},{6,4},{8,6},{10,8},{12,10},{14,12},{1,15},{3,1}... | collective-permute-start | bytes 552968 | tf_op jit(solution)/shard_map/ppermute | solution.py:428
  9.5 1.2 %copy.16.tokens_ref = bf16[8,128,180]{2,1,0:T(8,128)(2,1)S(1)} copy(bf16[8,128,180]{1,0,2:T(8,128)(2,1)} %param.9) | data formatting | bytes 737280 | tf_op jit(solution)/shard_map/optimization_barrier | solution.py:465
  10.8 0.0 copy-done.5
  10.8 0.3 copy.23.grad_ref
  11.1 0.0 copy-done.2
  11.1 0.1 copy.18
  11.2 0.1 pad_maximum_fusion
  11.3 0.0 collective-permute-start.1
  11.4 0.1 copy.21
  11.5 0.1 pad_maximum_fusion.1
  11.6 1.5 %collective-permute-start.2 = (bf16[4,4,361]{2,1,0:T(4,128)(2,1)S(1)}, bf16[4,4,361]{2,1,0:T(4,128)(2,1)S(1)}, u32[]{:S(2)}, u32[]{:S(2)}) collective-permute-start(bf16[4,4,361]{2,1,0:T(4,128)(2,1)S(1)} %pad_maximum_fusion.1), channel_id=1, source_target_pairs={{0,15},{1,14},{2,1},{3,0},{4,3},{5,2},{6,5},{7,4},{8,7},{9,6},{10,... | collective-permute-start | bytes 34664 | tf_op jit(solution)/shard_map/ppermute | solution.py:436
  13.1 0.0 copy-done.7
  13.1 0.0 copy-done.6
  13.1 0.0 copy-done
  13.1 0.0 copy-done.1
  13.1 1.1 %prepare.1 = (f32[6,64,128]{2,1,0:T(8,128)S(1)}, bf16[3,256,192]{2,1,0:T(8,128)(2,1)S(1)}, bf16[3,192,256]{2,1,0:T(8,128)(2,1)S(1)}, bf16[192,180]{1,0:T(8,128)(2,1)S(1)}, bf16[3,180,180]{2,1,0:T(8,128)(2,1)S(1)}) custom-call(bf16[180,540]{1,0:T(8,128)(2,1)S(1)} %copy-done, f32[1,540]{1,0:T(1,128)S(1)} %broadcast_in_dim.23.offsets_ref, ...), custom_call_target="tpu_custom_call" | custom-call | flops 1000 | bytes 1000 | tf_op jit(solution)/shard_map/prepare/pallas_call | solution.py:485
  14.2 0.0 copy-done.3
  14.2 0.0 copy-done.4
  14.2 0.0 collective-permute-done.1.right_ref
  14.2 0.0 collective-permute-done.3.x_below_ref
  14.2 1.8 %project.1 = (f32[1024,256]{1,0:T(8,128)S(1)}, f32[1024,1]{1,0:T(8,128)S(1)}, bf16[192,1024]{1,0:T(8,128)(2,1)S(1)}, bf16[1024,180]{1,0:T(8,128)(2,1)S(1)}, bf16...) custom-call(bf16[8,128,180]{2,1,0:T(8,128)(2,1)S(1)} %copy.16.tokens, ...), custom_call_target="tpu_custom_call" | custom-call | flops 1000 | bytes 1000 | tf_op jit(solution)/shard_map/project/pallas_call | solution.py:504
  16.1 0.0 collective-permute-done.2.corner_ref
  16.1 0.0 collective-permute-done.g_below_ref
  16.1 5.5 %window_attention_backward.1 = (bf16[560,128]{1,0:T(8,128)(2,1)S(1)}, bf16[560,128]{1,0:T(8,128)(2,1)S(1)}, bf16[3,1024,180]{2,1,0:T(8,128)(2,1)S(1)}, f32[16,8,...) custom-call(bf16[8,128,180]{2,1,0:T(8,128)(2,1)S(1)} %copy.23.grad_ref, ...), custom_call_target="tpu_custom_call" | custom-call | tf_op jit(solution)/shard_map/window_attention_backward/pallas_call | solution.py:528
  21.6 0.1 collective-permute-start.4
  21.7 1.4 %collective-permute-done.4 = bf16[560,128]{1,0:T(8,128)(2,1)S(1)} collective-permute-done((bf16[560,128]{1,0:T(8,128)(2,1)S(1)}, bf16[560,128]{1,0:T(8,128)(2,1)S(1)}, u32[]{:S(2)}, u32[]{:S(2)}) %collective-permute-start.4) | collective-permute-done | bytes 143392 | tf_op jit(solution)/shard_map/ppermute | solution.py:428
  23.1 1.2 %collective-permute-start.5 = (bf16[560,128]{1,0:T(8,128)(2,1)S(1)}, bf16[560,128]{1,0:T(8,128)(2,1)S(1)}, u32[]{:S(2)}, u32[]{:S(2)}) collective-permute-start(bf16[560,128]{1,0:T(8,128)(2,1)S(1)} %add_convert_fusion.3), channel_id=1, source_target_pairs={{0,2},{1,5},{2,0},{3,7},{4,6},{5,1},{6,4},{7,3},{8,10},{9,13},{10,... | collective-permute-start | bytes 430088 | tf_op jit(solution)/shard_map/ppermute | solution.py:580
  24.2 1.3 %input_backward.1 = bf16[180,8,128]{2,1,0:T(8,128)(2,1)S(1)} custom-call(bf16[3,1024,180]{2,1,0:T(8,128)(2,1)S(1)} %get-tuple-element.74.d_qkv_ref, f32[16,8,8,180]{3,2,1,0:T(8,128)S(1)} %get-tuple-element.75.g_ref, f32[128,256]{1,0:T(8,128)S(1)} %get-tuple-element.76.unit_last_ref, f32[128,1]{1,0:T(8,128)S(1)} %get-tuple-element.77.inv_last_ref, ...), custom_call_target="tpu_custom_call" | custom-call | flops 1000000000 | tf_op jit(solution)/shard_map/input_backward/pallas_call | solution.py:561
  25.6 2.6 %collective-permute-done.5 = bf16[560,128]{1,0:T(8,128)(2,1)S(1)} collective-permute-done((bf16[560,128]{1,0:T(8,128)(2,1)S(1)}, bf16[560,128]{1,0:T(8,128)(2,1)S(1)}, u32[]{:S(2)}, u32[]{:S(2)}) %collective-permute-start.5) | collective-permute-done | bytes 143392 | tf_op jit(solution)/shard_map/ppermute | solution.py:580
  28.3 1.6 %collective-permute-start.6 = (bf16[560,128]{1,0:T(8,128)(2,1)S(1)}, bf16[560,128]{1,0:T(8,128)(2,1)S(1)}, u32[]{:S(2)}, u32[]{:S(2)}) collective-permute-start(bf16[560,128]{1,0:T(8,128)(2,1)S(1)} %add_convert_fusion.2), channel_id=1, source_target_pairs={{0,4},{1,9},{2,6},{3,11},{4,0},{5,13},{6,2},{7,15},{8,12},{9,1},{1... | collective-permute-start | bytes 430088 | tf_op jit(solution)/shard_map/ppermute | solution.py:580
  29.9 0.0 collective-permute-start.7
  29.9 4.1 %collective-permute-done.6 = bf16[560,128]{1,0:T(8,128)(2,1)S(1)} collective-permute-done((bf16[560,128]{1,0:T(8,128)(2,1)S(1)}, bf16[560,128]{1,0:T(8,128)(2,1)S(1)}, u32[]{:S(2)}, u32[]{:S(2)}) %collective-permute-start.6) | collective-permute-done | bytes 143392 | tf_op jit(solution)/shard_map/ppermute | solution.py:580
  34.1 0.0 collective-permute-done.7
  34.1 0.1 broadcast_select_fusion
  34.2 1.8 %collective-permute-start.9 = (bf16[560,128]{1,0:T(8,128)(2,1)S(1)}, bf16[560,128]{1,0:T(8,128)(2,1)S(1)}, u32[]{:S(2)}, u32[]{:S(2)}) collective-permute-start(bf16[560,128]{1,0:T(8,128)(2,1)S(1)} %add_convert_fusion.1), channel_id=1, source_target_pairs={{0,8},{1,3},{2,10},{3,1},{4,12},{5,7},{6,14},{7,5},{8,0},{9,11},{1... | collective-permute-start | bytes 430088 | tf_op jit(solution)/shard_map/ppermute | solution.py:580
  36.0 0.1 fusion.2
  36.1 2.4 %collective-permute-start.8 = (bf16[180,4,128]{2,1,0:T(4,128)(2,1)S(1)}, bf16[180,4,128]{2,1,0:T(4,128)(2,1)S(1)}, u32[]{:S(2)}, u32[]{:S(2)}) collective-permute-start(bf16[180,4,128]{2,1,0:T(4,128)(2,1)S(1)} %get-tuple-element.95), channel_id=1, source_target_pairs={{0,2},{2,4},{4,6},{6,8},{8,10},{10,12},{12,14},{14,0},{1,3},{3,5},... | collective-permute-start | bytes 552968 | tf_op jit(solution)/shard_map/ppermute | solution.py:428
  38.5 3.2 %collective-permute-done.9 = bf16[560,128]{1,0:T(8,128)(2,1)S(1)} collective-permute-done((bf16[560,128]{1,0:T(8,128)(2,1)S(1)}, bf16[560,128]{1,0:T(8,128)(2,1)S(1)}, u32[]{:S(2)}, u32[]{:S(2)}) %collective-permute-start.9) | collective-permute-done | bytes 143392 | tf_op jit(solution)/shard_map/ppermute | solution.py:580
  41.8 0.1 collective-permute-start.10
  41.9 3.6 %collective-permute-done.8 = bf16[180,4,128]{2,1,0:T(4,128)(2,1)S(1)} collective-permute-done((bf16[180,4,128]{2,1,0:T(4,128)(2,1)S(1)}, bf16[180,4,128]{2,1,0:T(4,128)(2,1)S(1)}, u32[]{:S(2)}, u32[]{:S(2)}) %collective-permute-start.8) | collective-permute-done | bytes 184352 | tf_op jit(solution)/shard_map/ppermute | solution.py:428
  45.5 0.9 %maximum_bitcast_fusion = bf16[8,128,180]{1,0,2:T(8,128)(2,1)} fusion(bf16[180,4,128]{2,1,0:T(4,128)(2,1)S(1)} %get-tuple-element.96, bf16[180,4,128]{2,1,0:T(4,128)(2,1)S(1)} %collective-permute-done.8), kind=kLoop, calls=%fused_computation | loop fusion | flops 737280 | bytes 737280 | tf_op jit(solution)/shard_map/transpose | solution.py:581
  46.5 0.0 collective-permute-done.10.other_ref
  46.5 1.9 %finish.1 = (f32[180,540]{1,0:T(8,128)}, f32[540]{0:T(1024)}, f32[180,180]{1,0:T(8,128)}, f32[6,225]{1,0:T(8,128)}, f32[180]{0:T(256)}, /*index=5*/f32[180]{0:T(256)}) custom-call(bf16[560,128]{1,0:T(8,128)(2,1)S(1)} %add_convert_fusion.mine_ref, bf16[560,128]{1,0:T(8,128)(2,1)S(1)} %collective-permute-done.10.other_ref, s32[1]{0:T(128)} %bitcast.7.core_ref, ...), custom_call_target="tpu_custom_call" | custom-call | tf_op jit(solution)/shard_map/finish/pallas_call | solution.py:585
  (12 shorter events, 0.2 us)
Async XLA Ops:
  0.6 10.1 %copy-start.5 = (bf16[8,128,180]{1,0,2:T(8,128)(2,1)S(1)}, bf16[8,128,180]{1,0,2:T(8,128)(2,1)}, u32[]{:S(2)}) copy-start(bf16[8,128,180]{1,0,2:T(8,128)(2,1)} %param.10) | copy-start | bytes 1105924
  0.6 10.4 %copy-start.2 = (s32[8,128]{1,0:T(8,128)S(1)}, s32[8,128]{1,0:T(8,128)}, u32[]{:S(2)}) copy-start(s32[8,128]{1,0:T(8,128)} %region_ref) | copy-start | bytes 12292
  0.7 12.4 %copy-start.7 = (f32[540]{0:T(1024)S(1)}, f32[540]{0:T(1024)}, u32[]{:S(2)}) copy-start(f32[540]{0:T(1024)} %param.15) | copy-start | bytes 6484
  0.7 12.4 %copy-start.6 = (f32[225,6]{0,1:T(8,128)S(1)}, f32[225,6]{0,1:T(8,128)}, u32[]{:S(2)}) copy-start(f32[225,6]{0,1:T(8,128)} %param.17) | copy-start | bytes 16204
  0.7 12.4 %copy-start = (bf16[180,540]{1,0:T(8,128)(2,1)S(1)}, bf16[180,540]{1,0:T(8,128)(2,1)}, u32[]{:S(2)}) copy-start(bf16[180,540]{1,0:T(8,128)(2,1)} %weight_ref.3) | copy-start | bytes 583204
  0.7 12.4 %copy-start.1 = (bf16[180,180]{1,0:T(8,128)(2,1)S(1)}, bf16[180,180]{1,0:T(8,128)(2,1)}, u32[]{:S(2)}) copy-start(bf16[180,180]{1,0:T(8,128)(2,1)} %proj_ref.3) | copy-start | bytes 194404
  0.7 13.5 %copy-start.3 = (f32[180]{0:T(256)S(1)}, f32[180]{0:T(256)}, u32[]{:S(2)}) copy-start(f32[180]{0:T(256)} %param.12) | copy-start | bytes 2164
  0.7 13.5 %copy-start.4 = (f32[180]{0:T(256)S(1)}, f32[180]{0:T(256)}, u32[]{:S(2)}) copy-start(f32[180]{0:T(256)} %param.13) | copy-start | bytes 2164
  1.8 12.4 %collective-permute-start.3 = (bf16[180,4,128]{2,1,0:T(4,128)(2,1)S(1)}, bf16[180,4,128]{2,1,0:T(4,128)(2,1)S(1)}, u32[]{:S(2)}, u32[]{:S(2)}) collective-permute-start(bf16[180,4,128]{2,1,0:T(4,128)(2,1)S(1)} %slice.47), channel_id=1, source_target_pairs={{0,14},{2,0},{4,2},{6,4},{8,6},{10,8},{12,10},{14,12},{1,15},{3,1}... | collective-permute-start | bytes 552968 | tf_op jit(solution)/shard_map/ppermute | solution.py:428
  8.9 7.2 %collective-permute-start = (bf16[180,4,128]{2,1,0:T(4,128)(2,1)S(1)}, bf16[180,4,128]{2,1,0:T(4,128)(2,1)S(1)}, u32[]{:S(2)}, u32[]{:S(2)}) collective-permute-start(bf16[180,4,128]{2,1,0:T(4,128)(2,1)S(1)} %slice.42), channel_id=1, source_target_pairs={{0,14},{2,0},{4,2},{6,4},{8,6},{10,8},{12,10},{14,12},{1,15},{3,1}... | collective-permute-start | bytes 552968 | tf_op jit(solution)/shard_map/ppermute | solution.py:428
  11.3 2.9 %collective-permute-start.1 = (bf16[4,4,361]{2,1,0:T(4,128)(2,1)S(1)}, bf16[4,4,361]{2,1,0:T(4,128)(2,1)S(1)}, u32[]{:S(2)}, u32[]{:S(2)}) collective-permute-start(bf16[4,4,361]{2,1,0:T(4,128)(2,1)S(1)} %pad_maximum_fusion), channel_id=1, source_target_pairs={{0,1},{1,0},{2,3},{3,2},{4,5},{5,4},{6,7},{7,6},{8,9},{9,8},{10,11... | collective-permute-start | bytes 34664 | tf_op jit(solution)/shard_map/ppermute | solution.py:428
  11.6 4.5 %collective-permute-start.2 = (bf16[4,4,361]{2,1,0:T(4,128)(2,1)S(1)}, bf16[4,4,361]{2,1,0:T(4,128)(2,1)S(1)}, u32[]{:S(2)}, u32[]{:S(2)}) collective-permute-start(bf16[4,4,361]{2,1,0:T(4,128)(2,1)S(1)} %pad_maximum_fusion.1), channel_id=1, source_target_pairs={{0,15},{1,14},{2,1},{3,0},{4,3},{5,2},{6,5},{7,4},{8,7},{9,6},{10,... | collective-permute-start | bytes 34664 | tf_op jit(solution)/shard_map/ppermute | solution.py:436
  21.6 1.4 %collective-permute-start.4 = (bf16[560,128]{1,0:T(8,128)(2,1)S(1)}, bf16[560,128]{1,0:T(8,128)(2,1)S(1)}, u32[]{:S(2)}, u32[]{:S(2)}) collective-permute-start(bf16[560,128]{1,0:T(8,128)(2,1)S(1)} %get-tuple-element.66), channel_id=1, source_target_pairs={{0,1},{1,0},{2,3},{3,2},{4,5},{5,4},{6,7},{7,6},{8,9},{9,8},{10,11... | collective-permute-start | bytes 430088 | tf_op jit(solution)/shard_map/ppermute | solution.py:428
  23.1 5.2 %collective-permute-start.5 = (bf16[560,128]{1,0:T(8,128)(2,1)S(1)}, bf16[560,128]{1,0:T(8,128)(2,1)S(1)}, u32[]{:S(2)}, u32[]{:S(2)}) collective-permute-start(bf16[560,128]{1,0:T(8,128)(2,1)S(1)} %add_convert_fusion.3), channel_id=1, source_target_pairs={{0,2},{1,5},{2,0},{3,7},{4,6},{5,1},{6,4},{7,3},{8,10},{9,13},{10,... | collective-permute-start | bytes 430088 | tf_op jit(solution)/shard_map/ppermute | solution.py:580
  28.3 5.8 %collective-permute-start.6 = (bf16[560,128]{1,0:T(8,128)(2,1)S(1)}, bf16[560,128]{1,0:T(8,128)(2,1)S(1)}, u32[]{:S(2)}, u32[]{:S(2)}) collective-permute-start(bf16[560,128]{1,0:T(8,128)(2,1)S(1)} %add_convert_fusion.2), channel_id=1, source_target_pairs={{0,4},{1,9},{2,6},{3,11},{4,0},{5,13},{6,2},{7,15},{8,12},{9,1},{1... | collective-permute-start | bytes 430088 | tf_op jit(solution)/shard_map/ppermute | solution.py:580
  29.9 4.2 %collective-permute-start.7 = (bf16[180,8,128]{2,1,0:T(8,128)(2,1)S(1)}, bf16[180,8,128]{2,1,0:T(8,128)(2,1)S(1)}, u32[]{:S(2)}, u32[]{:S(2)}) collective-permute-start(bf16[180,8,128]{2,1,0:T(8,128)(2,1)S(1)} %input_backward.1), channel_id=1, source_target_pairs={{0,1},{1,0},{2,3},{3,2},{4,5},{5,4},{6,7},{7,6},{8,9},{9,8},{10,11... | collective-permute-start | bytes 1105928 | tf_op jit(solution)/shard_map/ppermute | solution.py:428
  34.2 7.6 %collective-permute-start.9 = (bf16[560,128]{1,0:T(8,128)(2,1)S(1)}, bf16[560,128]{1,0:T(8,128)(2,1)S(1)}, u32[]{:S(2)}, u32[]{:S(2)}) collective-permute-start(bf16[560,128]{1,0:T(8,128)(2,1)S(1)} %add_convert_fusion.1), channel_id=1, source_target_pairs={{0,8},{1,3},{2,10},{3,1},{4,12},{5,7},{6,14},{7,5},{8,0},{9,11},{1... | collective-permute-start | bytes 430088 | tf_op jit(solution)/shard_map/ppermute | solution.py:580
  36.1 9.4 %collective-permute-start.8 = (bf16[180,4,128]{2,1,0:T(4,128)(2,1)S(1)}, bf16[180,4,128]{2,1,0:T(4,128)(2,1)S(1)}, u32[]{:S(2)}, u32[]{:S(2)}) collective-permute-start(bf16[180,4,128]{2,1,0:T(4,128)(2,1)S(1)} %get-tuple-element.95), channel_id=1, source_target_pairs={{0,2},{2,4},{4,6},{6,8},{8,10},{10,12},{12,14},{14,0},{1,3},{3,5},... | collective-permute-start | bytes 552968 | tf_op jit(solution)/shard_map/ppermute | solution.py:428
  41.8 4.7 %collective-permute-start.10 = (bf16[560,128]{1,0:T(8,128)(2,1)S(1)}, bf16[560,128]{1,0:T(8,128)(2,1)S(1)}, u32[]{:S(2)}, u32[]{:S(2)}) collective-permute-start(bf16[560,128]{1,0:T(8,128)(2,1)S(1)} %add_convert_fusion.mine_ref), channel_id=1, source_target_pairs={{0,1},{1,0},{2,3},{3,2},{4,5},{5,4},{6,7},{7,6},{8,9},{9,8},{10,11... | collective-permute-start | bytes 430088 | tf_op jit(solution)/shard_map/ppermute | solution.py:428

commit v6 on v5

--- a/solution.py
+++ b/solution.py
@@ -129,7 +129,7 @@
 
 def project_kernel(
     tokens_ref,
-    x_below_ref,
+    x_above_ref,
     right_ref,
     gain_ref,
     offset_ref,
@@ -152,14 +152,14 @@
     wins = cols // WIN
     f32 = jnp.float32
     x_s[:, :, :, LANES:] = jnp.zeros(x_s.shape[:3] + (LANES,), f32)
-    turn_s[...] = x_below_ref[...].astype(f32)
+    turn_s[...] = x_above_ref[...].astype(f32)
     for r in range(rows):
-        if r < rows - SHIFT:
-            body = tokens_ref[r + SHIFT].astype(f32)
-            side = right_ref[r].astype(f32)[:, 0:channels]
+        if r < SHIFT:
+            body = turn_s[:, r, :].T
+            side = jnp.zeros((SHIFT, channels), f32)
         else:
-            body = turn_s[:, r - (rows - SHIFT), :].T
-            side = jnp.zeros((SHIFT, channels), f32)
+            body = tokens_ref[r - SHIFT].astype(f32)
+            side = right_ref[r - SHIFT].astype(f32)[:, 0:channels]
         row = jnp.concatenate([body[SHIFT:], side], 0)
         x_s[:, r, :, 0:channels] = row.reshape(wins, WIN, channels)
     x_last_ref[...] = x_s[wins - 2 :]
@@ -179,7 +179,7 @@
 def main_kernel(
     grad_ref,
     region_ref,
-    g_below_ref,
+    g_above_ref,
     right_ref,
     corner_ref,
     gain_ref,
@@ -222,20 +222,19 @@
     f32 = jnp.float32
     bf16 = jnp.bfloat16
 
-    turn_s[...] = g_below_ref[...].astype(f32)
+    turn_s[...] = g_above_ref[...].astype(f32)
     x_last_s[...] = x_last_ref[...]
     ids = region_ref[...].astype(f32).T
     at_id = slice(2 * channels, 2 * channels + 1)
     col_part = ids[:, 0:1] - 4.0 * jnp.floor(ids[:, 0:1] * 0.25)
     for r in range(rows):
-        if r < rows - SHIFT:
-            g_body = grad_ref[r + SHIFT].astype(f32)
-            side = right_ref[r].astype(f32)
-            id_body = ids[:, r + SHIFT : r + SHIFT + 1]
+        if r >= SHIFT:
+            g_body = grad_ref[r - SHIFT].astype(f32)
+            side = right_ref[r - SHIFT].astype(f32)
+            id_body = ids[:, r - SHIFT : r - SHIFT + 1]
         else:
-            here = r - (rows - SHIFT)
-            g_body = turn_s[:, here, :].T
-            side = corner_ref[here].astype(f32)
+            g_body = turn_s[:, r, :].T
+            side = corner_ref[r].astype(f32)
             id_body = col_part + 4.0 * jnp.floor(side[0:1, at_id] * 0.25)
             x_last_s[1, r, SHIFT:, 0:channels] = side[:, 0:channels]
         g_row = jnp.concatenate([g_body[SHIFT:], side[:, channels : 2 * channels]], 0)
@@ -428,10 +427,10 @@
     return lax.ppermute(shard, axis, [(i, (i + by) % count) for i in range(count)])
 
 
-def diagonal(shard, by):
+def diagonal(shard):
     rows, cols = lax.axis_size("row"), lax.axis_size("col")
     pairs = [
-        (r * cols + c, ((r + by) % rows) * cols + (c + by) % cols) for r in range(rows) for c in range(cols)
+        (r * cols + c, ((r + 1) % rows) * cols + (c - 1) % cols) for r in range(rows) for c in range(cols)
     ]
     return lax.ppermute(shard, ("row", "col"), pairs)
 
@@ -461,11 +460,11 @@
     g_turned = grad_out.transpose(2, 0, 1)
     core = lax.axis_index("col").astype(jnp.int32).reshape(1)
 
-    x_below = from_behind(x_turned[:, :SHIFT], "row", -1)
+    x_above = from_behind(x_turned[:, rows - SHIFT :], "row", 1)
     g_rows, near_tokens, near_grad, near_ids = lax.optimization_barrier(
-        (g_turned[:, :SHIFT], tokens, grad_out, regions)
-    )
-    g_below = from_behind(g_rows, "row", -1)
+        (g_turned[:, rows - SHIFT :], tokens, grad_out, regions)
+    )
+    g_above = from_behind(g_rows, "row", 1)
 
     def border(row_slice):
         return jnp.concatenate(
@@ -477,8 +476,8 @@
             -1,
         )
 
-    right = from_behind(border(slice(SHIFT, None)), "col", -1)
-    corner = diagonal(border(slice(0, SHIFT)), -1)
+    right = from_behind(border(slice(0, rows - SHIFT)), "col", -1)
+    corner = diagonal(border(slice(rows - SHIFT, None)))
 
     table = jnp.pad(bias_table.T, ((0, 8 - HEADS), (0, 2 * LANES - bias_table.shape[0])))
     wide = HEADS * SLOT
@@ -524,7 +523,7 @@
         ],
         compiler_params=params,
         cost_estimate=pl.CostEstimate(flops=1000, bytes_accessed=1000, transcendentals=0),
-    )(near_tokens, x_below, right, gain, offset, tok, chan)
+    )(near_tokens, x_above, right, gain, offset, tok, chan)
     keep, send, *saved = pl.pallas_call(
         main_kernel,
         name="window_attention_backward",
@@ -551,7 +550,7 @@
         ],
         compiler_params=params,
     )(
-        near_grad, near_ids, g_below, right, corner, gain, offset, bias, tok, chan, proj_weight, proj_slots,
+        near_grad, near_ids, g_above, right, corner, gain, offset, bias, tok, chan, proj_weight, proj_slots,
         *projected, core,
     )
     saved = [*saved, unit, inv]
@@ -576,9 +575,9 @@
             framed = jnp.where(jnp.arange(cols) < SHIFT, beside, framed)
         if at == min(2, len(steps) - 1):
             mine, framed = lax.optimization_barrier((mine, framed))
-            above = from_behind(framed[:, rows - SHIFT :], "row", 1)
+            below = from_behind(framed[:, :SHIFT], "row", -1)
         mine = add(mine, lax.ppermute(mine, ("row", "col"), pairs))
-    d_tokens = jnp.concatenate([above, framed[:, : rows - SHIFT]], 1).transpose(1, 2, 0)
+    d_tokens = jnp.concatenate([framed[:, SHIFT:], below], 1).transpose(1, 2, 0)
     other = from_behind(mine, "col", 1)
 
     total_tokens = count * lax.axis_size("row") * lax.axis_size("col")

time: 48.6 us -> 46.9 us (0.965); the launches traced: 48.4 us -> 46.1 us
  starting transfers between devices: 15.3 us -> 8.56 us
  waiting for transfers between devices: 15 us -> 19.5 us
    ppermute x3, waiting for transfers between devices: 10 us -> 15.4 us  [on_device(): mine = add(mine, lax.ppermute(mine, ('row', 'col'), pairs))]
    ppermute x3, starting transfers between devices: 4.63 us -> 0.21 us  [on_device(): mine = add(mine, lax.ppermute(mine, ('row', 'col'), pairs))]
    ppermute x7, starting transfers between devices: 9.21 us -> 6.75 us  [from_behind(): lax.ppermute(shard, axis, [(i, (i + by) % count) for i in range(count)])]
    ppermute x7, waiting for transfers between devices: 5.01 us -> 3.33 us  [from_behind(): lax.ppermute(shard, axis, [(i, (i + by) % count) for i in range(count)])]
    ppermute x1, waiting for transfers between devices: 0.01 us -> 0.8 us  [diagonal(): return lax.ppermute(shard, ('row', 'col'), pairs)]
  transfers between devices with their start and end apart: 11 -> 11, of which waited for: 5 -> 8; matrix products, arithmetic and copies ran while one was open for 9% -> 9% of each run, Pallas kernels for 9% -> 9%
where the time goes in v6:
time: 46.9 us; the launch traced here: 46.1 us
  waiting for transfers between devices  19.5 us (42%)
  Pallas kernels  11.5 us (25%)
  starting transfers between devices  8.56 us (18%)
  local copies, waits for them, and re-layouts  4.24 us (9%)
  other arithmetic  1.33 us (3%)
  between operations  0.94 us (2%)
    ppermute x3, waiting for transfers between devices, on_device(): mine = add(mine, lax.ppermute(mine, ('row', 'col'), pairs))  15.4 us
    ppermute x7, starting transfers between devices, from_behind(): lax.ppermute(shard, axis, [(i, (i + by) % count) for i in range(count)])  6.75 us
    pallas_call x1, Pallas kernels, on_device(): pl.pallas_call(main_kernel, name='window_attention_backward', out_shape=(...  5.44 us
    ppermute x7, waiting for transfers between devices, from_behind(): lax.ppermute(shard, axis, [(i, (i + by) % count) for i in range(count)])  3.33 us
    pallas_call x1, Pallas kernels, on_device(): pl.pallas_call(functools.partial(finish_kernel, total_tokens ** (-0.5)),...  1.94 us
    pallas_call x1, Pallas kernels, on_device(): pl.pallas_call(project_kernel, name='project', out_shape=(jax.ShapeDtypeS...  1.75 us
    ppermute x1, starting transfers between devices, diagonal(): return lax.ppermute(shard, ('row', 'col'), pairs)  1.6 us
    optimization_barrier x2, local copies, waits for them, and re-layouts, on_device(): lax.optimization_barrier((g_turned[:, rows - SHIFT:], tokens, grad_out, r...  1.53 us
  transfers between devices with their start and end apart: 11, of which 8 were waited for; matrix products, arithmetic and copies ran while one was open for 9% of the time, Pallas kernels for 9%

profile of v6, /device:TPU:0, one launch (start us, length us, event | category | flops | bytes accessed | tf_op | source)
XLA Modules:
  0.0 46.1 jit_solution(2830760167062964499)
XLA Ops:
  0.6 0.0 copy-start.5
  0.6 0.0 copy-start.2
  0.7 0.0 copy-start.7
  0.7 0.0 copy-start.6
  0.7 0.0 copy-start
  0.7 0.0 copy-start.1
  0.7 0.0 copy-start.3
  0.7 0.0 copy-start.4
  0.7 1.2 %slice.47 = bf16[180,4,128]{2,1,0:T(4,128)(2,1)S(1)} slice(bf16[180,8,128]{2,1,0:T(8,128)(2,1)} %bitcast.22), slice={[0:180], [4:8], [0:128]} | slice | bytes 368640 | tf_op jit(solution)/shard_map/slice | solution.py:463
  1.9 3.0 %collective-permute-start.3 = (bf16[180,4,128]{2,1,0:T(4,128)(2,1)S(1)}, bf16[180,4,128]{2,1,0:T(4,128)(2,1)S(1)}, u32[]{:S(2)}, u32[]{:S(2)}) collective-permute-start(bf16[180,4,128]{2,1,0:T(4,128)(2,1)S(1)} %slice.47), channel_id=1, source_target_pairs={{0,2},{2,4},{4,6},{6,8},{8,10},{10,12},{12,14},{14,0},{1,3},{3,5},... | collective-permute-start | bytes 552968 | tf_op jit(solution)/shard_map/ppermute | solution.py:427
  4.9 1.1 %slice.42 = bf16[180,4,128]{2,1,0:T(4,128)(2,1)S(1)} slice(bf16[180,8,128]{2,1,0:T(8,128)(2,1)} %bitcast.23), slice={[0:180], [4:8], [0:128]} | slice | bytes 368640 | tf_op jit(solution)/shard_map/slice | solution.py:465
  6.0 1.6 %collective-permute-start = (bf16[180,4,128]{2,1,0:T(4,128)(2,1)S(1)}, bf16[180,4,128]{2,1,0:T(4,128)(2,1)S(1)}, u32[]{:S(2)}, u32[]{:S(2)}) collective-permute-start(bf16[180,4,128]{2,1,0:T(4,128)(2,1)S(1)} %slice.42), channel_id=1, source_target_pairs={{0,2},{2,4},{4,6},{6,8},{8,10},{10,12},{12,14},{14,0},{1,3},{3,5},... | collective-permute-start | bytes 552968 | tf_op jit(solution)/shard_map/ppermute | solution.py:427
  7.6 1.2 %copy.16.tokens_ref = bf16[8,128,180]{2,1,0:T(8,128)(2,1)S(1)} copy(bf16[8,128,180]{1,0,2:T(8,128)(2,1)} %param.9) | data formatting | bytes 737280 | tf_op jit(solution)/shard_map/optimization_barrier | solution.py:464
  8.8 0.0 copy-done.5
  8.8 0.3 copy.23.grad_ref
  9.1 0.0 copy-done.2
  9.2 0.1 copy.18
  9.3 0.1 pad_maximum_fusion
  9.4 0.0 collective-permute-start.1
  9.4 0.1 copy.21
  9.6 0.1 pad_maximum_fusion.1
  9.6 1.6 %collective-permute-start.2 = (bf16[4,4,361]{2,1,0:T(4,128)(2,1)S(1)}, bf16[4,4,361]{2,1,0:T(4,128)(2,1)S(1)}, u32[]{:S(2)}, u32[]{:S(2)}) collective-permute-start(bf16[4,4,361]{2,1,0:T(4,128)(2,1)S(1)} %pad_maximum_fusion.1), channel_id=1, source_target_pairs={{0,3},{1,2},{2,5},{3,4},{4,7},{5,6},{6,9},{7,8},{8,11},{9,10},{10,... | collective-permute-start | bytes 34664 | tf_op jit(solution)/shard_map/ppermute | solution.py:435
  11.2 0.0 copy-done.7
  11.2 0.0 copy-done.6
  11.3 0.0 copy-done
  11.3 0.0 copy-done.1
  11.3 1.1 %prepare.1 = (f32[6,64,128]{2,1,0:T(8,128)S(1)}, bf16[3,256,192]{2,1,0:T(8,128)(2,1)S(1)}, bf16[3,192,256]{2,1,0:T(8,128)(2,1)S(1)}, bf16[192,180]{1,0:T(8,128)(2,1)S(1)}, bf16[3,180,180]{2,1,0:T(8,128)(2,1)S(1)}) custom-call(bf16[180,540]{1,0:T(8,128)(2,1)S(1)} %copy-done, f32[1,540]{1,0:T(1,128)S(1)} %broadcast_in_dim.23.offsets_ref, ...), custom_call_target="tpu_custom_call" | custom-call | flops 1000 | bytes 1000 | tf_op jit(solution)/shard_map/prepare/pallas_call | solution.py:484
  12.4 0.0 copy-done.3
  12.4 0.0 copy-done.4
  12.4 0.0 collective-permute-done.1.right_ref
  12.4 1.0 %collective-permute-done.3.x_above_ref = bf16[180,4,128]{2,1,0:T(4,128)(2,1)S(1)} collective-permute-done((bf16[180,4,128]{2,1,0:T(4,128)(2,1)S(1)}, bf16[180,4,128]{2,1,0:T(4,128)(2,1)S(1)}, u32[]{:S(2)}, u32[]{:S(2)}) %collective-permute-start.3) | collective-permute-done | bytes 184352 | tf_op jit(solution)/shard_map/ppermute | solution.py:427
  13.4 1.8 %project.1 = (f32[1024,256]{1,0:T(8,128)S(1)}, f32[1024,1]{1,0:T(8,128)S(1)}, bf16[192,1024]{1,0:T(8,128)(2,1)S(1)}, bf16[1024,180]{1,0:T(8,128)(2,1)S(1)}, bf16...) custom-call(bf16[8,128,180]{2,1,0:T(8,128)(2,1)S(1)} %copy.16.tokens, ...), custom_call_target="tpu_custom_call" | custom-call | flops 1000 | bytes 1000 | tf_op jit(solution)/shard_map/project/pallas_call | solution.py:503
  15.1 0.8 %collective-permute-done.2.corner_ref = bf16[4,4,361]{2,1,0:T(4,128)(2,1)S(1)} collective-permute-done((bf16[4,4,361]{2,1,0:T(4,128)(2,1)S(1)}, bf16[4,4,361]{2,1,0:T(4,128)(2,1)S(1)}, u32[]{:S(2)}, u32[]{:S(2)}) %collective-permute-start.2) | collective-permute-done | bytes 11584 | tf_op jit(solution)/shard_map/ppermute | solution.py:435
  15.9 0.7 %collective-permute-done.g_above_ref = bf16[180,4,128]{2,1,0:T(4,128)(2,1)S(1)} collective-permute-done((bf16[180,4,128]{2,1,0:T(4,128)(2,1)S(1)}, bf16[180,4,128]{2,1,0:T(4,128)(2,1)S(1)}, u32[]{:S(2)}, u32[]{:S(2)}) %collective-permute-start) | collective-permute-done | bytes 184352 | tf_op jit(solution)/shard_map/ppermute | solution.py:427
  16.6 5.4 %window_attention_backward.1 = (bf16[560,128]{1,0:T(8,128)(2,1)S(1)}, bf16[560,128]{1,0:T(8,128)(2,1)S(1)}, bf16[3,1024,180]{2,1,0:T(8,128)(2,1)S(1)}, f32[16,8,...) custom-call(bf16[8,128,180]{2,1,0:T(8,128)(2,1)S(1)} %copy.23.grad_ref, ...), custom_call_target="tpu_custom_call" | custom-call | tf_op jit(solution)/shard_map/window_attention_backward/pallas_call | solution.py:527
  22.1 0.2 collective-permute-start.4
  22.3 1.2 %collective-permute-done.4 = bf16[560,128]{1,0:T(8,128)(2,1)S(1)} collective-permute-done((bf16[560,128]{1,0:T(8,128)(2,1)S(1)}, bf16[560,128]{1,0:T(8,128)(2,1)S(1)}, u32[]{:S(2)}, u32[]{:S(2)}) %collective-permute-start.4) | collective-permute-done | bytes 143392 | tf_op jit(solution)/shard_map/ppermute | solution.py:427
  23.6 0.1 collective-permute-start.5
  23.6 1.3 %input_backward.1 = bf16[180,8,128]{2,1,0:T(8,128)(2,1)S(1)} custom-call(bf16[3,1024,180]{2,1,0:T(8,128)(2,1)S(1)} %get-tuple-element.74.d_qkv_ref, f32[16,8,8,180]{3,2,1,0:T(8,128)S(1)} %get-tuple-element.75.g_ref, f32[128,256]{1,0:T(8,128)S(1)} %get-tuple-element.76.unit_last_ref, f32[128,1]{1,0:T(8,128)S(1)} %get-tuple-element.77.inv_last_ref, ...), custom_call_target="tpu_custom_call" | custom-call | flops 1000000000 | tf_op jit(solution)/shard_map/input_backward/pallas_call | solution.py:560
  25.0 3.7 %collective-permute-done.5 = bf16[560,128]{1,0:T(8,128)(2,1)S(1)} collective-permute-done((bf16[560,128]{1,0:T(8,128)(2,1)S(1)}, bf16[560,128]{1,0:T(8,128)(2,1)S(1)}, u32[]{:S(2)}, u32[]{:S(2)}) %collective-permute-start.5) | collective-permute-done | bytes 143392 | tf_op jit(solution)/shard_map/ppermute | solution.py:579
  28.8 0.1 collective-permute-start.6
  28.9 0.1 collective-permute-start.7
  28.9 6.5 %collective-permute-done.6 = bf16[560,128]{1,0:T(8,128)(2,1)S(1)} collective-permute-done((bf16[560,128]{1,0:T(8,128)(2,1)S(1)}, bf16[560,128]{1,0:T(8,128)(2,1)S(1)}, u32[]{:S(2)}, u32[]{:S(2)}) %collective-permute-start.6) | collective-permute-done | bytes 143392 | tf_op jit(solution)/shard_map/ppermute | solution.py:579
  35.4 0.0 collective-permute-done.7
  35.5 0.1 broadcast_select_fusion
  35.5 0.1 collective-permute-start.9
  35.6 0.1 fusion.2
  35.7 1.8 %collective-permute-start.8 = (bf16[180,4,128]{2,1,0:T(4,128)(2,1)S(1)}, bf16[180,4,128]{2,1,0:T(4,128)(2,1)S(1)}, u32[]{:S(2)}, u32[]{:S(2)}) collective-permute-start(bf16[180,4,128]{2,1,0:T(4,128)(2,1)S(1)} %get-tuple-element.96), channel_id=1, source_target_pairs={{0,14},{2,0},{4,2},{6,4},{8,6},{10,8},{12,10},{14,12},{1,15},{3,1}... | collective-permute-start | bytes 552968 | tf_op jit(solution)/shard_map/ppermute | solution.py:427
  37.5 5.2 %collective-permute-done.9 = bf16[560,128]{1,0:T(8,128)(2,1)S(1)} collective-permute-done((bf16[560,128]{1,0:T(8,128)(2,1)S(1)}, bf16[560,128]{1,0:T(8,128)(2,1)S(1)}, u32[]{:S(2)}, u32[]{:S(2)}) %collective-permute-start.9) | collective-permute-done | bytes 143392 | tf_op jit(solution)/shard_map/ppermute | solution.py:579
  42.8 0.1 collective-permute-start.10
  42.8 0.0 collective-permute-done.8
  42.8 0.9 %maximum_bitcast_fusion = bf16[8,128,180]{1,0,2:T(8,128)(2,1)} fusion(bf16[180,4,128]{2,1,0:T(4,128)(2,1)S(1)} %collective-permute-done.8, bf16[180,4,128]{2,1,0:T(4,128)(2,1)S(1)} %get-tuple-element.95), kind=kLoop, calls=%fused_computation | loop fusion | flops 737280 | bytes 737280 | tf_op jit(solution)/shard_map/transpose | solution.py:580
  43.8 0.4 collective-permute-done.10.other_ref
  44.2 1.9 %finish.1 = (f32[180,540]{1,0:T(8,128)}, f32[540]{0:T(1024)}, f32[180,180]{1,0:T(8,128)}, f32[6,225]{1,0:T(8,128)}, f32[180]{0:T(256)}, /*index=5*/f32[180]{0:T(256)}) custom-call(bf16[560,128]{1,0:T(8,128)(2,1)S(1)} %add_convert_fusion.mine_ref, bf16[560,128]{1,0:T(8,128)(2,1)S(1)} %collective-permute-done.10.other_ref, s32[1]{0:T(128)} %bitcast.7.core_ref, ...), custom_call_target="tpu_custom_call" | custom-call | tf_op jit(solution)/shard_map/finish/pallas_call | solution.py:584
  (12 shorter events, 0.2 us)
Async XLA Ops:
  0.6 8.2 %copy-start.5 = (bf16[8,128,180]{1,0,2:T(8,128)(2,1)S(1)}, bf16[8,128,180]{1,0,2:T(8,128)(2,1)}, u32[]{:S(2)}) copy-start(bf16[8,128,180]{1,0,2:T(8,128)(2,1)} %param.10) | copy-start | bytes 1105924
  0.6 8.5 %copy-start.2 = (s32[8,128]{1,0:T(8,128)S(1)}, s32[8,128]{1,0:T(8,128)}, u32[]{:S(2)}) copy-start(s32[8,128]{1,0:T(8,128)} %region_ref) | copy-start | bytes 12292
  0.7 10.6 %copy-start.7 = (f32[540]{0:T(1024)S(1)}, f32[540]{0:T(1024)}, u32[]{:S(2)}) copy-start(f32[540]{0:T(1024)} %param.15) | copy-start | bytes 6484
  0.7 10.6 %copy-start.6 = (f32[225,6]{0,1:T(8,128)S(1)}, f32[225,6]{0,1:T(8,128)}, u32[]{:S(2)}) copy-start(f32[225,6]{0,1:T(8,128)} %param.17) | copy-start | bytes 16204
  0.7 10.6 %copy-start = (bf16[180,540]{1,0:T(8,128)(2,1)S(1)}, bf16[180,540]{1,0:T(8,128)(2,1)}, u32[]{:S(2)}) copy-start(bf16[180,540]{1,0:T(8,128)(2,1)} %weight_ref.3) | copy-start | bytes 583204
  0.7 10.6 %copy-start.1 = (bf16[180,180]{1,0:T(8,128)(2,1)S(1)}, bf16[180,180]{1,0:T(8,128)(2,1)}, u32[]{:S(2)}) copy-start(bf16[180,180]{1,0:T(8,128)(2,1)} %proj_ref.3) | copy-start | bytes 194404
  0.7 11.7 %copy-start.3 = (f32[180]{0:T(256)S(1)}, f32[180]{0:T(256)}, u32[]{:S(2)}) copy-start(f32[180]{0:T(256)} %param.12) | copy-start | bytes 2164
  0.7 11.7 %copy-start.4 = (f32[180]{0:T(256)S(1)}, f32[180]{0:T(256)}, u32[]{:S(2)}) copy-start(f32[180]{0:T(256)} %param.13) | copy-start | bytes 2164
  1.9 11.5 %collective-permute-start.3 = (bf16[180,4,128]{2,1,0:T(4,128)(2,1)S(1)}, bf16[180,4,128]{2,1,0:T(4,128)(2,1)S(1)}, u32[]{:S(2)}, u32[]{:S(2)}) collective-permute-start(bf16[180,4,128]{2,1,0:T(4,128)(2,1)S(1)} %slice.47), channel_id=1, source_target_pairs={{0,2},{2,4},{4,6},{6,8},{8,10},{10,12},{12,14},{14,0},{1,3},{3,5},... | collective-permute-start | bytes 552968 | tf_op jit(solution)/shard_map/ppermute | solution.py:427
  6.0 10.7 %collective-permute-start = (bf16[180,4,128]{2,1,0:T(4,128)(2,1)S(1)}, bf16[180,4,128]{2,1,0:T(4,128)(2,1)S(1)}, u32[]{:S(2)}, u32[]{:S(2)}) collective-permute-start(bf16[180,4,128]{2,1,0:T(4,128)(2,1)S(1)} %slice.42), channel_id=1, source_target_pairs={{0,2},{2,4},{4,6},{6,8},{8,10},{10,12},{12,14},{14,0},{1,3},{3,5},... | collective-permute-start | bytes 552968 | tf_op jit(solution)/shard_map/ppermute | solution.py:427
  9.4 3.0 %collective-permute-start.1 = (bf16[4,4,361]{2,1,0:T(4,128)(2,1)S(1)}, bf16[4,4,361]{2,1,0:T(4,128)(2,1)S(1)}, u32[]{:S(2)}, u32[]{:S(2)}) collective-permute-start(bf16[4,4,361]{2,1,0:T(4,128)(2,1)S(1)} %pad_maximum_fusion), channel_id=1, source_target_pairs={{0,1},{1,0},{2,3},{3,2},{4,5},{5,4},{6,7},{7,6},{8,9},{9,8},{10,11... | collective-permute-start | bytes 34664 | tf_op jit(solution)/shard_map/ppermute | solution.py:427
  9.6 6.3 %collective-permute-start.2 = (bf16[4,4,361]{2,1,0:T(4,128)(2,1)S(1)}, bf16[4,4,361]{2,1,0:T(4,128)(2,1)S(1)}, u32[]{:S(2)}, u32[]{:S(2)}) collective-permute-start(bf16[4,4,361]{2,1,0:T(4,128)(2,1)S(1)} %pad_maximum_fusion.1), channel_id=1, source_target_pairs={{0,3},{1,2},{2,5},{3,4},{4,7},{5,6},{6,9},{7,8},{8,11},{9,10},{10,... | collective-permute-start | bytes 34664 | tf_op jit(solution)/shard_map/ppermute | solution.py:435
  22.1 1.4 %collective-permute-start.4 = (bf16[560,128]{1,0:T(8,128)(2,1)S(1)}, bf16[560,128]{1,0:T(8,128)(2,1)S(1)}, u32[]{:S(2)}, u32[]{:S(2)}) collective-permute-start(bf16[560,128]{1,0:T(8,128)(2,1)S(1)} %get-tuple-element.66), channel_id=1, source_target_pairs={{0,1},{1,0},{2,3},{3,2},{4,5},{5,4},{6,7},{7,6},{8,9},{9,8},{10,11... | collective-permute-start | bytes 430088 | tf_op jit(solution)/shard_map/ppermute | solution.py:427
  23.6 5.2 %collective-permute-start.5 = (bf16[560,128]{1,0:T(8,128)(2,1)S(1)}, bf16[560,128]{1,0:T(8,128)(2,1)S(1)}, u32[]{:S(2)}, u32[]{:S(2)}) collective-permute-start(bf16[560,128]{1,0:T(8,128)(2,1)S(1)} %add_convert_fusion.3), channel_id=1, source_target_pairs={{0,2},{1,5},{2,0},{3,7},{4,6},{5,1},{6,4},{7,3},{8,10},{9,13},{10,... | collective-permute-start | bytes 430088 | tf_op jit(solution)/shard_map/ppermute | solution.py:579
  28.8 6.6 %collective-permute-start.6 = (bf16[560,128]{1,0:T(8,128)(2,1)S(1)}, bf16[560,128]{1,0:T(8,128)(2,1)S(1)}, u32[]{:S(2)}, u32[]{:S(2)}) collective-permute-start(bf16[560,128]{1,0:T(8,128)(2,1)S(1)} %add_convert_fusion.2), channel_id=1, source_target_pairs={{0,4},{1,9},{2,6},{3,11},{4,0},{5,13},{6,2},{7,15},{8,12},{9,1},{1... | collective-permute-start | bytes 430088 | tf_op jit(solution)/shard_map/ppermute | solution.py:579
  28.9 6.6 %collective-permute-start.7 = (bf16[180,8,128]{2,1,0:T(8,128)(2,1)S(1)}, bf16[180,8,128]{2,1,0:T(8,128)(2,1)S(1)}, u32[]{:S(2)}, u32[]{:S(2)}) collective-permute-start(bf16[180,8,128]{2,1,0:T(8,128)(2,1)S(1)} %input_backward.1), channel_id=1, source_target_pairs={{0,1},{1,0},{2,3},{3,2},{4,5},{5,4},{6,7},{7,6},{8,9},{9,8},{10,11... | collective-permute-start | bytes 1105928 | tf_op jit(solution)/shard_map/ppermute | solution.py:427
  35.5 7.2 %collective-permute-start.9 = (bf16[560,128]{1,0:T(8,128)(2,1)S(1)}, bf16[560,128]{1,0:T(8,128)(2,1)S(1)}, u32[]{:S(2)}, u32[]{:S(2)}) collective-permute-start(bf16[560,128]{1,0:T(8,128)(2,1)S(1)} %add_convert_fusion.1), channel_id=1, source_target_pairs={{0,8},{1,3},{2,10},{3,1},{4,12},{5,7},{6,14},{7,5},{8,0},{9,11},{1... | collective-permute-start | bytes 430088 | tf_op jit(solution)/shard_map/ppermute | solution.py:579
  35.7 7.1 %collective-permute-start.8 = (bf16[180,4,128]{2,1,0:T(4,128)(2,1)S(1)}, bf16[180,4,128]{2,1,0:T(4,128)(2,1)S(1)}, u32[]{:S(2)}, u32[]{:S(2)}) collective-permute-start(bf16[180,4,128]{2,1,0:T(4,128)(2,1)S(1)} %get-tuple-element.96), channel_id=1, source_target_pairs={{0,14},{2,0},{4,2},{6,4},{8,6},{10,8},{12,10},{14,12},{1,15},{3,1}... | collective-permute-start | bytes 552968 | tf_op jit(solution)/shard_map/ppermute | solution.py:427
  42.8 1.4 %collective-permute-start.10 = (bf16[560,128]{1,0:T(8,128)(2,1)S(1)}, bf16[560,128]{1,0:T(8,128)(2,1)S(1)}, u32[]{:S(2)}, u32[]{:S(2)}) collective-permute-start(bf16[560,128]{1,0:T(8,128)(2,1)S(1)} %add_convert_fusion.mine_ref), channel_id=1, source_target_pairs={{0,1},{1,0},{2,3},{3,2},{4,5},{5,4},{6,7},{7,6},{8,9},{9,8},{10,11... | collective-permute-start | bytes 430088 | tf_op jit(solution)/shard_map/ppermute | solution.py:427

commit v7 on v6

--- a/solution.py
+++ b/solution.py
@@ -377,7 +377,21 @@
     framed_ref[...] = turn_s[...].astype(framed_ref.dtype)
 
 
-def finish_kernel(out_scale, mine_ref, other_ref, core_ref, weight_ref, gain_ref, offset_ref, d_weight_ref, d_bias_ref, d_proj_ref, d_table_ref, d_gain_ref, d_offset_ref):
+def finish_kernel(
+    out_scale,
+    mine_ref,
+    other_ref,
+    core_ref,
+    weight_ref,
+    gain_ref,
+    offset_ref,
+    d_weight_ref,
+    d_bias_ref,
+    d_proj_ref,
+    d_table_ref,
+    d_gain_ref,
+    d_offset_ref,
+):
     channels = weight_ref.shape[0]
     f32 = jnp.float32
     rest = channels - LANES
@@ -398,21 +412,24 @@
         )
     gain = gain_ref[...].T
     offset = offset_ref[...].T
-    d_gain = jnp.zeros((channels, 1), f32)
-    d_offset = jnp.zeros((channels, 1), f32)
+    ones = jnp.ones((8, channels), jnp.bfloat16)
+    products = jnp.zeros((channels, channels), f32)
+    d_offset = jnp.zeros((8, channels), f32)
     biases = []
     for part in range(3):
         across = slice(part * channels, (part + 1) * channels)
         unit = pieces[part][0:channels]
         bias = pieces[part][channels : channels + 1]
-        weight = weight_ref[:, across].astype(f32)
+        weight = weight_ref[:, across]
         d_weight_ref[:, across] = gain * unit + offset * bias
         biases.append(bias)
-        d_gain += jnp.sum(weight * unit, -1, keepdims=True)
-        d_offset += jnp.sum(weight * bias, -1, keepdims=True)
+        products += weight.astype(f32) * unit
+        for term in split_three(bias):
+            d_offset += nt(jnp.broadcast_to(term, (8, channels)), weight)
     d_bias_ref[...] = jnp.concatenate(biases, 1).reshape(d_bias_ref.shape)
-    d_gain_ref[...] = d_gain.T.reshape(channels)
-    d_offset_ref[...] = d_offset.T.reshape(channels)
+    d_gain = sum(nt(ones, term) for term in split_three(products))
+    d_gain_ref[...] = d_gain[0:1].reshape(channels)
+    d_offset_ref[...] = d_offset[0:1].reshape(channels)
     d_proj_ref[...] = pieces[3][0:channels]
     table = jnp.concatenate([both[6 * ROWS : 6 * ROWS + 8], both[6 * ROWS + 8 :]], 1)
     d_table_ref[...] = table[0:HEADS, 0 : d_table_ref.shape[1]]
@@ -440,7 +457,7 @@
     steps = [1 << bit for bit in range((rows - 1).bit_length())]
     for at in range(len(steps)):
         yield [
-            (r * cols + c, (r ^ steps[(at + c) % len(steps)]) * cols + c) for r in range(rows) for c in range(cols)
+            (r * cols + c, (r ^ steps[(at - c) % len(steps)]) * cols + c) for r in range(rows) for c in range(cols)
         ]
 
 
@@ -567,17 +584,12 @@
         compiler_params=params,
         cost_estimate=pl.CostEstimate(flops=10**9, bytes_accessed=0, transcendentals=0),
     )(*saved, gain, parts)
-    steps = list(exchange_steps())
-    for at, pairs in enumerate(steps):
-        if at == min(1, len(steps) - 1):
-            mine, framed = lax.optimization_barrier((mine, framed))
-            beside = from_behind(framed, "col", 1)
-            framed = jnp.where(jnp.arange(cols) < SHIFT, beside, framed)
-        if at == min(2, len(steps) - 1):
-            mine, framed = lax.optimization_barrier((mine, framed))
-            below = from_behind(framed[:, :SHIFT], "row", -1)
+    below = from_behind(framed[:, :SHIFT], "row", -1)
+    for pairs in exchange_steps():
         mine = add(mine, lax.ppermute(mine, ("row", "col"), pairs))
-    d_tokens = jnp.concatenate([framed[:, SHIFT:], below], 1).transpose(1, 2, 0)
+    framed = jnp.concatenate([framed[:, SHIFT:], below], 1)
+    beside = from_behind(framed, "col", 1)
+    d_tokens = jnp.where(jnp.arange(cols) < SHIFT, beside, framed).transpose(1, 2, 0)
     other = from_behind(mine, "col", 1)
 
     total_tokens = count * lax.axis_size("row") * lax.axis_size("col")

time: 46.9 us -> 44.8 us (0.955); the launches traced: 46.1 us -> 44.6 us
  waiting for transfers between devices: 19.5 us -> 15.9 us
  starting transfers between devices: 8.56 us -> 10.8 us
    ppermute x3, waiting for transfers between devices: 15.4 us -> 11.1 us  [on_device(): mine = add(mine, lax.ppermute(mine, ('row', 'col'), pairs))]
    ppermute x7, starting transfers between devices: 6.75 us -> 7.98 us  [from_behind(): lax.ppermute(shard, axis, [(i, (i + by) % count) for i in range(count)])]
    ppermute x3, starting transfers between devices: 0.21 us -> 1.23 us  [on_device(): mine = add(mine, lax.ppermute(mine, ('row', 'col'), pairs))]
    ppermute x7, waiting for transfers between devices: 3.33 us -> 4.09 us  [from_behind(): lax.ppermute(shard, axis, [(i, (i + by) % count) for i in range(count)])]
  transfers between devices with their start and end apart: 11 -> 11, of which waited for: 8 -> 9; matrix products, arithmetic and copies ran while one was open for 9% -> 10% of each run, Pallas kernels for 9% -> 9%
where the time goes in v7:
time: 44.8 us; the launch traced here: 44.6 us
  waiting for transfers between devices  15.9 us (35%)
  Pallas kernels  11.2 us (25%)
  starting transfers between devices  10.8 us (24%)
  local copies, waits for them, and re-layouts  4.24 us (9%)
  other arithmetic  1.53 us (3%)
  between operations  0.92 us (2%)
    ppermute x3, waiting for transfers between devices, on_device(): mine = add(mine, lax.ppermute(mine, ('row', 'col'), pairs))  11.1 us
    ppermute x7, starting transfers between devices, from_behind(): lax.ppermute(shard, axis, [(i, (i + by) % count) for i in range(count)])  7.98 us
    pallas_call x1, Pallas kernels, on_device(): pl.pallas_call(main_kernel, name='window_attention_backward', out_shape=(...  5.44 us
    ppermute x7, waiting for transfers between devices, from_behind(): lax.ppermute(shard, axis, [(i, (i + by) % count) for i in range(count)])  4.09 us
    pallas_call x1, Pallas kernels, on_device(): pl.pallas_call(project_kernel, name='project', out_shape=(jax.ShapeDtypeS...  1.75 us
    ppermute x1, starting transfers between devices, diagonal(): return lax.ppermute(shard, ('row', 'col'), pairs)  1.6 us
    pallas_call x1, Pallas kernels, on_device(): pl.pallas_call(functools.partial(finish_kernel, total_tokens ** (-0.5)),...  1.54 us
    optimization_barrier x2, local copies, waits for them, and re-layouts, on_device(): lax.optimization_barrier((g_turned[:, rows - SHIFT:], tokens, grad_out, r...  1.53 us
  transfers between devices with their start and end apart: 11, of which 9 were waited for; matrix products, arithmetic and copies ran while one was open for 10% of the time, Pallas kernels for 9%

profile of v7, /device:TPU:0, one launch (start us, length us, event | category | flops | bytes accessed | tf_op | source)
XLA Modules:
  0.0 44.6 jit_solution(232370739376925047)
XLA Ops:
  0.6 0.0 copy-start.5
  0.6 0.0 copy-start.2
  0.7 0.0 copy-start.7
  0.7 0.0 copy-start.6
  0.7 0.0 copy-start
  0.7 0.0 copy-start.1
  0.7 0.0 copy-start.3
  0.7 0.0 copy-start.4
  0.7 1.2 %slice.47 = bf16[180,4,128]{2,1,0:T(4,128)(2,1)S(1)} slice(bf16[180,8,128]{2,1,0:T(8,128)(2,1)} %bitcast.22), slice={[0:180], [4:8], [0:128]} | slice | bytes 368640 | tf_op jit(solution)/shard_map/slice | solution.py:480
  1.9 3.0 %collective-permute-start.3 = (bf16[180,4,128]{2,1,0:T(4,128)(2,1)S(1)}, bf16[180,4,128]{2,1,0:T(4,128)(2,1)S(1)}, u32[]{:S(2)}, u32[]{:S(2)}) collective-permute-start(bf16[180,4,128]{2,1,0:T(4,128)(2,1)S(1)} %slice.47), channel_id=1, source_target_pairs={{0,2},{2,4},{4,6},{6,8},{8,10},{10,12},{12,14},{14,0},{1,3},{3,5},... | collective-permute-start | bytes 552968 | tf_op jit(solution)/shard_map/ppermute | solution.py:444
  4.9 1.1 %slice.42 = bf16[180,4,128]{2,1,0:T(4,128)(2,1)S(1)} slice(bf16[180,8,128]{2,1,0:T(8,128)(2,1)} %bitcast.23), slice={[0:180], [4:8], [0:128]} | slice | bytes 368640 | tf_op jit(solution)/shard_map/slice | solution.py:482
  6.0 1.6 %collective-permute-start = (bf16[180,4,128]{2,1,0:T(4,128)(2,1)S(1)}, bf16[180,4,128]{2,1,0:T(4,128)(2,1)S(1)}, u32[]{:S(2)}, u32[]{:S(2)}) collective-permute-start(bf16[180,4,128]{2,1,0:T(4,128)(2,1)S(1)} %slice.42), channel_id=1, source_target_pairs={{0,2},{2,4},{4,6},{6,8},{8,10},{10,12},{12,14},{14,0},{1,3},{3,5},... | collective-permute-start | bytes 552968 | tf_op jit(solution)/shard_map/ppermute | solution.py:444
  7.6 1.2 %copy.16.tokens_ref = bf16[8,128,180]{2,1,0:T(8,128)(2,1)S(1)} copy(bf16[8,128,180]{1,0,2:T(8,128)(2,1)} %param.9) | data formatting | bytes 737280 | tf_op jit(solution)/shard_map/optimization_barrier | solution.py:481
  8.8 0.0 copy-done.5
  8.8 0.3 copy.23.grad_ref
  9.1 0.0 copy-done.2
  9.2 0.1 copy.18
  9.3 0.1 pad_maximum_fusion.1
  9.4 0.0 collective-permute-start.1
  9.4 0.1 copy.21
  9.6 0.1 pad_maximum_fusion.2
  9.6 1.6 %collective-permute-start.2 = (bf16[4,4,361]{2,1,0:T(4,128)(2,1)S(1)}, bf16[4,4,361]{2,1,0:T(4,128)(2,1)S(1)}, u32[]{:S(2)}, u32[]{:S(2)}) collective-permute-start(bf16[4,4,361]{2,1,0:T(4,128)(2,1)S(1)} %pad_maximum_fusion.2), channel_id=1, source_target_pairs={{0,3},{1,2},{2,5},{3,4},{4,7},{5,6},{6,9},{7,8},{8,11},{9,10},{10,... | collective-permute-start | bytes 34664 | tf_op jit(solution)/shard_map/ppermute | solution.py:452
  11.2 0.0 copy-done.7
  11.2 0.0 copy-done.6
  11.3 0.0 copy-done
  11.3 0.0 copy-done.1
  11.3 1.1 %prepare.1 = (f32[6,64,128]{2,1,0:T(8,128)S(1)}, bf16[3,256,192]{2,1,0:T(8,128)(2,1)S(1)}, bf16[3,192,256]{2,1,0:T(8,128)(2,1)S(1)}, bf16[192,180]{1,0:T(8,128)(2,1)S(1)}, bf16[3,180,180]{2,1,0:T(8,128)(2,1)S(1)}) custom-call(bf16[180,540]{1,0:T(8,128)(2,1)S(1)} %copy-done, f32[1,540]{1,0:T(1,128)S(1)} %broadcast_in_dim.24.offsets_ref, ...), custom_call_target="tpu_custom_call" | custom-call | flops 1000 | bytes 1000 | tf_op jit(solution)/shard_map/prepare/pallas_call | solution.py:501
  12.4 0.0 copy-done.3
  12.4 0.0 copy-done.4
  12.4 0.0 collective-permute-done.1.right_ref
  12.4 1.0 %collective-permute-done.3.x_above_ref = bf16[180,4,128]{2,1,0:T(4,128)(2,1)S(1)} collective-permute-done((bf16[180,4,128]{2,1,0:T(4,128)(2,1)S(1)}, bf16[180,4,128]{2,1,0:T(4,128)(2,1)S(1)}, u32[]{:S(2)}, u32[]{:S(2)}) %collective-permute-start.3) | collective-permute-done | bytes 184352 | tf_op jit(solution)/shard_map/ppermute | solution.py:444
  13.4 1.8 %project.1 = (f32[1024,256]{1,0:T(8,128)S(1)}, f32[1024,1]{1,0:T(8,128)S(1)}, bf16[192,1024]{1,0:T(8,128)(2,1)S(1)}, bf16[1024,180]{1,0:T(8,128)(2,1)S(1)}, bf16...) custom-call(bf16[8,128,180]{2,1,0:T(8,128)(2,1)S(1)} %copy.16.tokens, ...), custom_call_target="tpu_custom_call" | custom-call | flops 1000 | bytes 1000 | tf_op jit(solution)/shard_map/project/pallas_call | solution.py:520
  15.1 0.8 %collective-permute-done.2.corner_ref = bf16[4,4,361]{2,1,0:T(4,128)(2,1)S(1)} collective-permute-done((bf16[4,4,361]{2,1,0:T(4,128)(2,1)S(1)}, bf16[4,4,361]{2,1,0:T(4,128)(2,1)S(1)}, u32[]{:S(2)}, u32[]{:S(2)}) %collective-permute-start.2) | collective-permute-done | bytes 11584 | tf_op jit(solution)/shard_map/ppermute | solution.py:452
  15.9 0.7 %collective-permute-done.g_above_ref = bf16[180,4,128]{2,1,0:T(4,128)(2,1)S(1)} collective-permute-done((bf16[180,4,128]{2,1,0:T(4,128)(2,1)S(1)}, bf16[180,4,128]{2,1,0:T(4,128)(2,1)S(1)}, u32[]{:S(2)}, u32[]{:S(2)}) %collective-permute-start) | collective-permute-done | bytes 184352 | tf_op jit(solution)/shard_map/ppermute | solution.py:444
  16.6 5.4 %window_attention_backward.1 = (bf16[560,128]{1,0:T(8,128)(2,1)S(1)}, bf16[560,128]{1,0:T(8,128)(2,1)S(1)}, bf16[3,1024,180]{2,1,0:T(8,128)(2,1)S(1)}, f32[16,8,...) custom-call(bf16[8,128,180]{2,1,0:T(8,128)(2,1)S(1)} %copy.23.grad_ref, ...), custom_call_target="tpu_custom_call" | custom-call | tf_op jit(solution)/shard_map/window_attention_backward/pallas_call | solution.py:544
  22.1 0.2 collective-permute-start.4
  22.3 1.2 %collective-permute-done.4 = bf16[560,128]{1,0:T(8,128)(2,1)S(1)} collective-permute-done((bf16[560,128]{1,0:T(8,128)(2,1)S(1)}, bf16[560,128]{1,0:T(8,128)(2,1)S(1)}, u32[]{:S(2)}, u32[]{:S(2)}) %collective-permute-start.4) | collective-permute-done | bytes 143392 | tf_op jit(solution)/shard_map/ppermute | solution.py:444
  23.6 0.1 collective-permute-start.7
  23.6 1.3 %input_backward.1 = bf16[180,8,128]{2,1,0:T(8,128)(2,1)S(1)} custom-call(bf16[3,1024,180]{2,1,0:T(8,128)(2,1)S(1)} %get-tuple-element.69.d_qkv_ref, f32[16,8,8,180]{3,2,1,0:T(8,128)S(1)} %get-tuple-element.70.g_ref, f32[128,256]{1,0:T(8,128)S(1)} %get-tuple-element.71.unit_last_ref, f32[128,1]{1,0:T(8,128)S(1)} %get-tuple-element.72.inv_last_ref, ...), custom_call_target="tpu_custom_call" | custom-call | flops 1000000000 | tf_op jit(solution)/shard_map/input_backward/pallas_call | solution.py:577
  25.0 3.7 %collective-permute-done.7 = bf16[560,128]{1,0:T(8,128)(2,1)S(1)} collective-permute-done((bf16[560,128]{1,0:T(8,128)(2,1)S(1)}, bf16[560,128]{1,0:T(8,128)(2,1)S(1)}, u32[]{:S(2)}, u32[]{:S(2)}) %collective-permute-start.7) | collective-permute-done | bytes 143392 | tf_op jit(solution)/shard_map/ppermute | solution.py:589
  28.8 0.1 collective-permute-start.8
  28.9 0.1 fusion.2
  29.0 2.2 %collective-permute-start.5 = (bf16[180,4,128]{2,1,0:T(4,128)(2,1)S(1)}, bf16[180,4,128]{2,1,0:T(4,128)(2,1)S(1)}, u32[]{:S(2)}, u32[]{:S(2)}) collective-permute-start(bf16[180,4,128]{2,1,0:T(4,128)(2,1)S(1)} %get-tuple-element.88), channel_id=1, source_target_pairs={{0,14},{2,0},{4,2},{6,4},{8,6},{10,8},{12,10},{14,12},{1,15},{3,1}... | collective-permute-start | bytes 552968 | tf_op jit(solution)/shard_map/ppermute | solution.py:444
  31.2 3.3 %collective-permute-done.8 = bf16[560,128]{1,0:T(8,128)(2,1)S(1)} collective-permute-done((bf16[560,128]{1,0:T(8,128)(2,1)S(1)}, bf16[560,128]{1,0:T(8,128)(2,1)S(1)}, u32[]{:S(2)}, u32[]{:S(2)}) %collective-permute-start.8) | collective-permute-done | bytes 143392 | tf_op jit(solution)/shard_map/ppermute | solution.py:589
  34.6 1.1 %collective-permute-start.9 = (bf16[560,128]{1,0:T(8,128)(2,1)S(1)}, bf16[560,128]{1,0:T(8,128)(2,1)S(1)}, u32[]{:S(2)}, u32[]{:S(2)}) collective-permute-start(bf16[560,128]{1,0:T(8,128)(2,1)S(1)} %add_convert_fusion.1), channel_id=1, source_target_pairs={{0,8},{1,5},{2,10},{3,7},{4,12},{5,1},{6,14},{7,3},{8,0},{9,13},{1... | collective-permute-start | bytes 430088 | tf_op jit(solution)/shard_map/ppermute | solution.py:589
  35.7 0.8 %collective-permute-done.5 = bf16[180,4,128]{2,1,0:T(4,128)(2,1)S(1)} collective-permute-done((bf16[180,4,128]{2,1,0:T(4,128)(2,1)S(1)}, bf16[180,4,128]{2,1,0:T(4,128)(2,1)S(1)}, u32[]{:S(2)}, u32[]{:S(2)}) %collective-permute-start.5) | collective-permute-done | bytes 184352 | tf_op jit(solution)/shard_map/ppermute | solution.py:444
  36.5 0.2 pad_maximum_fusion
  36.7 0.9 %collective-permute-start.6 = (bf16[180,8,128]{2,1,0:T(8,128)(2,1)S(1)}, bf16[180,8,128]{2,1,0:T(8,128)(2,1)S(1)}, u32[]{:S(2)}, u32[]{:S(2)}) collective-permute-start(bf16[180,8,128]{2,1,0:T(8,128)(2,1)S(1)} %pad_maximum_fusion), channel_id=1, source_target_pairs={{0,1},{1,0},{2,3},{3,2},{4,5},{5,4},{6,7},{7,6},{8,9},{9,8},{10,11... | collective-permute-start | bytes 1105928 | tf_op jit(solution)/shard_map/ppermute | solution.py:444
  37.6 4.0 %collective-permute-done.9 = bf16[560,128]{1,0:T(8,128)(2,1)S(1)} collective-permute-done((bf16[560,128]{1,0:T(8,128)(2,1)S(1)}, bf16[560,128]{1,0:T(8,128)(2,1)S(1)}, u32[]{:S(2)}, u32[]{:S(2)}) %collective-permute-start.9) | collective-permute-done | bytes 143392 | tf_op jit(solution)/shard_map/ppermute | solution.py:589
  41.6 0.1 collective-permute-start.10
  41.7 0.0 collective-permute-done.6
  41.7 1.0 %select_bitcast_fusion = bf16[8,128,180]{1,0,2:T(8,128)(2,1)} fusion(bf16[180,8,128]{2,1,0:T(8,128)(2,1)S(1)} %collective-permute-done.6, pred[128]{0:T(512)(128)(4,1)S(1)} %iota_compare_fusion, bf16[180,4,128]{2,1,0:T(4,128)(2,1)S(1)} %collective-permute-done.5, bf16[180,4,128]{2,1,0:T(4,128)(2,1)S(1)} %get-tuple-element.87), kind=kLoop, calls=%fused_computation.1 | loop fusion | flops 921600 | bytes 1106048 | tf_op jit(solution)/shard_map/transpose | solution.py:592
  42.7 0.3 collective-permute-done.10.other_ref
  43.0 1.5 %finish.1 = (f32[180,540]{1,0:T(8,128)}, f32[540]{0:T(1024)}, f32[180,180]{1,0:T(8,128)}, f32[6,225]{1,0:T(8,128)}, f32[180]{0:T(256)}, /*index=5*/f32[180]{0:T(256)}) custom-call(bf16[560,128]{1,0:T(8,128)(2,1)S(1)} %add_convert_fusion.mine_ref, bf16[560,128]{1,0:T(8,128)(2,1)S(1)} %collective-permute-done.10.other_ref, s32[1]{0:T(128)} %bitcast.7.core_ref, ...), custom_call_target="tpu_custom_call" | custom-call | tf_op jit(solution)/shard_map/finish/pallas_call | solution.py:596
  (12 shorter events, 0.2 us)
Async XLA Ops:
  0.6 8.2 %copy-start.5 = (bf16[8,128,180]{1,0,2:T(8,128)(2,1)S(1)}, bf16[8,128,180]{1,0,2:T(8,128)(2,1)}, u32[]{:S(2)}) copy-start(bf16[8,128,180]{1,0,2:T(8,128)(2,1)} %param.10) | copy-start | bytes 1105924
  0.6 8.5 %copy-start.2 = (s32[8,128]{1,0:T(8,128)S(1)}, s32[8,128]{1,0:T(8,128)}, u32[]{:S(2)}) copy-start(s32[8,128]{1,0:T(8,128)} %region_ref) | copy-start | bytes 12292
  0.7 10.6 %copy-start.7 = (f32[540]{0:T(1024)S(1)}, f32[540]{0:T(1024)}, u32[]{:S(2)}) copy-start(f32[540]{0:T(1024)} %param.15) | copy-start | bytes 6484
  0.7 10.6 %copy-start.6 = (f32[225,6]{0,1:T(8,128)S(1)}, f32[225,6]{0,1:T(8,128)}, u32[]{:S(2)}) copy-start(f32[225,6]{0,1:T(8,128)} %param.17) | copy-start | bytes 16204
  0.7 10.6 %copy-start = (bf16[180,540]{1,0:T(8,128)(2,1)S(1)}, bf16[180,540]{1,0:T(8,128)(2,1)}, u32[]{:S(2)}) copy-start(bf16[180,540]{1,0:T(8,128)(2,1)} %weight_ref.3) | copy-start | bytes 583204
  0.7 10.6 %copy-start.1 = (bf16[180,180]{1,0:T(8,128)(2,1)S(1)}, bf16[180,180]{1,0:T(8,128)(2,1)}, u32[]{:S(2)}) copy-start(bf16[180,180]{1,0:T(8,128)(2,1)} %proj_ref.3) | copy-start | bytes 194404
  0.7 11.7 %copy-start.3 = (f32[180]{0:T(256)S(1)}, f32[180]{0:T(256)}, u32[]{:S(2)}) copy-start(f32[180]{0:T(256)} %param.12) | copy-start | bytes 2164
  0.7 11.7 %copy-start.4 = (f32[180]{0:T(256)S(1)}, f32[180]{0:T(256)}, u32[]{:S(2)}) copy-start(f32[180]{0:T(256)} %param.13) | copy-start | bytes 2164
  1.9 11.5 %collective-permute-start.3 = (bf16[180,4,128]{2,1,0:T(4,128)(2,1)S(1)}, bf16[180,4,128]{2,1,0:T(4,128)(2,1)S(1)}, u32[]{:S(2)}, u32[]{:S(2)}) collective-permute-start(bf16[180,4,128]{2,1,0:T(4,128)(2,1)S(1)} %slice.47), channel_id=1, source_target_pairs={{0,2},{2,4},{4,6},{6,8},{8,10},{10,12},{12,14},{14,0},{1,3},{3,5},... | collective-permute-start | bytes 552968 | tf_op jit(solution)/shard_map/ppermute | solution.py:444
  6.0 10.7 %collective-permute-start = (bf16[180,4,128]{2,1,0:T(4,128)(2,1)S(1)}, bf16[180,4,128]{2,1,0:T(4,128)(2,1)S(1)}, u32[]{:S(2)}, u32[]{:S(2)}) collective-permute-start(bf16[180,4,128]{2,1,0:T(4,128)(2,1)S(1)} %slice.42), channel_id=1, source_target_pairs={{0,2},{2,4},{4,6},{6,8},{8,10},{10,12},{12,14},{14,0},{1,3},{3,5},... | collective-permute-start | bytes 552968 | tf_op jit(solution)/shard_map/ppermute | solution.py:444
  9.4 3.0 %collective-permute-start.1 = (bf16[4,4,361]{2,1,0:T(4,128)(2,1)S(1)}, bf16[4,4,361]{2,1,0:T(4,128)(2,1)S(1)}, u32[]{:S(2)}, u32[]{:S(2)}) collective-permute-start(bf16[4,4,361]{2,1,0:T(4,128)(2,1)S(1)} %pad_maximum_fusion.1), channel_id=1, source_target_pairs={{0,1},{1,0},{2,3},{3,2},{4,5},{5,4},{6,7},{7,6},{8,9},{9,8},{10,11... | collective-permute-start | bytes 34664 | tf_op jit(solution)/shard_map/ppermute | solution.py:444
  9.6 6.3 %collective-permute-start.2 = (bf16[4,4,361]{2,1,0:T(4,128)(2,1)S(1)}, bf16[4,4,361]{2,1,0:T(4,128)(2,1)S(1)}, u32[]{:S(2)}, u32[]{:S(2)}) collective-permute-start(bf16[4,4,361]{2,1,0:T(4,128)(2,1)S(1)} %pad_maximum_fusion.2), channel_id=1, source_target_pairs={{0,3},{1,2},{2,5},{3,4},{4,7},{5,6},{6,9},{7,8},{8,11},{9,10},{10,... | collective-permute-start | bytes 34664 | tf_op jit(solution)/shard_map/ppermute | solution.py:452
  22.1 1.4 %collective-permute-start.4 = (bf16[560,128]{1,0:T(8,128)(2,1)S(1)}, bf16[560,128]{1,0:T(8,128)(2,1)S(1)}, u32[]{:S(2)}, u32[]{:S(2)}) collective-permute-start(bf16[560,128]{1,0:T(8,128)(2,1)S(1)} %get-tuple-element.62), channel_id=1, source_target_pairs={{0,1},{1,0},{2,3},{3,2},{4,5},{5,4},{6,7},{7,6},{8,9},{9,8},{10,11... | collective-permute-start | bytes 430088 | tf_op jit(solution)/shard_map/ppermute | solution.py:444
  23.6 5.2 %collective-permute-start.7 = (bf16[560,128]{1,0:T(8,128)(2,1)S(1)}, bf16[560,128]{1,0:T(8,128)(2,1)S(1)}, u32[]{:S(2)}, u32[]{:S(2)}) collective-permute-start(bf16[560,128]{1,0:T(8,128)(2,1)S(1)} %add_convert_fusion.3), channel_id=1, source_target_pairs={{0,2},{1,9},{2,0},{3,11},{4,6},{5,13},{6,4},{7,15},{8,10},{9,1},{1... | collective-permute-start | bytes 430088 | tf_op jit(solution)/shard_map/ppermute | solution.py:589
  28.8 5.8 %collective-permute-start.8 = (bf16[560,128]{1,0:T(8,128)(2,1)S(1)}, bf16[560,128]{1,0:T(8,128)(2,1)S(1)}, u32[]{:S(2)}, u32[]{:S(2)}) collective-permute-start(bf16[560,128]{1,0:T(8,128)(2,1)S(1)} %add_convert_fusion.2), channel_id=1, source_target_pairs={{0,4},{1,3},{2,6},{3,1},{4,0},{5,7},{6,2},{7,5},{8,12},{9,11},{10,... | collective-permute-start | bytes 430088 | tf_op jit(solution)/shard_map/ppermute | solution.py:589
  29.0 7.5 %collective-permute-start.5 = (bf16[180,4,128]{2,1,0:T(4,128)(2,1)S(1)}, bf16[180,4,128]{2,1,0:T(4,128)(2,1)S(1)}, u32[]{:S(2)}, u32[]{:S(2)}) collective-permute-start(bf16[180,4,128]{2,1,0:T(4,128)(2,1)S(1)} %get-tuple-element.88), channel_id=1, source_target_pairs={{0,14},{2,0},{4,2},{6,4},{8,6},{10,8},{12,10},{14,12},{1,15},{3,1}... | collective-permute-start | bytes 552968 | tf_op jit(solution)/shard_map/ppermute | solution.py:444
  34.6 7.0 %collective-permute-start.9 = (bf16[560,128]{1,0:T(8,128)(2,1)S(1)}, bf16[560,128]{1,0:T(8,128)(2,1)S(1)}, u32[]{:S(2)}, u32[]{:S(2)}) collective-permute-start(bf16[560,128]{1,0:T(8,128)(2,1)S(1)} %add_convert_fusion.1), channel_id=1, source_target_pairs={{0,8},{1,5},{2,10},{3,7},{4,12},{5,1},{6,14},{7,3},{8,0},{9,13},{1... | collective-permute-start | bytes 430088 | tf_op jit(solution)/shard_map/ppermute | solution.py:589
  36.7 5.0 %collective-permute-start.6 = (bf16[180,8,128]{2,1,0:T(8,128)(2,1)S(1)}, bf16[180,8,128]{2,1,0:T(8,128)(2,1)S(1)}, u32[]{:S(2)}, u32[]{:S(2)}) collective-permute-start(bf16[180,8,128]{2,1,0:T(8,128)(2,1)S(1)} %pad_maximum_fusion), channel_id=1, source_target_pairs={{0,1},{1,0},{2,3},{3,2},{4,5},{5,4},{6,7},{7,6},{8,9},{9,8},{10,11... | collective-permute-start | bytes 1105928 | tf_op jit(solution)/shard_map/ppermute | solution.py:444
  41.6 1.4 %collective-permute-start.10 = (bf16[560,128]{1,0:T(8,128)(2,1)S(1)}, bf16[560,128]{1,0:T(8,128)(2,1)S(1)}, u32[]{:S(2)}, u32[]{:S(2)}) collective-permute-start(bf16[560,128]{1,0:T(8,128)(2,1)S(1)} %add_convert_fusion.mine_ref), channel_id=1, source_target_pairs={{0,1},{1,0},{2,3},{3,2},{4,5},{5,4},{6,7},{7,6},{8,9},{9,8},{10,11... | collective-permute-start | bytes 430088 | tf_op jit(solution)/shard_map/ppermute | solution.py:444

commit v8 on v7

--- a/solution.py
+++ b/solution.py
@@ -410,8 +410,8 @@
                 [both[at * ROWS : (at + 1) * ROWS, :], both[row : row + ROWS, side : side + rest]], 1
             )
         )
-    gain = gain_ref[...].T
-    offset = offset_ref[...].T
+    gain = gain_ref[...]
+    offset = offset_ref[...]
     ones = jnp.ones((8, channels), jnp.bfloat16)
     products = jnp.zeros((channels, channels), f32)
     d_offset = jnp.zeros((8, channels), f32)
@@ -457,7 +457,7 @@
     steps = [1 << bit for bit in range((rows - 1).bit_length())]
     for at in range(len(steps)):
         yield [
-            (r * cols + c, (r ^ steps[(at - c) % len(steps)]) * cols + c) for r in range(rows) for c in range(cols)
+            (r * cols + c, (r ^ steps[(at - 1 - c) % len(steps)]) * cols + c) for r in range(rows) for c in range(cols)
         ]
 
 
@@ -607,7 +607,7 @@
         in_specs=[whole(), whole(), whole(pltpu.SMEM), whole(), whole(), whole()],
         out_specs=(whole(),) * 6,
         compiler_params=params,
-    )(mine, other, core, qkv_weight, ln_gain[None], ln_offset[None])
+    )(mine, other, core, qkv_weight, ln_gain[:, None], ln_offset[:, None])
     return (d_tokens, d_weight, d_bias, d_proj, d_table.T, d_gain, d_offset)
 
 

time: 44.8 us -> 44.3 us (0.989)
  waiting for transfers between devices: 15.9 us -> 14.8 us
  starting transfers between devices: 10.8 us -> 11.3 us
    ppermute x3, waiting for transfers between devices: 11.1 us -> 8.24 us  [on_device(): mine = add(mine, lax.ppermute(mine, ('row', 'col'), pairs))]
    ppermute x7, waiting for transfers between devices: 4.09 us -> 5.71 us  [from_behind(): lax.ppermute(shard, axis, [(i, (i + by) % count) for i in range(count)])]
    ppermute x7, starting transfers between devices: 7.98 us -> 8.59 us  [from_behind(): lax.ppermute(shard, axis, [(i, (i + by) % count) for i in range(count)])]
  transfers between devices with their start and end apart: 11 -> 11, of which waited for: 9 -> 9; matrix products, arithmetic and copies ran while one was open for 10% -> 11% of each run, Pallas kernels for 9% -> 9%
where the time goes in v8:
time: 44.3 us; the launch traced here: 44 us
  waiting for transfers between devices  14.8 us (33%)
  starting transfers between devices  11.3 us (26%)
  Pallas kernels  11 us (25%)
  local copies, waits for them, and re-layouts  4.47 us (10%)
  other arithmetic  1.53 us (3%)
  between operations  0.94 us (2%)
    ppermute x7, starting transfers between devices, from_behind(): lax.ppermute(shard, axis, [(i, (i + by) % count) for i in range(count)])  8.59 us
    ppermute x3, waiting for transfers between devices, on_device(): mine = add(mine, lax.ppermute(mine, ('row', 'col'), pairs))  8.24 us
    ppermute x7, waiting for transfers between devices, from_behind(): lax.ppermute(shard, axis, [(i, (i + by) % count) for i in range(count)])  5.71 us
    pallas_call x1, Pallas kernels, on_device(): pl.pallas_call(main_kernel, name='window_attention_backward', out_shape=(...  5.44 us
    pallas_call x1, Pallas kernels, on_device(): pl.pallas_call(project_kernel, name='project', out_shape=(jax.ShapeDtypeS...  1.75 us
    ppermute x1, starting transfers between devices, diagonal(): return lax.ppermute(shard, ('row', 'col'), pairs)  1.6 us
    optimization_barrier x2, local copies, waits for them, and re-layouts, on_device(): lax.optimization_barrier((g_turned[:, rows - SHIFT:], tokens, grad_out, r...  1.53 us
    pallas_call x1, Pallas kernels, on_device(): pl.pallas_call(functools.partial(finish_kernel, total_tokens ** (-0.5)),...  1.44 us
  transfers between devices with their start and end apart: 11, of which 9 were waited for; matrix products, arithmetic and copies ran while one was open for 11% of the time, Pallas kernels for 9%

profile of v8, /device:TPU:0, one launch (start us, length us, event | category | flops | bytes accessed | tf_op | source)
XLA Modules:
  0.0 44.0 jit_solution(11106530462388949455)
XLA Ops:
  0.6 0.0 copy-start.3
  0.6 0.0 copy-start.2
  0.7 0.0 copy-start.7
  0.7 0.0 copy-start.4
  0.7 0.0 copy-start
  0.7 0.0 copy-start.1
  0.7 0.0 copy-start.5
  0.7 0.0 copy-start.6
  0.7 1.2 %slice.47 = bf16[180,4,128]{2,1,0:T(4,128)(2,1)S(1)} slice(bf16[180,8,128]{2,1,0:T(8,128)(2,1)} %bitcast.20), slice={[0:180], [4:8], [0:128]} | slice | bytes 368640 | tf_op jit(solution)/shard_map/slice | solution.py:480
  1.9 3.0 %collective-permute-start.3 = (bf16[180,4,128]{2,1,0:T(4,128)(2,1)S(1)}, bf16[180,4,128]{2,1,0:T(4,128)(2,1)S(1)}, u32[]{:S(2)}, u32[]{:S(2)}) collective-permute-start(bf16[180,4,128]{2,1,0:T(4,128)(2,1)S(1)} %slice.47), channel_id=1, source_target_pairs={{0,2},{2,4},{4,6},{6,8},{8,10},{10,12},{12,14},{14,0},{1,3},{3,5},... | collective-permute-start | bytes 552968 | tf_op jit(solution)/shard_map/ppermute | solution.py:444
  4.9 1.1 %slice.42 = bf16[180,4,128]{2,1,0:T(4,128)(2,1)S(1)} slice(bf16[180,8,128]{2,1,0:T(8,128)(2,1)} %bitcast.21), slice={[0:180], [4:8], [0:128]} | slice | bytes 368640 | tf_op jit(solution)/shard_map/slice | solution.py:482
  6.0 1.6 %collective-permute-start = (bf16[180,4,128]{2,1,0:T(4,128)(2,1)S(1)}, bf16[180,4,128]{2,1,0:T(4,128)(2,1)S(1)}, u32[]{:S(2)}, u32[]{:S(2)}) collective-permute-start(bf16[180,4,128]{2,1,0:T(4,128)(2,1)S(1)} %slice.42), channel_id=1, source_target_pairs={{0,2},{2,4},{4,6},{6,8},{8,10},{10,12},{12,14},{14,0},{1,3},{3,5},... | collective-permute-start | bytes 552968 | tf_op jit(solution)/shard_map/ppermute | solution.py:444
  7.6 1.2 %copy.24.tokens_ref = bf16[8,128,180]{2,1,0:T(8,128)(2,1)S(1)} copy(bf16[8,128,180]{1,0,2:T(8,128)(2,1)} %param.9) | data formatting | bytes 737280 | tf_op jit(solution)/shard_map/optimization_barrier | solution.py:481
  8.8 0.0 copy-done.3
  8.8 0.3 copy.31.grad_ref
  9.1 0.0 copy-done.2
  9.2 0.1 copy.26
  9.3 0.1 pad_maximum_fusion.1
  9.4 0.0 collective-permute-start.1
  9.4 0.1 copy.29
  9.6 0.1 pad_maximum_fusion.2
  9.6 1.6 %collective-permute-start.2 = (bf16[4,4,361]{2,1,0:T(4,128)(2,1)S(1)}, bf16[4,4,361]{2,1,0:T(4,128)(2,1)S(1)}, u32[]{:S(2)}, u32[]{:S(2)}) collective-permute-start(bf16[4,4,361]{2,1,0:T(4,128)(2,1)S(1)} %pad_maximum_fusion.2), channel_id=1, source_target_pairs={{0,3},{1,2},{2,5},{3,4},{4,7},{5,6},{6,9},{7,8},{8,11},{9,10},{10,... | collective-permute-start | bytes 34664 | tf_op jit(solution)/shard_map/ppermute | solution.py:452
  11.2 0.0 copy-done.7
  11.2 0.0 copy-done.4
  11.3 0.0 copy-done
  11.3 0.0 copy-done.1
  11.3 1.1 %prepare.1 = (f32[6,64,128]{2,1,0:T(8,128)S(1)}, bf16[3,256,192]{2,1,0:T(8,128)(2,1)S(1)}, bf16[3,192,256]{2,1,0:T(8,128)(2,1)S(1)}, bf16[192,180]{1,0:T(8,128)(2,1)S(1)}, bf16[3,180,180]{2,1,0:T(8,128)(2,1)S(1)}) custom-call(bf16[180,540]{1,0:T(8,128)(2,1)S(1)} %copy-done, f32[1,540]{1,0:T(1,128)S(1)} %broadcast_in_dim.24.offsets_ref, ...), custom_call_target="tpu_custom_call" | custom-call | flops 1000 | bytes 1000 | tf_op jit(solution)/shard_map/prepare/pallas_call | solution.py:501
  12.4 0.0 copy-done.5
  12.4 0.0 copy-done.6
  12.4 0.0 collective-permute-done.1.right_ref
  12.4 1.0 %collective-permute-done.3.x_above_ref = bf16[180,4,128]{2,1,0:T(4,128)(2,1)S(1)} collective-permute-done((bf16[180,4,128]{2,1,0:T(4,128)(2,1)S(1)}, bf16[180,4,128]{2,1,0:T(4,128)(2,1)S(1)}, u32[]{:S(2)}, u32[]{:S(2)}) %collective-permute-start.3) | collective-permute-done | bytes 184352 | tf_op jit(solution)/shard_map/ppermute | solution.py:444
  13.4 1.8 %project.1 = (f32[1024,256]{1,0:T(8,128)S(1)}, f32[1024,1]{1,0:T(8,128)S(1)}, bf16[192,1024]{1,0:T(8,128)(2,1)S(1)}, bf16[1024,180]{1,0:T(8,128)(2,1)S(1)}, bf16...) custom-call(bf16[8,128,180]{2,1,0:T(8,128)(2,1)S(1)} %copy.24.tokens, ...), custom_call_target="tpu_custom_call" | custom-call | flops 1000 | bytes 1000 | tf_op jit(solution)/shard_map/project/pallas_call | solution.py:520
  15.1 0.8 %collective-permute-done.2.corner_ref = bf16[4,4,361]{2,1,0:T(4,128)(2,1)S(1)} collective-permute-done((bf16[4,4,361]{2,1,0:T(4,128)(2,1)S(1)}, bf16[4,4,361]{2,1,0:T(4,128)(2,1)S(1)}, u32[]{:S(2)}, u32[]{:S(2)}) %collective-permute-start.2) | collective-permute-done | bytes 11584 | tf_op jit(solution)/shard_map/ppermute | solution.py:452
  15.9 0.7 %collective-permute-done.g_above_ref = bf16[180,4,128]{2,1,0:T(4,128)(2,1)S(1)} collective-permute-done((bf16[180,4,128]{2,1,0:T(4,128)(2,1)S(1)}, bf16[180,4,128]{2,1,0:T(4,128)(2,1)S(1)}, u32[]{:S(2)}, u32[]{:S(2)}) %collective-permute-start) | collective-permute-done | bytes 184352 | tf_op jit(solution)/shard_map/ppermute | solution.py:444
  16.6 5.4 %window_attention_backward.1 = (bf16[560,128]{1,0:T(8,128)(2,1)S(1)}, bf16[560,128]{1,0:T(8,128)(2,1)S(1)}, bf16[3,1024,180]{2,1,0:T(8,128)(2,1)S(1)}, f32[16,8,...) custom-call(bf16[8,128,180]{2,1,0:T(8,128)(2,1)S(1)} %copy.31.grad_ref, ...), custom_call_target="tpu_custom_call" | custom-call | tf_op jit(solution)/shard_map/window_attention_backward/pallas_call | solution.py:544
  22.1 0.2 collective-permute-start.4
  22.3 1.2 %collective-permute-done.4 = bf16[560,128]{1,0:T(8,128)(2,1)S(1)} collective-permute-done((bf16[560,128]{1,0:T(8,128)(2,1)S(1)}, bf16[560,128]{1,0:T(8,128)(2,1)S(1)}, u32[]{:S(2)}, u32[]{:S(2)}) %collective-permute-start.4) | collective-permute-done | bytes 143392 | tf_op jit(solution)/shard_map/ppermute | solution.py:444
  23.6 0.8 %collective-permute-start.7 = (bf16[560,128]{1,0:T(8,128)(2,1)S(1)}, bf16[560,128]{1,0:T(8,128)(2,1)S(1)}, u32[]{:S(2)}, u32[]{:S(2)}) collective-permute-start(bf16[560,128]{1,0:T(8,128)(2,1)S(1)} %add_convert_fusion.3), channel_id=1, source_target_pairs={{0,8},{1,5},{2,10},{3,7},{4,12},{5,1},{6,14},{7,3},{8,0},{9,13},{1... | collective-permute-start | bytes 430088 | tf_op jit(solution)/shard_map/ppermute | solution.py:589
  24.3 1.3 %input_backward.1 = bf16[180,8,128]{2,1,0:T(8,128)(2,1)S(1)} custom-call(bf16[3,1024,180]{2,1,0:T(8,128)(2,1)S(1)} %get-tuple-element.69.d_qkv_ref, f32[16,8,8,180]{3,2,1,0:T(8,128)S(1)} %get-tuple-element.70.g_ref, f32[128,256]{1,0:T(8,128)S(1)} %get-tuple-element.71.unit_last_ref, f32[128,1]{1,0:T(8,128)S(1)} %get-tuple-element.72.inv_last_ref, ...), custom_call_target="tpu_custom_call" | custom-call | flops 1000000000 | tf_op jit(solution)/shard_map/input_backward/pallas_call | solution.py:577
  25.7 5.0 %collective-permute-done.7 = bf16[560,128]{1,0:T(8,128)(2,1)S(1)} collective-permute-done((bf16[560,128]{1,0:T(8,128)(2,1)S(1)}, bf16[560,128]{1,0:T(8,128)(2,1)S(1)}, u32[]{:S(2)}, u32[]{:S(2)}) %collective-permute-start.7) | collective-permute-done | bytes 143392 | tf_op jit(solution)/shard_map/ppermute | solution.py:589
  30.7 0.1 collective-permute-start.8
  30.8 0.1 fusion.2
  31.0 3.6 %collective-permute-start.5 = (bf16[180,4,128]{2,1,0:T(4,128)(2,1)S(1)}, bf16[180,4,128]{2,1,0:T(4,128)(2,1)S(1)}, u32[]{:S(2)}, u32[]{:S(2)}) collective-permute-start(bf16[180,4,128]{2,1,0:T(4,128)(2,1)S(1)} %get-tuple-element.88), channel_id=1, source_target_pairs={{0,14},{2,0},{4,2},{6,4},{8,6},{10,8},{12,10},{14,12},{1,15},{3,1}... | collective-permute-start | bytes 552968 | tf_op jit(solution)/shard_map/ppermute | solution.py:444
  34.6 1.3 %collective-permute-done.8 = bf16[560,128]{1,0:T(8,128)(2,1)S(1)} collective-permute-done((bf16[560,128]{1,0:T(8,128)(2,1)S(1)}, bf16[560,128]{1,0:T(8,128)(2,1)S(1)}, u32[]{:S(2)}, u32[]{:S(2)}) %collective-permute-start.8) | collective-permute-done | bytes 143392 | tf_op jit(solution)/shard_map/ppermute | solution.py:589
  36.0 0.3 collective-permute-start.9
  36.2 2.4 %collective-permute-done.5 = bf16[180,4,128]{2,1,0:T(4,128)(2,1)S(1)} collective-permute-done((bf16[180,4,128]{2,1,0:T(4,128)(2,1)S(1)}, bf16[180,4,128]{2,1,0:T(4,128)(2,1)S(1)}, u32[]{:S(2)}, u32[]{:S(2)}) %collective-permute-start.5) | collective-permute-done | bytes 184352 | tf_op jit(solution)/shard_map/ppermute | solution.py:444
  38.7 0.2 pad_maximum_fusion
  38.9 0.1 collective-permute-start.6
  39.0 0.1 copy.32.gain_ref
  39.1 0.1 copy.33.offset_ref
  39.2 1.9 %collective-permute-done.9 = bf16[560,128]{1,0:T(8,128)(2,1)S(1)} collective-permute-done((bf16[560,128]{1,0:T(8,128)(2,1)S(1)}, bf16[560,128]{1,0:T(8,128)(2,1)S(1)}, u32[]{:S(2)}, u32[]{:S(2)}) %collective-permute-start.9) | collective-permute-done | bytes 143392 | tf_op jit(solution)/shard_map/ppermute | solution.py:589
  41.2 0.1 collective-permute-start.10
  41.2 0.0 collective-permute-done.6
  41.3 1.0 %select_bitcast_fusion = bf16[8,128,180]{1,0,2:T(8,128)(2,1)} fusion(bf16[180,8,128]{2,1,0:T(8,128)(2,1)S(1)} %collective-permute-done.6, pred[128]{0:T(512)(128)(4,1)S(1)} %iota_compare_fusion, bf16[180,4,128]{2,1,0:T(4,128)(2,1)S(1)} %collective-permute-done.5, bf16[180,4,128]{2,1,0:T(4,128)(2,1)S(1)} %get-tuple-element.87), kind=kLoop, calls=%fused_computation.1 | loop fusion | flops 921600 | bytes 1106048 | tf_op jit(solution)/shard_map/transpose | solution.py:592
  42.3 0.3 collective-permute-done.10.other_ref
  42.6 1.4 %finish.1 = (f32[180,540]{1,0:T(8,128)}, f32[540]{0:T(1024)}, f32[180,180]{1,0:T(8,128)}, f32[6,225]{1,0:T(8,128)}, f32[180]{0:T(256)}, /*index=5*/f32[180]{0:T(256)}) custom-call(bf16[560,128]{1,0:T(8,128)(2,1)S(1)} %add_convert_fusion.mine_ref, bf16[560,128]{1,0:T(8,128)(2,1)S(1)} %collective-permute-done.10.other_ref, s32[1]{0:T(128)} %bitcast.7.core_ref, ...), custom_call_target="tpu_custom_call" | custom-call | tf_op jit(solution)/shard_map/finish/pallas_call | solution.py:596
  (12 shorter events, 0.2 us)
Async XLA Ops:
  0.6 8.2 %copy-start.3 = (bf16[8,128,180]{1,0,2:T(8,128)(2,1)S(1)}, bf16[8,128,180]{1,0,2:T(8,128)(2,1)}, u32[]{:S(2)}) copy-start(bf16[8,128,180]{1,0,2:T(8,128)(2,1)} %param.10) | copy-start | bytes 1105924
  0.6 8.5 %copy-start.2 = (s32[8,128]{1,0:T(8,128)S(1)}, s32[8,128]{1,0:T(8,128)}, u32[]{:S(2)}) copy-start(s32[8,128]{1,0:T(8,128)} %region_ref) | copy-start | bytes 12292
  0.7 10.6 %copy-start.7 = (f32[540]{0:T(1024)S(1)}, f32[540]{0:T(1024)}, u32[]{:S(2)}) copy-start(f32[540]{0:T(1024)} %param.15) | copy-start | bytes 6484
  0.7 10.6 %copy-start.4 = (f32[225,6]{0,1:T(8,128)S(1)}, f32[225,6]{0,1:T(8,128)}, u32[]{:S(2)}) copy-start(f32[225,6]{0,1:T(8,128)} %param.17) | copy-start | bytes 16204
  0.7 10.6 %copy-start = (bf16[180,540]{1,0:T(8,128)(2,1)S(1)}, bf16[180,540]{1,0:T(8,128)(2,1)}, u32[]{:S(2)}) copy-start(bf16[180,540]{1,0:T(8,128)(2,1)} %weight_ref.3) | copy-start | bytes 583204
  0.7 10.6 %copy-start.1 = (bf16[180,180]{1,0:T(8,128)(2,1)S(1)}, bf16[180,180]{1,0:T(8,128)(2,1)}, u32[]{:S(2)}) copy-start(bf16[180,180]{1,0:T(8,128)(2,1)} %proj_ref.3) | copy-start | bytes 194404
  0.7 11.7 %copy-start.5 = (f32[180]{0:T(256)S(1)}, f32[180]{0:T(256)}, u32[]{:S(2)}) copy-start(f32[180]{0:T(256)} %param.12) | copy-start | bytes 2164
  0.7 11.7 %copy-start.6 = (f32[180]{0:T(256)S(1)}, f32[180]{0:T(256)}, u32[]{:S(2)}) copy-start(f32[180]{0:T(256)} %param.13) | copy-start | bytes 2164
  1.9 11.5 %collective-permute-start.3 = (bf16[180,4,128]{2,1,0:T(4,128)(2,1)S(1)}, bf16[180,4,128]{2,1,0:T(4,128)(2,1)S(1)}, u32[]{:S(2)}, u32[]{:S(2)}) collective-permute-start(bf16[180,4,128]{2,1,0:T(4,128)(2,1)S(1)} %slice.47), channel_id=1, source_target_pairs={{0,2},{2,4},{4,6},{6,8},{8,10},{10,12},{12,14},{14,0},{1,3},{3,5},... | collective-permute-start | bytes 552968 | tf_op jit(solution)/shard_map/ppermute | solution.py:444
  6.0 10.7 %collective-permute-start = (bf16[180,4,128]{2,1,0:T(4,128)(2,1)S(1)}, bf16[180,4,128]{2,1,0:T(4,128)(2,1)S(1)}, u32[]{:S(2)}, u32[]{:S(2)}) collective-permute-start(bf16[180,4,128]{2,1,0:T(4,128)(2,1)S(1)} %slice.42), channel_id=1, source_target_pairs={{0,2},{2,4},{4,6},{6,8},{8,10},{10,12},{12,14},{14,0},{1,3},{3,5},... | collective-permute-start | bytes 552968 | tf_op jit(solution)/shard_map/ppermute | solution.py:444
  9.4 3.0 %collective-permute-start.1 = (bf16[4,4,361]{2,1,0:T(4,128)(2,1)S(1)}, bf16[4,4,361]{2,1,0:T(4,128)(2,1)S(1)}, u32[]{:S(2)}, u32[]{:S(2)}) collective-permute-start(bf16[4,4,361]{2,1,0:T(4,128)(2,1)S(1)} %pad_maximum_fusion.1), channel_id=1, source_target_pairs={{0,1},{1,0},{2,3},{3,2},{4,5},{5,4},{6,7},{7,6},{8,9},{9,8},{10,11... | collective-permute-start | bytes 34664 | tf_op jit(solution)/shard_map/ppermute | solution.py:444
  9.6 6.3 %collective-permute-start.2 = (bf16[4,4,361]{2,1,0:T(4,128)(2,1)S(1)}, bf16[4,4,361]{2,1,0:T(4,128)(2,1)S(1)}, u32[]{:S(2)}, u32[]{:S(2)}) collective-permute-start(bf16[4,4,361]{2,1,0:T(4,128)(2,1)S(1)} %pad_maximum_fusion.2), channel_id=1, source_target_pairs={{0,3},{1,2},{2,5},{3,4},{4,7},{5,6},{6,9},{7,8},{8,11},{9,10},{10,... | collective-permute-start | bytes 34664 | tf_op jit(solution)/shard_map/ppermute | solution.py:452
  22.1 1.4 %collective-permute-start.4 = (bf16[560,128]{1,0:T(8,128)(2,1)S(1)}, bf16[560,128]{1,0:T(8,128)(2,1)S(1)}, u32[]{:S(2)}, u32[]{:S(2)}) collective-permute-start(bf16[560,128]{1,0:T(8,128)(2,1)S(1)} %get-tuple-element.62), channel_id=1, source_target_pairs={{0,1},{1,0},{2,3},{3,2},{4,5},{5,4},{6,7},{7,6},{8,9},{9,8},{10,11... | collective-permute-start | bytes 430088 | tf_op jit(solution)/shard_map/ppermute | solution.py:444
  23.6 7.1 %collective-permute-start.7 = (bf16[560,128]{1,0:T(8,128)(2,1)S(1)}, bf16[560,128]{1,0:T(8,128)(2,1)S(1)}, u32[]{:S(2)}, u32[]{:S(2)}) collective-permute-start(bf16[560,128]{1,0:T(8,128)(2,1)S(1)} %add_convert_fusion.3), channel_id=1, source_target_pairs={{0,8},{1,5},{2,10},{3,7},{4,12},{5,1},{6,14},{7,3},{8,0},{9,13},{1... | collective-permute-start | bytes 430088 | tf_op jit(solution)/shard_map/ppermute | solution.py:589
  30.7 5.2 %collective-permute-start.8 = (bf16[560,128]{1,0:T(8,128)(2,1)S(1)}, bf16[560,128]{1,0:T(8,128)(2,1)S(1)}, u32[]{:S(2)}, u32[]{:S(2)}) collective-permute-start(bf16[560,128]{1,0:T(8,128)(2,1)S(1)} %add_convert_fusion.2), channel_id=1, source_target_pairs={{0,2},{1,9},{2,0},{3,11},{4,6},{5,13},{6,4},{7,15},{8,10},{9,1},{1... | collective-permute-start | bytes 430088 | tf_op jit(solution)/shard_map/ppermute | solution.py:589
  31.0 7.7 %collective-permute-start.5 = (bf16[180,4,128]{2,1,0:T(4,128)(2,1)S(1)}, bf16[180,4,128]{2,1,0:T(4,128)(2,1)S(1)}, u32[]{:S(2)}, u32[]{:S(2)}) collective-permute-start(bf16[180,4,128]{2,1,0:T(4,128)(2,1)S(1)} %get-tuple-element.88), channel_id=1, source_target_pairs={{0,14},{2,0},{4,2},{6,4},{8,6},{10,8},{12,10},{14,12},{1,15},{3,1}... | collective-permute-start | bytes 552968 | tf_op jit(solution)/shard_map/ppermute | solution.py:444
  36.0 5.2 %collective-permute-start.9 = (bf16[560,128]{1,0:T(8,128)(2,1)S(1)}, bf16[560,128]{1,0:T(8,128)(2,1)S(1)}, u32[]{:S(2)}, u32[]{:S(2)}) collective-permute-start(bf16[560,128]{1,0:T(8,128)(2,1)S(1)} %add_convert_fusion.1), channel_id=1, source_target_pairs={{0,4},{1,3},{2,6},{3,1},{4,0},{5,7},{6,2},{7,5},{8,12},{9,11},{10,... | collective-permute-start | bytes 430088 | tf_op jit(solution)/shard_map/ppermute | solution.py:589
  38.9 2.4 %collective-permute-start.6 = (bf16[180,8,128]{2,1,0:T(8,128)(2,1)S(1)}, bf16[180,8,128]{2,1,0:T(8,128)(2,1)S(1)}, u32[]{:S(2)}, u32[]{:S(2)}) collective-permute-start(bf16[180,8,128]{2,1,0:T(8,128)(2,1)S(1)} %pad_maximum_fusion), channel_id=1, source_target_pairs={{0,1},{1,0},{2,3},{3,2},{4,5},{5,4},{6,7},{7,6},{8,9},{9,8},{10,11... | collective-permute-start | bytes 1105928 | tf_op jit(solution)/shard_map/ppermute | solution.py:444
  41.2 1.4 %collective-permute-start.10 = (bf16[560,128]{1,0:T(8,128)(2,1)S(1)}, bf16[560,128]{1,0:T(8,128)(2,1)S(1)}, u32[]{:S(2)}, u32[]{:S(2)}) collective-permute-start(bf16[560,128]{1,0:T(8,128)(2,1)S(1)} %add_convert_fusion.mine_ref), channel_id=1, source_target_pairs={{0,1},{1,0},{2,3},{3,2},{4,5},{5,4},{6,7},{7,6},{8,9},{9,8},{10,11... | collective-permute-start | bytes 430088 | tf_op jit(solution)/shard_map/ppermute | solution.py:444

commit v9 on v8

--- a/solution.py
+++ b/solution.py
@@ -392,7 +392,7 @@
     d_gain_ref,
     d_offset_ref,
 ):
-    channels = weight_ref.shape[0]
+    channels = weight_ref.shape[1]
     f32 = jnp.float32
     rest = channels - LANES
     mine = mine_ref[...].astype(f32)
@@ -420,7 +420,7 @@
         across = slice(part * channels, (part + 1) * channels)
         unit = pieces[part][0:channels]
         bias = pieces[part][channels : channels + 1]
-        weight = weight_ref[:, across]
+        weight = weight_ref[part]
         d_weight_ref[:, across] = gain * unit + offset * bias
         biases.append(bias)
         products += weight.astype(f32) * unit
@@ -607,7 +607,7 @@
         in_specs=[whole(), whole(), whole(pltpu.SMEM), whole(), whole(), whole()],
         out_specs=(whole(),) * 6,
         compiler_params=params,
-    )(mine, other, core, qkv_weight, ln_gain[:, None], ln_offset[:, None])
+    )(mine, other, core, parts, ln_gain[:, None], ln_offset[:, None])
     return (d_tokens, d_weight, d_bias, d_proj, d_table.T, d_gain, d_offset)
 
 

time: 44.3 us -> 44 us (level)
  no operation moved by 1% of the time
where the time goes in v9:
time: 44 us; the launch traced here: 43.8 us
  waiting for transfers between devices  14.8 us (34%)
  starting transfers between devices  11.3 us (26%)
  Pallas kernels  10.8 us (25%)
  local copies, waits for them, and re-layouts  4.47 us (10%)
  other arithmetic  1.53 us (3%)
  between operations  0.94 us (2%)
    ppermute x7, starting transfers between devices, from_behind(): lax.ppermute(shard, axis, [(i, (i + by) % count) for i in range(count)])  8.57 us
    ppermute x3, waiting for transfers between devices, on_device(): mine = add(mine, lax.ppermute(mine, ('row', 'col'), pairs))  8.25 us
    ppermute x7, waiting for transfers between devices, from_behind(): lax.ppermute(shard, axis, [(i, (i + by) % count) for i in range(count)])  5.73 us
    pallas_call x1, Pallas kernels, on_device(): pl.pallas_call(main_kernel, name='window_attention_backward', out_shape=(...  5.44 us
    pallas_call x1, Pallas kernels, on_device(): pl.pallas_call(project_kernel, name='project', out_shape=(jax.ShapeDtypeS...  1.75 us
    ppermute x1, starting transfers between devices, diagonal(): return lax.ppermute(shard, ('row', 'col'), pairs)  1.6 us
    optimization_barrier x2, local copies, waits for them, and re-layouts, on_device(): lax.optimization_barrier((g_turned[:, rows - SHIFT:], tokens, grad_out, r...  1.53 us
    pallas_call x1, Pallas kernels, on_device(): pl.pallas_call(input_kernel, name='input_backward', out_shape=(jax.ShapeD...  1.33 us
  transfers between devices with their start and end apart: 11, of which 9 were waited for; matrix products, arithmetic and copies ran while one was open for 11% of the time, Pallas kernels for 9%

profile of v9, /device:TPU:0, one launch (start us, length us, event | category | flops | bytes accessed | tf_op | source)
XLA Modules:
  0.0 43.8 jit_solution(10919763473466021554)
XLA Ops:
  0.6 0.0 copy-start.3
  0.6 0.0 copy-start.2
  0.7 0.0 copy-start.7
  0.7 0.0 copy-start.4
  0.7 0.0 copy-start.1
  0.7 0.0 copy-start
  0.7 0.0 copy-start.5
  0.7 0.0 copy-start.6
  0.7 1.2 %slice.47 = bf16[180,4,128]{2,1,0:T(4,128)(2,1)S(1)} slice(bf16[180,8,128]{2,1,0:T(8,128)(2,1)} %bitcast.20), slice={[0:180], [4:8], [0:128]} | slice | bytes 368640 | tf_op jit(solution)/shard_map/slice | solution.py:480
  1.9 3.0 %collective-permute-start.3 = (bf16[180,4,128]{2,1,0:T(4,128)(2,1)S(1)}, bf16[180,4,128]{2,1,0:T(4,128)(2,1)S(1)}, u32[]{:S(2)}, u32[]{:S(2)}) collective-permute-start(bf16[180,4,128]{2,1,0:T(4,128)(2,1)S(1)} %slice.47), channel_id=1, source_target_pairs={{0,2},{2,4},{4,6},{6,8},{8,10},{10,12},{12,14},{14,0},{1,3},{3,5},... | collective-permute-start | bytes 552968 | tf_op jit(solution)/shard_map/ppermute | solution.py:444
  4.9 1.1 %slice.42 = bf16[180,4,128]{2,1,0:T(4,128)(2,1)S(1)} slice(bf16[180,8,128]{2,1,0:T(8,128)(2,1)} %bitcast.21), slice={[0:180], [4:8], [0:128]} | slice | bytes 368640 | tf_op jit(solution)/shard_map/slice | solution.py:482
  6.0 1.6 %collective-permute-start = (bf16[180,4,128]{2,1,0:T(4,128)(2,1)S(1)}, bf16[180,4,128]{2,1,0:T(4,128)(2,1)S(1)}, u32[]{:S(2)}, u32[]{:S(2)}) collective-permute-start(bf16[180,4,128]{2,1,0:T(4,128)(2,1)S(1)} %slice.42), channel_id=1, source_target_pairs={{0,2},{2,4},{4,6},{6,8},{8,10},{10,12},{12,14},{14,0},{1,3},{3,5},... | collective-permute-start | bytes 552968 | tf_op jit(solution)/shard_map/ppermute | solution.py:444
  7.6 1.2 %copy.24.tokens_ref = bf16[8,128,180]{2,1,0:T(8,128)(2,1)S(1)} copy(bf16[8,128,180]{1,0,2:T(8,128)(2,1)} %param.9) | data formatting | bytes 737280 | tf_op jit(solution)/shard_map/optimization_barrier | solution.py:481
  8.8 0.0 copy-done.3
  8.8 0.3 copy.31.grad_ref
  9.1 0.0 copy-done.2
  9.2 0.1 copy.26
  9.3 0.1 pad_maximum_fusion.1
  9.4 0.0 collective-permute-start.1
  9.4 0.1 copy.29
  9.6 0.1 pad_maximum_fusion.2
  9.6 1.6 %collective-permute-start.2 = (bf16[4,4,361]{2,1,0:T(4,128)(2,1)S(1)}, bf16[4,4,361]{2,1,0:T(4,128)(2,1)S(1)}, u32[]{:S(2)}, u32[]{:S(2)}) collective-permute-start(bf16[4,4,361]{2,1,0:T(4,128)(2,1)S(1)} %pad_maximum_fusion.2), channel_id=1, source_target_pairs={{0,3},{1,2},{2,5},{3,4},{4,7},{5,6},{6,9},{7,8},{8,11},{9,10},{10,... | collective-permute-start | bytes 34664 | tf_op jit(solution)/shard_map/ppermute | solution.py:452
  11.2 0.0 copy-done.7
  11.2 0.0 copy-done.4
  11.3 0.0 copy-done.1
  11.3 0.0 copy-done
  11.3 1.1 %prepare.1 = (f32[6,64,128]{2,1,0:T(8,128)S(1)}, bf16[3,256,192]{2,1,0:T(8,128)(2,1)S(1)}, bf16[3,192,256]{2,1,0:T(8,128)(2,1)S(1)}, bf16[192,180]{1,0:T(8,128)(2,1)S(1)}, bf16[3,180,180]{2,1,0:T(8,128)(2,1)S(1)}) custom-call(bf16[180,540]{1,0:T(8,128)(2,1)S(1)} %copy-done.1, f32[1,540]{1,0:T(1,128)S(1)} %broadcast_in_dim.24.offsets_ref, ...), custom_call_target="tpu_custom_call" | custom-call | flops 1000 | bytes 1000 | tf_op jit(solution)/shard_map/prepare/pallas_call | solution.py:501
  12.4 0.0 copy-done.5
  12.4 0.0 copy-done.6
  12.4 0.0 collective-permute-done.1.right_ref
  12.4 1.0 %collective-permute-done.3.x_above_ref = bf16[180,4,128]{2,1,0:T(4,128)(2,1)S(1)} collective-permute-done((bf16[180,4,128]{2,1,0:T(4,128)(2,1)S(1)}, bf16[180,4,128]{2,1,0:T(4,128)(2,1)S(1)}, u32[]{:S(2)}, u32[]{:S(2)}) %collective-permute-start.3) | collective-permute-done | bytes 184352 | tf_op jit(solution)/shard_map/ppermute | solution.py:444
  13.4 1.7 %project.1 = (f32[1024,256]{1,0:T(8,128)S(1)}, f32[1024,1]{1,0:T(8,128)S(1)}, bf16[192,1024]{1,0:T(8,128)(2,1)S(1)}, bf16[1024,180]{1,0:T(8,128)(2,1)S(1)}, bf16...) custom-call(bf16[8,128,180]{2,1,0:T(8,128)(2,1)S(1)} %copy.24.tokens, ...), custom_call_target="tpu_custom_call" | custom-call | flops 1000 | bytes 1000 | tf_op jit(solution)/shard_map/project/pallas_call | solution.py:520
  15.1 0.8 %collective-permute-done.2.corner_ref = bf16[4,4,361]{2,1,0:T(4,128)(2,1)S(1)} collective-permute-done((bf16[4,4,361]{2,1,0:T(4,128)(2,1)S(1)}, bf16[4,4,361]{2,1,0:T(4,128)(2,1)S(1)}, u32[]{:S(2)}, u32[]{:S(2)}) %collective-permute-start.2) | collective-permute-done | bytes 11584 | tf_op jit(solution)/shard_map/ppermute | solution.py:452
  15.9 0.7 %collective-permute-done.g_above_ref = bf16[180,4,128]{2,1,0:T(4,128)(2,1)S(1)} collective-permute-done((bf16[180,4,128]{2,1,0:T(4,128)(2,1)S(1)}, bf16[180,4,128]{2,1,0:T(4,128)(2,1)S(1)}, u32[]{:S(2)}, u32[]{:S(2)}) %collective-permute-start) | collective-permute-done | bytes 184352 | tf_op jit(solution)/shard_map/ppermute | solution.py:444
  16.6 5.4 %window_attention_backward.1 = (bf16[560,128]{1,0:T(8,128)(2,1)S(1)}, bf16[560,128]{1,0:T(8,128)(2,1)S(1)}, bf16[3,1024,180]{2,1,0:T(8,128)(2,1)S(1)}, f32[16,8,...) custom-call(bf16[8,128,180]{2,1,0:T(8,128)(2,1)S(1)} %copy.31.grad_ref, ...), custom_call_target="tpu_custom_call" | custom-call | tf_op jit(solution)/shard_map/window_attention_backward/pallas_call | solution.py:544
  22.1 0.2 collective-permute-start.4
  22.3 1.3 %collective-permute-done.4 = bf16[560,128]{1,0:T(8,128)(2,1)S(1)} collective-permute-done((bf16[560,128]{1,0:T(8,128)(2,1)S(1)}, bf16[560,128]{1,0:T(8,128)(2,1)S(1)}, u32[]{:S(2)}, u32[]{:S(2)}) %collective-permute-start.4) | collective-permute-done | bytes 143392 | tf_op jit(solution)/shard_map/ppermute | solution.py:444
  23.6 0.8 %collective-permute-start.7 = (bf16[560,128]{1,0:T(8,128)(2,1)S(1)}, bf16[560,128]{1,0:T(8,128)(2,1)S(1)}, u32[]{:S(2)}, u32[]{:S(2)}) collective-permute-start(bf16[560,128]{1,0:T(8,128)(2,1)S(1)} %add_convert_fusion.3), channel_id=1, source_target_pairs={{0,8},{1,5},{2,10},{3,7},{4,12},{5,1},{6,14},{7,3},{8,0},{9,13},{1... | collective-permute-start | bytes 430088 | tf_op jit(solution)/shard_map/ppermute | solution.py:589
  24.3 1.3 %input_backward.1 = bf16[180,8,128]{2,1,0:T(8,128)(2,1)S(1)} custom-call(bf16[3,1024,180]{2,1,0:T(8,128)(2,1)S(1)} %get-tuple-element.69.d_qkv_ref, f32[16,8,8,180]{3,2,1,0:T(8,128)S(1)} %get-tuple-element.70.g_ref, f32[128,256]{1,0:T(8,128)S(1)} %get-tuple-element.71.unit_last_ref, f32[128,1]{1,0:T(8,128)S(1)} %get-tuple-element.72.inv_last_ref, ...), custom_call_target="tpu_custom_call" | custom-call | flops 1000000000 | tf_op jit(solution)/shard_map/input_backward/pallas_call | solution.py:577
  25.7 5.0 %collective-permute-done.7 = bf16[560,128]{1,0:T(8,128)(2,1)S(1)} collective-permute-done((bf16[560,128]{1,0:T(8,128)(2,1)S(1)}, bf16[560,128]{1,0:T(8,128)(2,1)S(1)}, u32[]{:S(2)}, u32[]{:S(2)}) %collective-permute-start.7) | collective-permute-done | bytes 143392 | tf_op jit(solution)/shard_map/ppermute | solution.py:589
  30.7 0.1 collective-permute-start.8
  30.8 0.1 fusion.2
  31.0 3.6 %collective-permute-start.5 = (bf16[180,4,128]{2,1,0:T(4,128)(2,1)S(1)}, bf16[180,4,128]{2,1,0:T(4,128)(2,1)S(1)}, u32[]{:S(2)}, u32[]{:S(2)}) collective-permute-start(bf16[180,4,128]{2,1,0:T(4,128)(2,1)S(1)} %get-tuple-element.88), channel_id=1, source_target_pairs={{0,14},{2,0},{4,2},{6,4},{8,6},{10,8},{12,10},{14,12},{1,15},{3,1}... | collective-permute-start | bytes 552968 | tf_op jit(solution)/shard_map/ppermute | solution.py:444
  34.6 1.3 %collective-permute-done.8 = bf16[560,128]{1,0:T(8,128)(2,1)S(1)} collective-permute-done((bf16[560,128]{1,0:T(8,128)(2,1)S(1)}, bf16[560,128]{1,0:T(8,128)(2,1)S(1)}, u32[]{:S(2)}, u32[]{:S(2)}) %collective-permute-start.8) | collective-permute-done | bytes 143392 | tf_op jit(solution)/shard_map/ppermute | solution.py:589
  36.0 0.3 collective-permute-start.9
  36.2 2.5 %collective-permute-done.5 = bf16[180,4,128]{2,1,0:T(4,128)(2,1)S(1)} collective-permute-done((bf16[180,4,128]{2,1,0:T(4,128)(2,1)S(1)}, bf16[180,4,128]{2,1,0:T(4,128)(2,1)S(1)}, u32[]{:S(2)}, u32[]{:S(2)}) %collective-permute-start.5) | collective-permute-done | bytes 184352 | tf_op jit(solution)/shard_map/ppermute | solution.py:444
  38.7 0.2 pad_maximum_fusion
  38.9 0.1 collective-permute-start.6
  39.0 0.1 copy.32.gain_ref
  39.1 0.1 copy.33.offset_ref
  39.2 1.9 %collective-permute-done.9 = bf16[560,128]{1,0:T(8,128)(2,1)S(1)} collective-permute-done((bf16[560,128]{1,0:T(8,128)(2,1)S(1)}, bf16[560,128]{1,0:T(8,128)(2,1)S(1)}, u32[]{:S(2)}, u32[]{:S(2)}) %collective-permute-start.9) | collective-permute-done | bytes 143392 | tf_op jit(solution)/shard_map/ppermute | solution.py:589
  41.2 0.1 collective-permute-start.10
  41.2 0.0 collective-permute-done.6
  41.3 1.0 %select_bitcast_fusion = bf16[8,128,180]{1,0,2:T(8,128)(2,1)} fusion(bf16[180,8,128]{2,1,0:T(8,128)(2,1)S(1)} %collective-permute-done.6, pred[128]{0:T(512)(128)(4,1)S(1)} %iota_compare_fusion, bf16[180,4,128]{2,1,0:T(4,128)(2,1)S(1)} %collective-permute-done.5, bf16[180,4,128]{2,1,0:T(4,128)(2,1)S(1)} %get-tuple-element.87), kind=kLoop, calls=%fused_computation.1 | loop fusion | flops 921600 | bytes 1106048 | tf_op jit(solution)/shard_map/transpose | solution.py:592
  42.2 0.3 collective-permute-done.10.other_ref
  42.6 1.2 %finish.1 = (f32[180,540]{1,0:T(8,128)}, f32[540]{0:T(1024)}, f32[180,180]{1,0:T(8,128)}, f32[6,225]{1,0:T(8,128)}, f32[180]{0:T(256)}, /*index=5*/f32[180]{0:T(256)}) custom-call(bf16[560,128]{1,0:T(8,128)(2,1)S(1)} %add_convert_fusion.mine_ref, bf16[560,128]{1,0:T(8,128)(2,1)S(1)} %collective-permute-done.10.other_ref, s32[1]{0:T(128)} %bitcast.7.core_ref, ...), custom_call_target="tpu_custom_call" | custom-call | tf_op jit(solution)/shard_map/finish/pallas_call | solution.py:596
  (12 shorter events, 0.2 us)
Async XLA Ops:
  0.6 8.2 %copy-start.3 = (bf16[8,128,180]{1,0,2:T(8,128)(2,1)S(1)}, bf16[8,128,180]{1,0,2:T(8,128)(2,1)}, u32[]{:S(2)}) copy-start(bf16[8,128,180]{1,0,2:T(8,128)(2,1)} %param.10) | copy-start | bytes 1105924
  0.6 8.5 %copy-start.2 = (s32[8,128]{1,0:T(8,128)S(1)}, s32[8,128]{1,0:T(8,128)}, u32[]{:S(2)}) copy-start(s32[8,128]{1,0:T(8,128)} %region_ref) | copy-start | bytes 12292
  0.7 10.6 %copy-start.7 = (f32[540]{0:T(1024)S(1)}, f32[540]{0:T(1024)}, u32[]{:S(2)}) copy-start(f32[540]{0:T(1024)} %param.15) | copy-start | bytes 6484
  0.7 10.6 %copy-start.4 = (f32[225,6]{0,1:T(8,128)S(1)}, f32[225,6]{0,1:T(8,128)}, u32[]{:S(2)}) copy-start(f32[225,6]{0,1:T(8,128)} %param.17) | copy-start | bytes 16204
  0.7 10.6 %copy-start.1 = (bf16[180,540]{1,0:T(8,128)(2,1)S(1)}, bf16[180,540]{1,0:T(8,128)(2,1)}, u32[]{:S(2)}) copy-start(bf16[180,540]{1,0:T(8,128)(2,1)} %weight_ref.1) | copy-start | bytes 583204
  0.7 10.6 %copy-start = (bf16[180,180]{1,0:T(8,128)(2,1)S(1)}, bf16[180,180]{1,0:T(8,128)(2,1)}, u32[]{:S(2)}) copy-start(bf16[180,180]{1,0:T(8,128)(2,1)} %proj_ref.3) | copy-start | bytes 194404
  0.7 11.7 %copy-start.5 = (f32[180]{0:T(256)S(1)}, f32[180]{0:T(256)}, u32[]{:S(2)}) copy-start(f32[180]{0:T(256)} %param.12) | copy-start | bytes 2164
  0.7 11.7 %copy-start.6 = (f32[180]{0:T(256)S(1)}, f32[180]{0:T(256)}, u32[]{:S(2)}) copy-start(f32[180]{0:T(256)} %param.13) | copy-start | bytes 2164
  1.9 11.5 %collective-permute-start.3 = (bf16[180,4,128]{2,1,0:T(4,128)(2,1)S(1)}, bf16[180,4,128]{2,1,0:T(4,128)(2,1)S(1)}, u32[]{:S(2)}, u32[]{:S(2)}) collective-permute-start(bf16[180,4,128]{2,1,0:T(4,128)(2,1)S(1)} %slice.47), channel_id=1, source_target_pairs={{0,2},{2,4},{4,6},{6,8},{8,10},{10,12},{12,14},{14,0},{1,3},{3,5},... | collective-permute-start | bytes 552968 | tf_op jit(solution)/shard_map/ppermute | solution.py:444
  6.0 10.7 %collective-permute-start = (bf16[180,4,128]{2,1,0:T(4,128)(2,1)S(1)}, bf16[180,4,128]{2,1,0:T(4,128)(2,1)S(1)}, u32[]{:S(2)}, u32[]{:S(2)}) collective-permute-start(bf16[180,4,128]{2,1,0:T(4,128)(2,1)S(1)} %slice.42), channel_id=1, source_target_pairs={{0,2},{2,4},{4,6},{6,8},{8,10},{10,12},{12,14},{14,0},{1,3},{3,5},... | collective-permute-start | bytes 552968 | tf_op jit(solution)/shard_map/ppermute | solution.py:444
  9.4 3.0 %collective-permute-start.1 = (bf16[4,4,361]{2,1,0:T(4,128)(2,1)S(1)}, bf16[4,4,361]{2,1,0:T(4,128)(2,1)S(1)}, u32[]{:S(2)}, u32[]{:S(2)}) collective-permute-start(bf16[4,4,361]{2,1,0:T(4,128)(2,1)S(1)} %pad_maximum_fusion.1), channel_id=1, source_target_pairs={{0,1},{1,0},{2,3},{3,2},{4,5},{5,4},{6,7},{7,6},{8,9},{9,8},{10,11... | collective-permute-start | bytes 34664 | tf_op jit(solution)/shard_map/ppermute | solution.py:444
  9.6 6.3 %collective-permute-start.2 = (bf16[4,4,361]{2,1,0:T(4,128)(2,1)S(1)}, bf16[4,4,361]{2,1,0:T(4,128)(2,1)S(1)}, u32[]{:S(2)}, u32[]{:S(2)}) collective-permute-start(bf16[4,4,361]{2,1,0:T(4,128)(2,1)S(1)} %pad_maximum_fusion.2), channel_id=1, source_target_pairs={{0,3},{1,2},{2,5},{3,4},{4,7},{5,6},{6,9},{7,8},{8,11},{9,10},{10,... | collective-permute-start | bytes 34664 | tf_op jit(solution)/shard_map/ppermute | solution.py:452
  22.1 1.4 %collective-permute-start.4 = (bf16[560,128]{1,0:T(8,128)(2,1)S(1)}, bf16[560,128]{1,0:T(8,128)(2,1)S(1)}, u32[]{:S(2)}, u32[]{:S(2)}) collective-permute-start(bf16[560,128]{1,0:T(8,128)(2,1)S(1)} %get-tuple-element.62), channel_id=1, source_target_pairs={{0,1},{1,0},{2,3},{3,2},{4,5},{5,4},{6,7},{7,6},{8,9},{9,8},{10,11... | collective-permute-start | bytes 430088 | tf_op jit(solution)/shard_map/ppermute | solution.py:444
  23.6 7.1 %collective-permute-start.7 = (bf16[560,128]{1,0:T(8,128)(2,1)S(1)}, bf16[560,128]{1,0:T(8,128)(2,1)S(1)}, u32[]{:S(2)}, u32[]{:S(2)}) collective-permute-start(bf16[560,128]{1,0:T(8,128)(2,1)S(1)} %add_convert_fusion.3), channel_id=1, source_target_pairs={{0,8},{1,5},{2,10},{3,7},{4,12},{5,1},{6,14},{7,3},{8,0},{9,13},{1... | collective-permute-start | bytes 430088 | tf_op jit(solution)/shard_map/ppermute | solution.py:589
  30.7 5.2 %collective-permute-start.8 = (bf16[560,128]{1,0:T(8,128)(2,1)S(1)}, bf16[560,128]{1,0:T(8,128)(2,1)S(1)}, u32[]{:S(2)}, u32[]{:S(2)}) collective-permute-start(bf16[560,128]{1,0:T(8,128)(2,1)S(1)} %add_convert_fusion.2), channel_id=1, source_target_pairs={{0,2},{1,9},{2,0},{3,11},{4,6},{5,13},{6,4},{7,15},{8,10},{9,1},{1... | collective-permute-start | bytes 430088 | tf_op jit(solution)/shard_map/ppermute | solution.py:589
  31.0 7.7 %collective-permute-start.5 = (bf16[180,4,128]{2,1,0:T(4,128)(2,1)S(1)}, bf16[180,4,128]{2,1,0:T(4,128)(2,1)S(1)}, u32[]{:S(2)}, u32[]{:S(2)}) collective-permute-start(bf16[180,4,128]{2,1,0:T(4,128)(2,1)S(1)} %get-tuple-element.88), channel_id=1, source_target_pairs={{0,14},{2,0},{4,2},{6,4},{8,6},{10,8},{12,10},{14,12},{1,15},{3,1}... | collective-permute-start | bytes 552968 | tf_op jit(solution)/shard_map/ppermute | solution.py:444
  36.0 5.2 %collective-permute-start.9 = (bf16[560,128]{1,0:T(8,128)(2,1)S(1)}, bf16[560,128]{1,0:T(8,128)(2,1)S(1)}, u32[]{:S(2)}, u32[]{:S(2)}) collective-permute-start(bf16[560,128]{1,0:T(8,128)(2,1)S(1)} %add_convert_fusion.1), channel_id=1, source_target_pairs={{0,4},{1,3},{2,6},{3,1},{4,0},{5,7},{6,2},{7,5},{8,12},{9,11},{10,... | collective-permute-start | bytes 430088 | tf_op jit(solution)/shard_map/ppermute | solution.py:589
  38.9 2.4 %collective-permute-start.6 = (bf16[180,8,128]{2,1,0:T(8,128)(2,1)S(1)}, bf16[180,8,128]{2,1,0:T(8,128)(2,1)S(1)}, u32[]{:S(2)}, u32[]{:S(2)}) collective-permute-start(bf16[180,8,128]{2,1,0:T(8,128)(2,1)S(1)} %pad_maximum_fusion), channel_id=1, source_target_pairs={{0,1},{1,0},{2,3},{3,2},{4,5},{5,4},{6,7},{7,6},{8,9},{9,8},{10,11... | collective-permute-start | bytes 1105928 | tf_op jit(solution)/shard_map/ppermute | solution.py:444
  41.2 1.4 %collective-permute-start.10 = (bf16[560,128]{1,0:T(8,128)(2,1)S(1)}, bf16[560,128]{1,0:T(8,128)(2,1)S(1)}, u32[]{:S(2)}, u32[]{:S(2)}) collective-permute-start(bf16[560,128]{1,0:T(8,128)(2,1)S(1)} %add_convert_fusion.mine_ref), channel_id=1, source_target_pairs={{0,1},{1,0},{2,3},{3,2},{4,5},{5,4},{6,7},{7,6},{8,9},{9,8},{10,11... | collective-permute-start | bytes 430088 | tf_op jit(solution)/shard_map/ppermute | solution.py:444
